TPU v7x, 32 devices: a whole 2x2x4 slice. The times are simulated.
32 devices in a mesh: dp: 8 (over z, y), fsdp: 4 (over x, core).
Axes of the slice: x: 2, y: 2, z: 4, core: 2. Of those that a mesh axis runs over, the one named last changes fastest.
Arguments:
- tokens: bfloat16 [6144, 768], P(('dp', 'fsdp')), may hold values from -6 to 6
- lengths: int32 [32, 4], P(('dp', 'fsdp')), may hold values from 1 to 168, 192 in all within a row
- cotangent: bfloat16 [6144, 768], P(('dp', 'fsdp')), may hold values from -6 to 6
- w_qkv: bfloat16 [768, 2304], P(('dp', 'fsdp')), may hold values from -0.21875 to 0.21875
- bias_q: bfloat16 [768], P(('dp', 'fsdp')), may hold values from -3 to 3
- bias_v: bfloat16 [768], P(('dp', 'fsdp')), may hold values from -3 to 3
- w_out: bfloat16 [768, 768], P(('dp', 'fsdp')), may hold values from -0.625 to 0.625
- bias_out: bfloat16 [768], P(('dp', 'fsdp')), may hold values from -2 to 2
- gain_attn: bfloat16 [768], P(('dp', 'fsdp')), may hold values from 0.25 to 1.75
- shift_attn: bfloat16 [768], P(('dp', 'fsdp')), may hold values from -2 to 2
- gain_mlp: bfloat16 [768], P(('dp', 'fsdp')), may hold values from 0.25 to 1.75
- shift_mlp: bfloat16 [768], P(('dp', 'fsdp')), may hold values from -2 to 2
- w_up: bfloat16 [768, 3072], P(('dp', 'fsdp')), may hold values from -0.21875 to 0.21875
- bias_up: bfloat16 [3072], P(('dp', 'fsdp')), may hold values from -2 to 2
- w_down: bfloat16 [3072, 768], P(('dp', 'fsdp')), may hold values from -0.109375 to 0.109375
- bias_down: bfloat16 [768], P(('dp', 'fsdp')), may hold values from -2 to 2
- pass_embed: bfloat16 [3, 768], P(None, ('dp', 'fsdp')), may hold values from -3 to 3
Outputs:
- output: bfloat16 [6144, 768], P(('dp', 'fsdp'))
- token_grad: bfloat16 [6144, 768], P(('dp', 'fsdp'))
- grad_w_qkv: float32 [768, 2304], P(('dp', 'fsdp'))
- grad_bias_q: float32 [768], P(('dp', 'fsdp'))
- grad_bias_v: float32 [768], P(('dp', 'fsdp'))
- grad_w_out: float32 [768, 768], P(('dp', 'fsdp'))
- grad_bias_out: float32 [768], P(('dp', 'fsdp'))
- grad_gain_attn: float32 [768], P(('dp', 'fsdp'))
- grad_shift_attn: float32 [768], P(('dp', 'fsdp'))
- grad_gain_mlp: float32 [768], P(('dp', 'fsdp'))
- grad_shift_mlp: float32 [768], P(('dp', 'fsdp'))
- grad_w_up: float32 [768, 3072], P(('dp', 'fsdp'))
- grad_bias_up: float32 [3072], P(('dp', 'fsdp'))
- grad_w_down: float32 [3072, 768], P(('dp', 'fsdp'))
- grad_bias_down: float32 [768], P(('dp', 'fsdp'))
- grad_pass_embed: float32 [3, 768], P(None, ('dp', 'fsdp'))
Inputs may be any that keep to these rules, and one draw needn't show every extreme that they name: The 4 lengths of each row sum to 192; in every row the longest is exactly 168.
All inputs are finite; a program needn't handle non-finite values.
Results may differ from a plain program's by a relative error of at most 0.015.
Values may be sent and summed in bfloat16 or wider, within the bound.
No kernel may reach another device: no remote copies, remote signals or barrier semaphores. Data moves between devices by JAX's collectives and lax.ppermute only.
A program may use at most 192 MiB of HBM per device.

v0:
```python
import functools

import jax
import jax.numpy as jnp
from jax import lax
from jax.experimental import pallas as pl
from jax.experimental.pallas import tpu as pltpu
from jax.sharding import PartitionSpec as P

HEAD_DIM = 64
PASSES = 3
EPSILON = 1e-05
AXES = ("dp", "fsdp")
F32 = jnp.float32
BF16 = jnp.bfloat16


def pairs(partner):
    return [(i, partner(i)) for i in range(32)]


TO_MATE = pairs(lambda i: i ^ 1)
TO_Z = [pairs(lambda i, k=k: i ^ (8 * k)) for k in range(4)]
TO_NEAR = pairs(lambda i: i ^ (2 if i & 1 else 4))
TO_FAR = pairs(lambda i: i ^ (4 if i & 1 else 2))


def send(x, route):
    return lax.ppermute(x, AXES, route)


def after(x, *earlier):
    earlier = tuple(e for e in earlier if e is not None)
    return lax.optimization_barrier((x, earlier))[0] if earlier else x


def in_core_order(core, mine, other, axis):
    return jnp.where(
        core == 0,
        jnp.concatenate([mine, other], axis=axis),
        jnp.concatenate([other, mine], axis=axis),
    )


def gather_chunks(blocks):
    pieces, crossed, far = [], [], []
    for n, block in enumerate(blocks):
        if n >= 1:
            block = after(block, crossed[n - 1])
        z = [send(block, TO_Z[k]) for k in (1, 2, 3)]
        crossed.append(z)
        stack = jnp.stack([block] + z)
        if n >= 2:
            stack = after(stack, far[n - 2])
        both = jnp.stack([stack, send(stack, TO_NEAR)])
        distant = send(both, TO_FAR)
        far.append(distant)
        pieces.append([both, distant, send(both, TO_MATE), send(distant, TO_MATE)])
    return pieces


def chip_of(place, swapped, far, near, z):
    chip, core = place
    order = core ^ swapped
    near_bit = 2 - order
    far_bit = 1 + order
    return chip ^ (far * far_bit) ^ (near * near_bit) ^ (z * 4)


def run_copies(copies):
    for copy in copies:
        copy.start()
    for copy in copies:
        copy.wait()


def assemble_kernel(widths, place_ref, both, distant, mate_both, mate_distant, *rest):
    outs, sem = rest[:-1], rest[-1]
    place = (place_ref[0], place_ref[1])
    rows = both.shape[2]
    copies = []
    for source, swapped, far in (
        (both, 0, 0),
        (distant, 0, 1),
        (mate_both, 1, 0),
        (mate_distant, 1, 1),
    ):
        half = place[1] ^ swapped
        for near in range(2):
            for z in range(4):
                chip = chip_of(place, swapped, far, near, z)
                first = 0
                for out, width in zip(outs, widths):
                    copies.append(
                        pltpu.make_async_copy(
                            source.at[near, z, :, pl.ds(first, width)],
                            out.at[
                                pl.ds(pl.multiple_of(chip * rows, 16), rows),
                                pl.ds(pl.multiple_of(half * width, 128), width),
                            ],
                            sem,
                        )
                    )
                    first += width
    run_copies(copies)


def assemble(place, pieces, widths):
    rows = pieces[0].shape[2] * 16
    anywhere = pl.BlockSpec(memory_space=pl.ANY)
    return pl.pallas_call(
        functools.partial(assemble_kernel, widths),
        out_shape=[jax.ShapeDtypeStruct((rows, 2 * w), BF16) for w in widths],
        in_specs=[pl.BlockSpec(memory_space=pltpu.SMEM)] + [anywhere] * 4,
        out_specs=[pl.BlockSpec(memory_space=pltpu.VMEM)] * len(widths),
        scratch_shapes=[pltpu.SemaphoreType.DMA(())],
    )(place, *pieces)


def spread_kernel(widths, place_ref, *refs):
    count = len(widths)
    sources, (give, keep), sem = refs[:count], refs[count : count + 2], refs[-1]
    place = (place_ref[0], place_ref[1])
    rows = give.shape[3]
    copies = []
    for target, swapped in ((give, 1), (keep, 0)):
        half = place[1] ^ swapped
        for far in range(2):
            for near in range(2):
                for z in range(4):
                    chip = chip_of(place, swapped, far, near, z)
                    first = 0
                    for source, width in zip(sources, widths):
                        copies.append(
                            pltpu.make_async_copy(
                                source.at[
                                    pl.ds(pl.multiple_of(chip * rows, 16), rows),
                                    pl.ds(pl.multiple_of(half * width, 128), width),
                                ],
                                target.at[far, near, z, :, pl.ds(first, width)],
                                sem,
                            )
                        )
                        first += width
    run_copies(copies)


def spread(place, grads):
    widths = [g.shape[1] // 2 for g in grads]
    rows = grads[0].shape[0] // 16
    anywhere = pl.BlockSpec(memory_space=pl.ANY)
    shape = jax.ShapeDtypeStruct((2, 2, 4, rows, sum(widths)), BF16)
    return pl.pallas_call(
        functools.partial(spread_kernel, widths),
        out_shape=[shape, shape],
        in_specs=[pl.BlockSpec(memory_space=pltpu.SMEM)] + [pl.BlockSpec(memory_space=pltpu.VMEM)] * len(grads),
        out_specs=[anywhere] * 2,
        scratch_shapes=[pltpu.SemaphoreType.DMA(())],
    )(place, *grads)


def add_low(a, b):
    return (a.astype(F32) + b.astype(F32)).astype(BF16)


def scatter_chunk(core, give, keep, extra, earlier):
    parts = [(send(give, TO_MATE), keep)]
    if extra is not None:
        parts.append((send(extra[0], TO_MATE), extra[1]))
    give, keep = (
        jnp.concatenate([add_low(kept[far], got[far]) for got, kept in parts], axis=-1) for far in (1, 0)
    )
    got = send(after(give, earlier.get("near")), TO_FAR)
    give, keep = add_low(keep[1], got[1]), add_low(keep[0], got[0])
    got = send(give, TO_NEAR)
    near = got
    give = [add_low(keep[k], got[k]) for k in (1, 2, 3)]
    total = keep[0].astype(F32) + got[0].astype(F32)
    give = after(give, earlier.get("z"))
    z = [send(give[k - 1], TO_Z[k]) for k in (1, 2, 3)]
    for part in z:
        total = total + part.astype(F32)
    rows = total.shape[0] // 2
    total = total.reshape(2, rows, total.shape[1])
    mine = jnp.where(core == 0, total[0], total[1])
    other = send(jnp.where(core == 0, total[1], total[0]), TO_MATE)
    return (
        jnp.where(core == 0, mine, other),
        jnp.where(core == 0, other, mine),
    ), {"near": near, "z": z}


SMALL = 256


def pack_small(vectors, bias_up, pass_embed):
    rows = vectors[0].shape[0]
    first = jnp.stack(vectors, axis=1)
    second = jnp.concatenate([bias_up.reshape(rows, -1), pass_embed.T], axis=1)
    pad = lambda a: jnp.pad(a, ((0, 0), (0, SMALL // 2 - a.shape[1])))
    return jnp.concatenate([pad(first), pad(second)], axis=1)


def unpack_small(small):
    half = SMALL // 2
    vectors = [small[:, k] for k in range(8)]
    return vectors, small[:, half : half + 4].reshape(-1), small[:, half + 4 : half + 4 + PASSES].T


def is_known_slice():
    return lax.axis_size("dp") == 8 and lax.axis_size("fsdp") == 4


def place_of():
    index = lax.axis_index("dp") * 4 + lax.axis_index("fsdp")
    return jnp.stack([index >> 1, index & 1]).astype(jnp.int32)


def halves(*arrays):
    return [
        jnp.concatenate([a[:, h * (a.shape[1] // 2) : (h + 1) * (a.shape[1] // 2)] for a in arrays], axis=1)
        for h in range(2)
    ]


def gather_all(w_qkv, w_out, small, w_up, w_down):
    if not is_known_slice():
        whole = [lax.all_gather(a, AXES, axis=0, tiled=True) for a in (w_qkv, w_out, w_up, w_down, small)]
        return whole[:4], whole[4]
    place = place_of()
    core = place[1]
    blocks = []
    for arrays in ((w_qkv, w_out, small), (w_up,), (w_down,)):
        low, high = halves(*arrays)
        mine = jnp.where(core == 0, low, high)
        other = send(jnp.where(core == 0, high, low), TO_MATE)
        blocks.append(in_core_order(core, mine, other, 0))
    pieces = gather_chunks(blocks)
    first = (w_qkv.shape[1] + w_out.shape[1]) // 2
    (small,) = assemble(place, [p[..., first:] for p in pieces[0]], [small.shape[1] // 2])
    return pieces[0] + pieces[1] + pieces[2], small


def scatter_all(grads, small):
    if not is_known_slice():
        total = lambda g: lax.psum_scatter(g.astype(F32), AXES, scatter_dimension=0, tiled=True)
        return [total(g) for g in (*grads, small)]
    place = place_of()
    core = place[1]
    small_give, small_keep = spread(place, [small])
    sums, earlier = [], {}
    for n in range(3):
        give, keep = grads[2 * n], grads[2 * n + 1]
        extra = (small_give, small_keep) if n == 2 else None
        (low, high), earlier = scatter_chunk(core, give, keep, extra, earlier)
        sums.append((low, high))
    join = lambda n, first, width: jnp.concatenate([s[:, first : first + width] for s in sums[n]], axis=1)
    down_half, up_half, last = sums[0][0].shape[1], sums[1][0].shape[1], sums[2][0].shape[1]
    small_half = small.shape[1] // 2
    out_half = (last - small_half) // 4
    return [
        join(2, 0, 3 * out_half),
        join(2, 3 * out_half, out_half),
        join(1, 0, up_half),
        join(0, 0, down_half),
        join(2, 4 * out_half, small_half),
    ]


BIAS_Q, BIAS_V, BIAS_OUT, GAIN_ATTN, SHIFT_ATTN, GAIN_MLP, SHIFT_MLP, BIAS_DOWN, EMBED = range(9)
VECTORS = 16
PAIR = 2 * HEAD_DIM
SCALE = HEAD_DIM**-0.5
LOG2_E = 1.4426950408889634
GELU_A = 0.7978845608028654
GELU_B = 0.044715


def dot(a, b, a_dim, b_dim):
    return lax.dot_general(a, b, (((a_dim,), (b_dim,)), ((), ())), preferred_element_type=F32)


def nn(a, b):
    return dot(a, b, 1, 0)


def nt(a, b):
    return dot(a, b, 1, 1)


def tn(a, b):
    return dot(a, b, 0, 0)


def row_mean(x):
    return jnp.sum(x, axis=1, keepdims=True) * (1.0 / x.shape[1])


def normalized(x):
    centred = x - row_mean(x)
    inverse = lax.rsqrt(row_mean(centred * centred) + EPSILON)
    return centred * inverse, inverse


def gelu_and_slope(v):
    square = v * v
    t = jnp.tanh(v * (GELU_A + (GELU_A * GELU_B) * square))
    half = 0.5 * (1.0 + t)
    slope = half + v * (1.0 - t * t) * (0.5 * GELU_A + (1.5 * GELU_A * GELU_B) * square)
    return v * half, slope


def block_copies(place, arrays, targets, sems, out_of_full):
    copies = []
    for array, swapped, far in arrays:
        half = place[1] ^ swapped
        rows = array.shape[2]
        for near in range(2):
            for z in range(4):
                chip = chip_of(place, swapped, far, near, z)
                first = 0
                for (full, width), sem in zip(targets, sems):
                    inside = full.at[
                        pl.ds(pl.multiple_of(chip * rows, 16), rows),
                        pl.ds(pl.multiple_of(half * width, 128), width),
                    ]
                    block = array.at[near, z, :, pl.ds(first, width)]
                    source, target = (inside, block) if out_of_full else (block, inside)
                    copies.append(pltpu.make_async_copy(source, target, sem))
                    first += width
    return copies


def start_all(copies):
    for copy in copies:
        copy.start()


def wait_whole(full, sem):
    pltpu.make_async_copy(full, full, sem).wait()


def layer_kernel(known, *refs):
    place_ref, lengths_ref, tokens, cotangent, vec, bias_up = refs[:6]
    sources, refs = (refs[6:18], refs[18:]) if known else (refs[6:10], refs[10:])
    output, token_grad, g_vec, g_bias_up = refs[:4]
    results, refs = (refs[4:10], refs[10:]) if known else (refs[4:8], refs[8:])
    (
        w_qkv,
        w_out,
        w_up,
        w_down,
        x_norm,
        x_context,
        x_mlp,
        x_active,
        d_z,
        d_y,
        d_hidden,
        d_mixed,
        q_all,
        k_all,
        v_all,
        probs_0,
        probs_1,
        probs_2,
        entry,
        middle,
        k_grad,
        v_grad,
        state,
        extra,
        d_context,
        scores,
        d_scores,
        mask,
        in_sems,
        out_sems,
    ) = refs
    probs = (probs_0, probs_1, probs_2)
    length, width = state.shape
    inner = w_up.shape[1]
    pair_count = width // PAIR
    place = (place_ref[0], place_ref[1])

    weights = (w_qkv, w_out, w_up, w_down)
    if known:
        chunks = (
            (sources[0:4], (w_qkv, w_out), (0, 1)),
            (sources[4:8], (w_up,), (2,)),
            (sources[8:12], (w_down,), (3,)),
        )
        for pieces, targets, numbers in chunks:
            start_all(
                block_copies(
                    place,
                    list(zip(pieces, (0, 0, 1, 1), (0, 1, 0, 1))),
                    [(t, t.shape[1] // 2) for t in targets],
                    [in_sems.at[n] for n in numbers],
                    False,
                )
            )
    else:
        for n in range(4):
            pltpu.make_async_copy(sources[n], weights[n], in_sems.at[n]).start()

    def cols(n, size):
        return pl.ds(pl.multiple_of(n * size, size), size)

    rows_at = lax.broadcasted_iota(jnp.int32, (length, PASSES * length), 0)
    keys_at = lax.broadcasted_iota(jnp.int32, (length, PASSES * length), 1)
    for _ in range(PASSES - 1):
        keys_at = jnp.where(keys_at >= length, keys_at - length, keys_at)
    same = keys_at <= rows_at
    end = 0
    for n in range(lengths_ref.shape[0]):
        end = end + lengths_ref[n]
        same = same & ((rows_at >= end) == (keys_at >= end))
    mask[...] = jnp.where(same, 0.0, -1e30)

    lane = lax.broadcasted_iota(jnp.int32, (1, PAIR), 1)
    first_head = (lane < HEAD_DIM).astype(F32).astype(BF16)
    second_head = (lane >= HEAD_DIM).astype(F32).astype(BF16)

    def stacked(x):
        return jnp.concatenate([x * first_head, x * second_head], axis=0)

    def unstacked(x):
        return jnp.where(lane < HEAD_DIM, x[:length], x[length:])

    def vector(n):
        return vec[n : n + 1, :]

    LN_ROWS = 32
    SOFT_ROWS = 64
    g_vec[...] = jnp.zeros(g_vec.shape, F32)

    for b in range(0, length, 64):
        state[b : b + 64, :] = tokens[b : b + 64, :].astype(F32)

    for r in range(PASSES):
        at = r * length
        mine = pl.ds(at, length)
        seen = (r + 1) * length
        for b in range(0, length, LN_ROWS):
            x = state[b : b + LN_ROWS, :] + vector(EMBED + r)
            entry[at + b : at + b + LN_ROWS, :] = x
            n, _ = normalized(x)
            x_norm[at + b : at + b + LN_ROWS, :] = (n * vector(GAIN_ATTN) + vector(SHIFT_ATTN)).astype(BF16)
        if r == 0:
            wait_whole(w_qkv, in_sems.at[0])
        for part, (target, bias) in enumerate(((q_all, BIAS_Q), (k_all, None), (v_all, BIAS_V))):
            for c in range(0, width, 256):
                acc = nn(x_norm[mine, :], w_qkv[:, part * width + c : part * width + c + 256])
                if bias is not None:
                    acc = acc + vec[bias : bias + 1, c : c + 256]
                target[mine, c : c + 256] = acc.astype(BF16)

        def attend(j, _):
            c = cols(j, PAIR)
            scores[:, :seen] = nt(stacked(q_all[mine, c]), k_all[:seen, c])
            for b in range(0, 2 * length, SOFT_ROWS):
                part = slice(b, b + SOFT_ROWS)
                m = b % length
                s = scores[part, :seen] + mask[m : m + SOFT_ROWS, :seen]
                p = jnp.exp2((s - jnp.max(s, axis=1, keepdims=True)) * (SCALE * LOG2_E))
                p = p * (1.0 / jnp.sum(p, axis=1, keepdims=True))
                probs[r][j, part, :] = p.astype(BF16)
            x_context[mine, c] = unstacked(nn(probs[r][j], v_all[:seen, c])).astype(BF16)

        lax.fori_loop(0, pair_count, attend, None)
        if r == 0:
            wait_whole(w_out, in_sems.at[1])
        for c in range(0, width, 256):
            acc = nn(x_context[mine, :], w_out[:, c : c + 256])
            middle[mine, c : c + 256] = entry[mine, c : c + 256] + acc + vec[BIAS_OUT : BIAS_OUT + 1, c : c + 256]
        for b in range(0, length, LN_ROWS):
            n, _ = normalized(middle[at + b : at + b + LN_ROWS, :])
            x_mlp[at + b : at + b + LN_ROWS, :] = (n * vector(GAIN_MLP) + vector(SHIFT_MLP)).astype(BF16)
        if r == 0:
            wait_whole(w_up, in_sems.at[2])

        def up(j, _):
            c = cols(j, 256)
            value, slope = gelu_and_slope(nn(x_mlp[mine, :], w_up[:, c]) + bias_up[:, c])
            x_active[mine, c] = value.astype(BF16)
            d_hidden[mine, c] = slope.astype(BF16)

        lax.fori_loop(0, inner // 256, up, None, unroll=6)
        if r == 0:
            wait_whole(w_down, in_sems.at[3])
        for c in range(0, width, 256):
            acc = nn(x_active[mine, :], w_down[:, c : c + 256])
            state[:, c : c + 256] = middle[mine, c : c + 256] + acc + vec[BIAS_DOWN : BIAS_DOWN + 1, c : c + 256]

    for b in range(0, length, 64):
        output[b : b + 64, :] = state[b : b + 64, :].astype(BF16)
        state[b : b + 64, :] = cotangent[b : b + 64, :].astype(F32)

    def norm_backward(source, at, gain, g_gain, g_shift, rounded, g_embed):
        for b in range(0, length, LN_ROWS):
            part = slice(b, b + LN_ROWS)
            n, inverse = normalized(source[at + b : at + b + LN_ROWS, :])
            e = extra[part, :]
            g_vec[g_gain : g_gain + 1, :] += jnp.sum(e * n, axis=0, keepdims=True)
            g_vec[g_shift : g_shift + 1, :] += jnp.sum(e, axis=0, keepdims=True)
            eg = e * vector(gain)
            back = state[part, :] + inverse * (eg - row_mean(eg) - n * row_mean(eg * n))
            state[part, :] = back
            if rounded is not None:
                rounded[at + b : at + b + LN_ROWS, :] = back.astype(BF16)
            if g_embed is not None:
                g_vec[g_embed : g_embed + 1, :] += jnp.sum(back, axis=0, keepdims=True)

    ones = jnp.ones((16, PASSES * length), BF16)

    def send_out(n, targets):
        if known:
            give, keep = results[2 * n], results[2 * n + 1]
            arrays = []
            for array, swapped in ((give, 1), (keep, 0)):
                arrays += [(array.at[0], swapped, 0), (array.at[1], swapped, 1)]
            start_all(
                block_copies(
                    place,
                    arrays,
                    [(weights[t], weights[t].shape[1] // 2) for t in targets],
                    [out_sems.at[t] for t in targets],
                    True,
                )
            )
        else:
            for t in targets:
                pltpu.make_async_copy(weights[t], results[t], out_sems.at[t]).start()

    for r in reversed(range(PASSES)):
        at = r * length
        mine = pl.ds(at, length)
        seen = (r + 1) * length
        for b in range(0, length, 64):
            d_z[at + b : at + b + 64, :] = state[b : b + 64, :].astype(BF16)

        def down_back(j, _):
            c = cols(j, 256)
            acc = nt(d_z[mine, :], w_down[c, :])
            d_hidden[mine, c] = (acc * d_hidden[mine, c].astype(F32)).astype(BF16)

        lax.fori_loop(0, inner // 256, down_back, None, unroll=6)
        if r == 0:

            def down_grad(j, _):
                c = cols(j, 256)
                w_down[c, :] = tn(x_active[:, c], d_z[...]).astype(BF16)

            lax.fori_loop(0, inner // 256, down_grad, None, unroll=2)
            send_out(0, (3,))
            g_vec[BIAS_DOWN : BIAS_DOWN + 1, :] = nn(ones, d_z[...])[:1]
        for c in range(0, width, 256):
            extra[:, c : c + 256] = nt(d_hidden[mine, :], w_up[c : c + 256, :])
        if r == 0:

            def up_grad(j, _):
                c = cols(j, 768)
                w_up[:, c] = tn(x_mlp[...], d_hidden[:, c]).astype(BF16)
                g_bias_up[:, c] = nn(ones, d_hidden[:, c])[:1]

            lax.fori_loop(0, inner // 768, up_grad, None)
            send_out(1, (2,))
        norm_backward(middle, at, GAIN_MLP, GAIN_MLP, SHIFT_MLP, d_y, None)
        for c in range(0, width, 256):
            d_context[:, c : c + 256] = nt(d_y[mine, :], w_out[c : c + 256, :]).astype(BF16)

        def attend_back(j, _):
            c = cols(j, PAIR)
            dc = d_context[:, c]
            both = stacked(dc)
            scores[:, :seen] = nt(both, v_all[:seen, c])
            product = dc.astype(F32) * x_context[mine, c].astype(F32)
            inner_0 = jnp.sum(jnp.where(lane < HEAD_DIM, product, 0.0), axis=1, keepdims=True)
            inner_1 = jnp.sum(jnp.where(lane < HEAD_DIM, 0.0, product), axis=1, keepdims=True)
            for b in range(0, 2 * length, SOFT_ROWS):
                part = slice(b, b + SOFT_ROWS)
                m = b % length
                shift = (inner_0 if b < length else inner_1)[m : m + SOFT_ROWS]
                d_scores[part, :seen] = (
                    probs[r][j, part, :].astype(F32) * (scores[part, :seen] - shift)
                ).astype(BF16)
            ds = d_scores[:, :seen]
            d_mixed[mine, c] = (unstacked(nn(ds, k_all[:seen, c])) * SCALE).astype(BF16)
            k_more = tn(ds, stacked(q_all[mine, c]))
            v_more = tn(probs[r][j], both)
            if r == PASSES - 1:
                k_grad[:seen, c] = k_more
                v_grad[:seen, c] = v_more
            else:
                k_grad[:seen, c] += k_more
                v_grad[:seen, c] += v_more

        lax.fori_loop(0, pair_count, attend_back, None)
        for b in range(0, length, 64):
            part = slice(at + b, at + b + 64)
            d_mixed[part, width : 2 * width] = (k_grad[part, :] * SCALE).astype(BF16)
            d_mixed[part, 2 * width :] = v_grad[part, :].astype(BF16)
        for c in range(0, width, 256):
            extra[:, c : c + 256] = nt(d_mixed[mine, :], w_qkv[c : c + 256, :])
        norm_backward(entry, at, GAIN_ATTN, GAIN_ATTN, SHIFT_ATTN, None, EMBED + r)

    for b in range(0, length, 64):
        token_grad[b : b + 64, :] = state[b : b + 64, :].astype(BF16)
    w_out[...] = tn(x_context[...], d_y[...]).astype(BF16)
    for c in range(0, 3 * width, width):
        w_qkv[:, c : c + width] = tn(x_norm[...], d_mixed[:, c : c + width]).astype(BF16)
    send_out(2, (0, 1))
    g_vec[BIAS_Q : BIAS_Q + 1, :] = nn(ones, d_mixed[:, :width])[:1]
    g_vec[BIAS_V : BIAS_V + 1, :] = nn(ones, d_mixed[:, 2 * width :])[:1]
    g_vec[BIAS_OUT : BIAS_OUT + 1, :] = nn(ones, d_y[...])[:1]
    for n in range(4):
        wait_whole(weights[n], out_sems.at[n])


def layer(place, lengths, tokens, cotangent, vec, bias_up, sources, known):
    length, width = tokens.shape
    inner = bias_up.shape[1]
    total = PASSES * length
    anywhere = pl.BlockSpec(memory_space=pl.ANY)
    local = pl.BlockSpec(memory_space=pltpu.VMEM)
    scalars = pl.BlockSpec(memory_space=pltpu.SMEM)
    struct = jax.ShapeDtypeStruct
    full = [(width, 3 * width), (width, width), (width, inner), (inner, width)]
    if known:
        results = []
        for rows, half in ((inner // 16, width // 2), (width // 16, inner // 2), (width // 16, 2 * width)):
            results += [struct((2, 2, 4, rows, half), BF16)] * 2
    else:
        results = [struct(shape, BF16) for shape in full]
    low = lambda *shape: pltpu.VMEM(shape, BF16)
    wide = lambda *shape: pltpu.VMEM(shape, F32)
    pairs_ = width // PAIR
    return pl.pallas_call(
        functools.partial(layer_kernel, known),
        out_shape=[
            struct((length, width), BF16),
            struct((length, width), BF16),
            struct((VECTORS, width), F32),
            struct((1, inner), F32),
        ]
        + results,
        in_specs=[scalars, scalars] + [local] * 4 + [anywhere] * len(sources),
        out_specs=[local] * 4 + [anywhere] * len(results),
        scratch_shapes=[low(*shape) for shape in full]
        + [low(total, width)] * 3
        + [low(total, inner)]
        + [low(total, width)] * 2
        + [low(total, inner), low(total, 3 * width)]
        + [low(total, width)] * 3
        + [low(pairs_, 2 * length, (r + 1) * length) for r in range(PASSES)]
        + [wide(total, width)] * 4
        + [wide(length, width)] * 2
        + [low(length, width), wide(2 * length, total), low(2 * length, total), wide(length, total)]
        + [pltpu.SemaphoreType.DMA((4,)), pltpu.SemaphoreType.DMA((4,))],
        compiler_params=pltpu.CompilerParams(vmem_limit_bytes=60 * 2**20),
        name="layer",
    )(place, lengths, tokens, cotangent, vec, bias_up, *sources)


def per_device(
    tokens,
    lengths,
    cotangent,
    w_qkv,
    bias_q,
    bias_v,
    w_out,
    bias_out,
    gain_attn,
    shift_attn,
    gain_mlp,
    shift_mlp,
    w_up,
    bias_up,
    w_down,
    bias_down,
    pass_embed,
):
    known = is_known_slice()
    place = place_of()
    small = pack_small(
        [bias_q, bias_v, bias_out, gain_attn, shift_attn, gain_mlp, shift_mlp, bias_down], bias_up, pass_embed
    )
    sources, small = gather_all(w_qkv, w_out, small, w_up, w_down)
    vectors, bias_up, pass_embed = unpack_small(small)
    vec = jnp.concatenate([jnp.stack(vectors), pass_embed], axis=0).astype(F32)
    vec = jnp.pad(vec, ((0, VECTORS - vec.shape[0]), (0, 0)))
    output, token_grad, g_vec, g_bias_up, *results = layer(
        place, lengths[0], tokens, cotangent, vec, bias_up.astype(F32)[None, :], sources, known
    )
    g_small = pack_small([g_vec[n] for n in range(8)], g_bias_up[0], g_vec[8 : 8 + PASSES]).astype(BF16)
    g_qkv, g_out, g_up, g_down, g_small = scatter_all(results, g_small)
    (g_bq, g_bv, g_bo, g_ga, g_sa, g_gm, g_sm, g_bd), g_bu, g_pe = unpack_small(g_small)
    return (
        output,
        token_grad,
        g_qkv,
        g_bq,
        g_bv,
        g_out,
        g_bo,
        g_ga,
        g_sa,
        g_gm,
        g_sm,
        g_up,
        g_bu,
        g_down,
        g_bd,
        g_pe,
    )


def solution(mesh):
    placed = (
        P(("dp", "fsdp"), None),
        P(("dp", "fsdp"), None),
        P(("dp", "fsdp"), None),
        P(("dp", "fsdp"), None),
        P(("dp", "fsdp")),
        P(("dp", "fsdp")),
        P(("dp", "fsdp"), None),
        P(("dp", "fsdp")),
        P(("dp", "fsdp")),
        P(("dp", "fsdp")),
        P(("dp", "fsdp")),
        P(("dp", "fsdp")),
        P(("dp", "fsdp"), None),
        P(("dp", "fsdp")),
        P(("dp", "fsdp"), None),
        P(("dp", "fsdp")),
        P(None, ("dp", "fsdp")),
    )
    return jax.shard_map(
        per_device,
        mesh=mesh,
        in_specs=placed,
        out_specs=(
            P(("dp", "fsdp"), None),
            P(("dp", "fsdp"), None),
            P(("dp", "fsdp"), None),
            P(("dp", "fsdp")),
            P(("dp", "fsdp")),
            P(("dp", "fsdp"), None),
            P(("dp", "fsdp")),
            P(("dp", "fsdp")),
            P(("dp", "fsdp")),
            P(("dp", "fsdp")),
            P(("dp", "fsdp")),
            P(("dp", "fsdp"), None),
            P(("dp", "fsdp")),
            P(("dp", "fsdp"), None),
            P(("dp", "fsdp")),
            P(None, ("dp", "fsdp")),
        ),
        check_vma=False,
    )
```

profile of v0, /device:TPU:0, one launch (start us, length us, event | category | flops | bytes accessed | tf_op | source)
XLA Modules:
  0.0 305.0 jit_solution(14474949852658414746)
XLA Ops:
  6.3 5.0 %collective-permute-start.3 = (bf16[48,1664]{1,0:T(8,128)(2,1)S(1)}, bf16[48,1664]{1,0:T(8,128)(2,1)S(1)}, u32[]{:S(2)}, u32[]{:S(2)}) collective-permute-start(bf16[48,1664]{1,0:T(8,128)(2,1)S(1)} %maximum_select_fusion.1), channel_id=1, source_target_pairs={{0,24},{1,25},{2,26},{3,27},{4,28},{5,29},{6,30},{7,31},{8,16},{9,... | collective-permute-start | bytes 479240 | tf_op jit(solution)/shard_map/ppermute | solution.py:29
  12.0 4.3 %collective-permute-done.3 = bf16[48,1664]{1,0:T(8,128)(2,1)S(1)} collective-permute-done((bf16[48,1664]{1,0:T(8,128)(2,1)S(1)}, bf16[48,1664]{1,0:T(8,128)(2,1)S(1)}, u32[]{:S(2)}, u32[]{:S(2)}) %collective-permute-start.3) | collective-permute-done | bytes 159776 | tf_op jit(solution)/shard_map/ppermute | solution.py:29
  16.3 8.8 %collective-permute-done.2 = bf16[48,1664]{1,0:T(8,128)(2,1)S(1)} collective-permute-done((bf16[48,1664]{1,0:T(8,128)(2,1)S(1)}, bf16[48,1664]{1,0:T(8,128)(2,1)S(1)}, u32[]{:S(2)}, u32[]{:S(2)}) %collective-permute-start.2) | collective-permute-done | bytes 159776 | tf_op jit(solution)/shard_map/ppermute | solution.py:29
  26.8 8.9 %collective-permute-done.4 = bf16[4,48,1664]{2,1,0:T(8,128)(2,1)S(1)} collective-permute-done((bf16[4,48,1664]{2,1,0:T(8,128)(2,1)S(1)}, bf16[4,48,1664]{2,1,0:T(8,128)(2,1)S(1)}, u32[]{:S(2)}, u32[]{:S(2)}) %collective-permute-start.4) | collective-permute-done | bytes 639008 | tf_op jit(solution)/shard_map/ppermute | solution.py:29
  38.8 2.5 collective-permute-start.11
  43.3 4.2 %collective-permute-done.11 = bf16[48,1536]{1,0:T(8,128)(2,1)S(1)} collective-permute-done((bf16[48,1536]{1,0:T(8,128)(2,1)S(1)}, bf16[48,1536]{1,0:T(8,128)(2,1)S(1)}, u32[]{:S(2)}, u32[]{:S(2)}) %collective-permute-start.11) | collective-permute-done | bytes 147488 | tf_op jit(solution)/shard_map/ppermute | solution.py:29
  47.5 5.8 %collective-permute-done.10 = bf16[48,1536]{1,0:T(8,128)(2,1)S(1)} collective-permute-done((bf16[48,1536]{1,0:T(8,128)(2,1)S(1)}, bf16[48,1536]{1,0:T(8,128)(2,1)S(1)}, u32[]{:S(2)}, u32[]{:S(2)}) %collective-permute-start.10) | collective-permute-done | bytes 147488 | tf_op jit(solution)/shard_map/ppermute | solution.py:29
  53.4 2.1 collective-permute-start.19
  55.4 2.3 collective-permute-start.17
  59.5 2.6 collective-permute-done.19
  62.0 5.7 %collective-permute-done.18 = bf16[192,384]{1,0:T(8,128)(2,1)S(1)} collective-permute-done((bf16[192,384]{1,0:T(8,128)(2,1)S(1)}, bf16[192,384]{1,0:T(8,128)(2,1)S(1)}, u32[]{:S(2)}, u32[]{:S(2)}) %collective-permute-start.18) | collective-permute-done | bytes 147488 | tf_op jit(solution)/shard_map/ppermute | solution.py:29
  70.4 12.5 %collective-permute-done.20 = bf16[4,192,384]{2,1,0:T(8,128)(2,1)S(1)} collective-permute-done((bf16[4,192,384]{2,1,0:T(8,128)(2,1)S(1)}, bf16[4,192,384]{2,1,0:T(8,128)(2,1)S(1)}, u32[]{:S(2)}, u32[]{:S(2)}) %collective-permute-start.20) | collective-permute-done | bytes 589856 | tf_op jit(solution)/shard_map/ppermute | solution.py:29
  85.3 3.8 %collective-permute-done.13.refs_11_ = bf16[2,4,48,1536]{3,2,1,0:T(8,128)(2,1)} collective-permute-done((bf16[2,4,48,1536]{3,2,1,0:T(8,128)(2,1)S(1)}, bf16[2,4,48,1536]{3,2,1,0:T(8,128)(2,1)}, u32[]{:S(2)}, u32[]{:S(2)}) %collective-permute-start.13) | collective-permute-done | bytes 1179680 | tf_op jit(solution)/shard_map/ppermute | solution.py:29
  91.7 10.1 %collective-permute-done.21.refs_15_ = bf16[2,4,192,384]{3,2,1,0:T(8,128)(2,1)} collective-permute-done((bf16[2,4,192,384]{3,2,1,0:T(8,128)(2,1)}, bf16[2,4,192,384]{3,2,1,0:T(8,128)(2,1)}, u32[]{:S(2)}, u32[]{:S(2)}) %collective-permute-start.21) | collective-permute-done | bytes 1179680 | tf_op jit(solution)/shard_map/ppermute | solution.py:29
  108.9 2.4 shard_map.288
  115.2 81.0 %layer.1 = (bf16[192,768]{1,0:T(8,128)(2,1)}, bf16[192,768]{1,0:T(8,128)(2,1)}, f32[16,768]{1,0:T(8,128)}, f32[1,3072]{1,0:T(1,128)}, bf16[2,2,4,192,384]{4,3,2,...) custom-call(s32[2]{0:T(128)} %pad_add_fusion.place_ref.refs_0_, ...), custom_call_target="tpu_custom_call" | custom-call | tf_op jit(solution)/shard_map/layer/pallas_call | solution.py:639
  196.8 4.2 %collective-permute-done.27 = bf16[2,2,4,192,384]{4,3,2,1,0:T(8,128)(2,1)S(1)} collective-permute-done((bf16[2,2,4,192,384]{4,3,2,1,0:T(8,128)(2,1)}, bf16[2,2,4,192,384]{4,3,2,1,0:T(8,128)(2,1)S(1)}, u32[]{:S(2)}, u32[]{:S(2)}) %collective-permute-start.27) | collective-permute-done | bytes 2359328 | tf_op jit(solution)/shard_map/ppermute | solution.py:29
  201.0 2.3 add_convert_fusion.1
  204.8 14.8 %collective-permute-done.28 = bf16[2,4,192,384]{3,2,1,0:T(8,128)(2,1)S(1)} collective-permute-done((bf16[2,4,192,384]{3,2,1,0:T(8,128)(2,1)S(1)}, bf16[2,4,192,384]{3,2,1,0:T(8,128)(2,1)S(1)}, u32[]{:S(2)}, u32[]{:S(2)}) %collective-permute-start.28) | collective-permute-done | bytes 1179680 | tf_op jit(solution)/shard_map/ppermute | solution.py:29
  222.2 7.6 %collective-permute-done.29 = bf16[4,192,384]{2,1,0:T(8,128)(2,1)S(1)} collective-permute-done((bf16[4,192,384]{2,1,0:T(8,128)(2,1)S(1)}, bf16[4,192,384]{2,1,0:T(8,128)(2,1)S(1)}, u32[]{:S(2)}, u32[]{:S(2)}) %collective-permute-start.29) | collective-permute-done | bytes 589856 | tf_op jit(solution)/shard_map/ppermute | solution.py:29
  238.2 8.0 %collective-permute-done.30 = bf16[2,4,48,1536]{3,2,1,0:T(8,128)(2,1)} collective-permute-done((bf16[2,4,48,1536]{3,2,1,0:T(8,128)(2,1)S(1)}, bf16[2,4,48,1536]{3,2,1,0:T(8,128)(2,1)}, u32[]{:S(2)}, u32[]{:S(2)}) %collective-permute-start.30) | collective-permute-done | bytes 1179680 | tf_op jit(solution)/shard_map/ppermute | solution.py:29
  249.5 2.4 fusion
  253.7 2.8 collective-permute-start.34
  259.5 4.5 %collective-permute-done.35 = bf16[192,384]{1,0:T(8,128)(2,1)S(1)} collective-permute-done((bf16[192,384]{1,0:T(8,128)(2,1)S(1)}, bf16[192,384]{1,0:T(8,128)(2,1)S(1)}, u32[]{:S(2)}, u32[]{:S(2)}) %collective-permute-start.35) | collective-permute-done | bytes 147488 | tf_op jit(solution)/shard_map/ppermute | solution.py:29
  266.5 2.2 collective-permute-start.38
  268.7 2.2 collective-permute-start.39
  270.9 5.8 %collective-permute-done.32 = bf16[2,4,48,1664]{3,2,1,0:T(8,128)(2,1)S(1)} collective-permute-done((bf16[2,4,48,1664]{3,2,1,0:T(8,128)(2,1)S(1)}, bf16[2,4,48,1664]{3,2,1,0:T(8,128)(2,1)S(1)}, u32[]{:S(2)}, u32[]{:S(2)}) %collective-permute-start.32) | collective-permute-done | bytes 1277984 | tf_op jit(solution)/shard_map/ppermute | solution.py:29
  280.8 6.8 %collective-permute-done.33 = bf16[4,48,1664]{2,1,0:T(8,128)(2,1)S(1)} collective-permute-done((bf16[4,48,1664]{2,1,0:T(8,128)(2,1)S(1)}, bf16[4,48,1664]{2,1,0:T(8,128)(2,1)S(1)}, u32[]{:S(2)}, u32[]{:S(2)}) %collective-permute-start.33) | collective-permute-done | bytes 639008 | tf_op jit(solution)/shard_map/ppermute | solution.py:29
  287.7 2.2 collective-permute-start.41
  289.9 2.2 collective-permute-start.42
  292.2 2.9 collective-permute-done.40
  295.1 4.3 %collective-permute-done.41 = bf16[48,1664]{1,0:T(8,128)(2,1)S(1)} collective-permute-done((bf16[48,1664]{1,0:T(8,128)(2,1)S(1)}, bf16[48,1664]{1,0:T(8,128)(2,1)S(1)}, u32[]{:S(2)}, u32[]{:S(2)}) %collective-permute-start.41) | collective-permute-done | bytes 159776 | tf_op jit(solution)/shard_map/ppermute | solution.py:29
  (177 shorter events, 65.8 us)
Async XLA Ops:
  11.3 13.9 %collective-permute-start.2 = (bf16[48,1664]{1,0:T(8,128)(2,1)S(1)}, bf16[48,1664]{1,0:T(8,128)(2,1)S(1)}, u32[]{:S(2)}, u32[]{:S(2)}) collective-permute-start(bf16[48,1664]{1,0:T(8,128)(2,1)S(1)} %maximum_select_fusion.1), channel_id=1, source_target_pairs={{0,16},{1,17},{2,18},{3,19},{4,20},{5,21},{6,22},{7,23},{8,24},{9,... | collective-permute-start | bytes 479240 | tf_op jit(solution)/shard_map/ppermute | solution.py:29
  11.3 13.9 %collective-permute-start.1 = (bf16[48,1664]{1,0:T(8,128)(2,1)S(1)}, bf16[48,1664]{1,0:T(8,128)(2,1)S(1)}, u32[]{:S(2)}, u32[]{:S(2)}) collective-permute-start(bf16[48,1664]{1,0:T(8,128)(2,1)S(1)} %maximum_select_fusion.1), channel_id=1, source_target_pairs={{0,8},{1,9},{2,10},{3,11},{4,12},{5,13},{6,14},{7,15},{8,0},{9,1},... | collective-permute-start | bytes 479240 | tf_op jit(solution)/shard_map/ppermute | solution.py:29
  25.3 10.5 %collective-permute-start.4 = (bf16[4,48,1664]{2,1,0:T(8,128)(2,1)S(1)}, bf16[4,48,1664]{2,1,0:T(8,128)(2,1)S(1)}, u32[]{:S(2)}, u32[]{:S(2)}) collective-permute-start(bf16[4,48,1664]{2,1,0:T(8,128)(2,1)S(1)} %get-tuple-element.187), channel_id=1, source_target_pairs={{0,4},{1,3},{2,6},{3,1},{4,0},{5,7},{6,2},{7,5},{8,12},{9,11},{10,... | collective-permute-start | bytes 1916936 | tf_op jit(solution)/shard_map/ppermute | solution.py:29
  35.9 32.0 %collective-permute-start.5 = (bf16[2,4,48,1664]{3,2,1,0:T(8,128)(2,1)S(1)}, bf16[2,4,48,1664]{3,2,1,0:T(8,128)(2,1)}, u32[]{:S(2)}, u32[]{:S(2)}) collective-permute-start(bf16[2,4,48,1664]{3,2,1,0:T(8,128)(2,1)S(1)} %pad_maximum_fusion.refs_6_), channel_id=1, source_target_pairs={{0,2},{1,5},{2,0},{3,7},{4,6},{5,1},{6,4},{7,3},{8,10},{9,13},{10,... | collective-permute-start | bytes 3833864 | tf_op jit(solution)/shard_map/ppermute | solution.py:29
  41.4 12.0 %collective-permute-start.10 = (bf16[48,1536]{1,0:T(8,128)(2,1)S(1)}, bf16[48,1536]{1,0:T(8,128)(2,1)S(1)}, u32[]{:S(2)}, u32[]{:S(2)}) collective-permute-start(bf16[48,1536]{1,0:T(8,128)(2,1)S(1)} %maximum_select_fusion.2), channel_id=1, source_target_pairs={{0,16},{1,17},{2,18},{3,19},{4,20},{5,21},{6,22},{7,23},{8,24},{9,... | collective-permute-start | bytes 442376 | tf_op jit(solution)/shard_map/ppermute | solution.py:29
  41.4 12.0 %collective-permute-start.9 = (bf16[48,1536]{1,0:T(8,128)(2,1)S(1)}, bf16[48,1536]{1,0:T(8,128)(2,1)S(1)}, u32[]{:S(2)}, u32[]{:S(2)}) collective-permute-start(bf16[48,1536]{1,0:T(8,128)(2,1)S(1)} %maximum_select_fusion.2), channel_id=1, source_target_pairs={{0,8},{1,9},{2,10},{3,11},{4,12},{5,13},{6,14},{7,15},{8,0},{9,1},... | collective-permute-start | bytes 442376 | tf_op jit(solution)/shard_map/ppermute | solution.py:29
  55.4 12.3 %collective-permute-start.18 = (bf16[192,384]{1,0:T(8,128)(2,1)S(1)}, bf16[192,384]{1,0:T(8,128)(2,1)S(1)}, u32[]{:S(2)}, u32[]{:S(2)}) collective-permute-start(bf16[192,384]{1,0:T(8,128)(2,1)S(1)} %maximum_select_fusion.3), channel_id=1, source_target_pairs={{0,16},{1,17},{2,18},{3,19},{4,20},{5,21},{6,22},{7,23},{8,24},{9,... | collective-permute-start | bytes 442376 | tf_op jit(solution)/shard_map/ppermute | solution.py:29
  55.4 12.3 %collective-permute-start.17 = (bf16[192,384]{1,0:T(8,128)(2,1)S(1)}, bf16[192,384]{1,0:T(8,128)(2,1)S(1)}, u32[]{:S(2)}, u32[]{:S(2)}) collective-permute-start(bf16[192,384]{1,0:T(8,128)(2,1)S(1)} %maximum_select_fusion.3), channel_id=1, source_target_pairs={{0,8},{1,9},{2,10},{3,11},{4,12},{5,13},{6,14},{7,15},{8,0},{9,1},... | collective-permute-start | bytes 442376 | tf_op jit(solution)/shard_map/ppermute | solution.py:29
  57.9 11.6 %collective-permute-start.12 = (bf16[4,48,1536]{2,1,0:T(8,128)(2,1)S(1)}, bf16[4,48,1536]{2,1,0:T(8,128)(2,1)S(1)}, u32[]{:S(2)}, u32[]{:S(2)}) collective-permute-start(bf16[4,48,1536]{2,1,0:T(8,128)(2,1)S(1)} %get-tuple-element.190), channel_id=1, source_target_pairs={{0,4},{1,3},{2,6},{3,1},{4,0},{5,7},{6,2},{7,5},{8,12},{9,11},{10,... | collective-permute-start | bytes 1769480 | tf_op jit(solution)/shard_map/ppermute | solution.py:29
  67.9 15.1 %collective-permute-start.20 = (bf16[4,192,384]{2,1,0:T(8,128)(2,1)S(1)}, bf16[4,192,384]{2,1,0:T(8,128)(2,1)S(1)}, u32[]{:S(2)}, u32[]{:S(2)}) collective-permute-start(bf16[4,192,384]{2,1,0:T(8,128)(2,1)S(1)} %pad_maximum_fusion.7), channel_id=1, source_target_pairs={{0,4},{1,3},{2,6},{3,1},{4,0},{5,7},{6,2},{7,5},{8,12},{9,11},{10,... | collective-permute-start | bytes 1769480 | tf_op jit(solution)/shard_map/ppermute | solution.py:29
  69.5 21.2 %collective-permute-start.6 = (bf16[2,4,48,1664]{3,2,1,0:T(8,128)(2,1)S(1)}, bf16[2,4,48,1664]{3,2,1,0:T(8,128)(2,1)S(1)}, u32[]{:S(2)}, u32[]{:S(2)}) collective-permute-start(bf16[2,4,48,1664]{3,2,1,0:T(8,128)(2,1)S(1)} %pad_maximum_fusion.refs_6_), channel_id=1, source_target_pairs={{0,1},{1,0},{2,3},{3,2},{4,5},{5,4},{6,7},{7,6},{8,9},{9,8},{10,11... | collective-permute-start | bytes 3833864 | tf_op jit(solution)/shard_map/ppermute | solution.py:29
  69.6 19.6 %collective-permute-start.13 = (bf16[2,4,48,1536]{3,2,1,0:T(8,128)(2,1)S(1)}, bf16[2,4,48,1536]{3,2,1,0:T(8,128)(2,1)}, u32[]{:S(2)}, u32[]{:S(2)}) collective-permute-start(bf16[2,4,48,1536]{3,2,1,0:T(8,128)(2,1)S(1)} %pad_maximum_fusion.2.refs_10_), channel_id=1, source_target_pairs={{0,2},{1,5},{2,0},{3,7},{4,6},{5,1},{6,4},{7,3},{8,10},{9,13},{10,... | collective-permute-start | bytes 3538952 | tf_op jit(solution)/shard_map/ppermute | solution.py:29
  84.1 17.7 %collective-permute-start.21 = (bf16[2,4,192,384]{3,2,1,0:T(8,128)(2,1)}, bf16[2,4,192,384]{3,2,1,0:T(8,128)(2,1)}, u32[]{:S(2)}, u32[]{:S(2)}) collective-permute-start(bf16[2,4,192,384]{3,2,1,0:T(8,128)(2,1)} %pad_maximum_fusion.3.refs_14_), channel_id=1, source_target_pairs={{0,2},{1,5},{2,0},{3,7},{4,6},{5,1},{6,4},{7,3},{8,10},{9,13},{10,... | collective-permute-start | bytes 3538952 | tf_op jit(solution)/shard_map/ppermute | solution.py:29
  84.8 22.5 %collective-permute-start.7 = (bf16[2,4,48,1664]{3,2,1,0:T(8,128)(2,1)}, bf16[2,4,48,1664]{3,2,1,0:T(8,128)(2,1)}, u32[]{:S(2)}, u32[]{:S(2)}) collective-permute-start(bf16[2,4,48,1664]{3,2,1,0:T(8,128)(2,1)} %collective-permute-done.5.refs_7_), channel_id=1, source_target_pairs={{0,1},{1,0},{2,3},{3,2},{4,5},{5,4},{6,7},{7,6},{8,9},{9,8},{10,11... | collective-permute-start | bytes 3833864 | tf_op jit(solution)/shard_map/ppermute | solution.py:29
  84.8 30.4 %collective-permute-start.14 = (bf16[2,4,48,1536]{3,2,1,0:T(8,128)(2,1)S(1)}, bf16[2,4,48,1536]{3,2,1,0:T(8,128)(2,1)}, u32[]{:S(2)}, u32[]{:S(2)}) collective-permute-start(bf16[2,4,48,1536]{3,2,1,0:T(8,128)(2,1)S(1)} %pad_maximum_fusion.2.refs_10_), channel_id=1, source_target_pairs={{0,1},{1,0},{2,3},{3,2},{4,5},{5,4},{6,7},{7,6},{8,9},{9,8},{10,11... | collective-permute-start | bytes 3538952 | tf_op jit(solution)/shard_map/ppermute | solution.py:29
  89.2 26.0 %collective-permute-start.15 = (bf16[2,4,48,1536]{3,2,1,0:T(8,128)(2,1)}, bf16[2,4,48,1536]{3,2,1,0:T(8,128)(2,1)}, u32[]{:S(2)}, u32[]{:S(2)}) collective-permute-start(bf16[2,4,48,1536]{3,2,1,0:T(8,128)(2,1)} %collective-permute-done.13.refs_11_), channel_id=1, source_target_pairs={{0,1},{1,0},{2,3},{3,2},{4,5},{5,4},{6,7},{7,6},{8,9},{9,8},{10,11... | collective-permute-start | bytes 3538952 | tf_op jit(solution)/shard_map/ppermute | solution.py:29
  91.7 23.5 %collective-permute-start.22 = (bf16[2,4,192,384]{3,2,1,0:T(8,128)(2,1)}, bf16[2,4,192,384]{3,2,1,0:T(8,128)(2,1)}, u32[]{:S(2)}, u32[]{:S(2)}) collective-permute-start(bf16[2,4,192,384]{3,2,1,0:T(8,128)(2,1)} %pad_maximum_fusion.3.refs_14_), channel_id=1, source_target_pairs={{0,1},{1,0},{2,3},{3,2},{4,5},{5,4},{6,7},{7,6},{8,9},{9,8},{10,11... | collective-permute-start | bytes 3538952 | tf_op jit(solution)/shard_map/ppermute | solution.py:29
  101.8 13.4 %collective-permute-start.23 = (bf16[2,4,192,384]{3,2,1,0:T(8,128)(2,1)}, bf16[2,4,192,384]{3,2,1,0:T(8,128)(2,1)}, u32[]{:S(2)}, u32[]{:S(2)}) collective-permute-start(bf16[2,4,192,384]{3,2,1,0:T(8,128)(2,1)} %collective-permute-done.21.refs_15_), channel_id=1, source_target_pairs={{0,1},{1,0},{2,3},{3,2},{4,5},{5,4},{6,7},{7,6},{8,9},{9,8},{10,11... | collective-permute-start | bytes 3538952 | tf_op jit(solution)/shard_map/ppermute | solution.py:29
  196.3 25.2 %collective-permute-start.26 = (bf16[2,2,4,48,1536]{4,3,2,1,0:T(8,128)(2,1)}, bf16[2,2,4,48,1536]{4,3,2,1,0:T(8,128)(2,1)S(1)}, u32[]{:S(2)}, u32[]{:S(2)}) collective-permute-start(bf16[2,2,4,48,1536]{4,3,2,1,0:T(8,128)(2,1)} %get-tuple-element.51), channel_id=1, source_target_pairs={{0,1},{1,0},{2,3},{3,2},{4,5},{5,4},{6,7},{7,6},{8,9},{9,8},{10,11... | collective-permute-start | bytes 7077896 | tf_op jit(solution)/shard_map/ppermute | solution.py:29
  203.4 16.3 %collective-permute-start.28 = (bf16[2,4,192,384]{3,2,1,0:T(8,128)(2,1)S(1)}, bf16[2,4,192,384]{3,2,1,0:T(8,128)(2,1)S(1)}, u32[]{:S(2)}, u32[]{:S(2)}) collective-permute-start(bf16[2,4,192,384]{3,2,1,0:T(8,128)(2,1)S(1)} %get-tuple-element.171), channel_id=1, source_target_pairs={{0,2},{1,5},{2,0},{3,7},{4,6},{5,1},{6,4},{7,3},{8,10},{9,13},{10,... | collective-permute-start | bytes 3538952 | tf_op jit(solution)/shard_map/ppermute | solution.py:29
  204.1 45.3 %collective-permute-start.24 = (bf16[2,2,4,48,1536]{4,3,2,1,0:T(8,128)(2,1)}, bf16[2,2,4,48,1536]{4,3,2,1,0:T(8,128)(2,1)}, u32[]{:S(2)}, u32[]{:S(2)}) collective-permute-start(bf16[2,2,4,48,1536]{4,3,2,1,0:T(8,128)(2,1)} %get-tuple-element.45), channel_id=1, source_target_pairs={{0,1},{1,0},{2,3},{3,2},{4,5},{5,4},{6,7},{7,6},{8,9},{9,8},{10,11... | collective-permute-start | bytes 7077896 | tf_op jit(solution)/shard_map/ppermute | solution.py:29
  229.9 16.3 %collective-permute-start.30 = (bf16[2,4,48,1536]{3,2,1,0:T(8,128)(2,1)S(1)}, bf16[2,4,48,1536]{3,2,1,0:T(8,128)(2,1)}, u32[]{:S(2)}, u32[]{:S(2)}) collective-permute-start(bf16[2,4,48,1536]{3,2,1,0:T(8,128)(2,1)S(1)} %get-tuple-element.54), channel_id=1, source_target_pairs={{0,2},{1,5},{2,0},{3,7},{4,6},{5,1},{6,4},{7,3},{8,10},{9,13},{10,... | collective-permute-start | bytes 3538952 | tf_op jit(solution)/shard_map/ppermute | solution.py:29
  247.9 10.6 %collective-permute-start.31 = (bf16[4,48,1536]{2,1,0:T(8,128)(2,1)S(1)}, bf16[4,48,1536]{2,1,0:T(8,128)(2,1)S(1)}, u32[]{:S(2)}, u32[]{:S(2)}) collective-permute-start(bf16[4,48,1536]{2,1,0:T(8,128)(2,1)S(1)} %get-tuple-element.177), channel_id=1, source_target_pairs={{0,4},{1,3},{2,6},{3,1},{4,0},{5,7},{6,2},{7,5},{8,12},{9,11},{10,... | collective-permute-start | bytes 1769480 | tf_op jit(solution)/shard_map/ppermute | solution.py:29
  253.7 10.3 %collective-permute-start.35 = (bf16[192,384]{1,0:T(8,128)(2,1)S(1)}, bf16[192,384]{1,0:T(8,128)(2,1)S(1)}, u32[]{:S(2)}, u32[]{:S(2)}) collective-permute-start(bf16[192,384]{1,0:T(8,128)(2,1)S(1)} %get-tuple-element.182), channel_id=1, source_target_pairs={{0,16},{1,17},{2,18},{3,19},{4,20},{5,21},{6,22},{7,23},{8,24},{9,... | collective-permute-start | bytes 442376 | tf_op jit(solution)/shard_map/ppermute | solution.py:29
  253.7 10.3 %collective-permute-start.34 = (bf16[192,384]{1,0:T(8,128)(2,1)S(1)}, bf16[192,384]{1,0:T(8,128)(2,1)S(1)}, u32[]{:S(2)}, u32[]{:S(2)}) collective-permute-start(bf16[192,384]{1,0:T(8,128)(2,1)S(1)} %get-tuple-element.183), channel_id=1, source_target_pairs={{0,8},{1,9},{2,10},{3,11},{4,12},{5,13},{6,14},{7,15},{8,0},{9,1},... | collective-permute-start | bytes 442376 | tf_op jit(solution)/shard_map/ppermute | solution.py:29
  258.5 18.3 %collective-permute-start.32 = (bf16[2,4,48,1664]{3,2,1,0:T(8,128)(2,1)S(1)}, bf16[2,4,48,1664]{3,2,1,0:T(8,128)(2,1)S(1)}, u32[]{:S(2)}, u32[]{:S(2)}) collective-permute-start(bf16[2,4,48,1664]{3,2,1,0:T(8,128)(2,1)S(1)} %pad_maximum_fusion.1), channel_id=1, source_target_pairs={{0,2},{1,5},{2,0},{3,7},{4,6},{5,1},{6,4},{7,3},{8,10},{9,13},{10,... | collective-permute-start | bytes 3833864 | tf_op jit(solution)/shard_map/ppermute | solution.py:29
  266.5 12.2 %collective-permute-start.37 = (bf16[48,1536]{1,0:T(8,128)(2,1)S(1)}, bf16[48,1536]{1,0:T(8,128)(2,1)S(1)}, u32[]{:S(2)}, u32[]{:S(2)}) collective-permute-start(bf16[48,1536]{1,0:T(8,128)(2,1)S(1)} %get-tuple-element.56), channel_id=1, source_target_pairs={{0,8},{1,9},{2,10},{3,11},{4,12},{5,13},{6,14},{7,15},{8,0},{9,1},... | collective-permute-start | bytes 442376 | tf_op jit(solution)/shard_map/ppermute | solution.py:29
  266.5 14.0 %collective-permute-start.38 = (bf16[48,1536]{1,0:T(8,128)(2,1)S(1)}, bf16[48,1536]{1,0:T(8,128)(2,1)S(1)}, u32[]{:S(2)}, u32[]{:S(2)}) collective-permute-start(bf16[48,1536]{1,0:T(8,128)(2,1)S(1)} %get-tuple-element.57), channel_id=1, source_target_pairs={{0,16},{1,17},{2,18},{3,19},{4,20},{5,21},{6,22},{7,23},{8,24},{9,... | collective-permute-start | bytes 442376 | tf_op jit(solution)/shard_map/ppermute | solution.py:29
  268.7 11.8 %collective-permute-start.39 = (bf16[48,1536]{1,0:T(8,128)(2,1)S(1)}, bf16[48,1536]{1,0:T(8,128)(2,1)S(1)}, u32[]{:S(2)}, u32[]{:S(2)}) collective-permute-start(bf16[48,1536]{1,0:T(8,128)(2,1)S(1)} %get-tuple-element.58), channel_id=1, source_target_pairs={{0,24},{1,25},{2,26},{3,27},{4,28},{5,29},{6,30},{7,31},{8,16},{9,... | collective-permute-start | bytes 442376 | tf_op jit(solution)/shard_map/ppermute | solution.py:29
  277.1 10.5 %collective-permute-start.33 = (bf16[4,48,1664]{2,1,0:T(8,128)(2,1)S(1)}, bf16[4,48,1664]{2,1,0:T(8,128)(2,1)S(1)}, u32[]{:S(2)}, u32[]{:S(2)}) collective-permute-start(bf16[4,48,1664]{2,1,0:T(8,128)(2,1)S(1)} %get-tuple-element.173), channel_id=1, source_target_pairs={{0,4},{1,3},{2,6},{3,1},{4,0},{5,7},{6,2},{7,5},{8,12},{9,11},{10,... | collective-permute-start | bytes 1916936 | tf_op jit(solution)/shard_map/ppermute | solution.py:29
  280.7 11.4 %collective-permute-start.44 = (f32[24,1536]{1,0:T(8,128)S(1)}, f32[24,1536]{1,0:T(8,128)S(1)}, u32[]{:S(2)}, u32[]{:S(2)}) collective-permute-start(f32[24,1536]{1,0:T(8,128)S(1)} %slice_select_fusion.4), channel_id=1, source_target_pairs={{0,1},{1,0},{2,3},{3,2},{4,5},{5,4},{6,7},{7,6},{8,9},{9,8},{10,11... | collective-permute-start | bytes 442376 | tf_op jit(solution)/shard_map/ppermute | solution.py:29
  287.7 11.6 %collective-permute-start.41 = (bf16[48,1664]{1,0:T(8,128)(2,1)S(1)}, bf16[48,1664]{1,0:T(8,128)(2,1)S(1)}, u32[]{:S(2)}, u32[]{:S(2)}) collective-permute-start(bf16[48,1664]{1,0:T(8,128)(2,1)S(1)} %get-tuple-element.60), channel_id=1, source_target_pairs={{0,16},{1,17},{2,18},{3,19},{4,20},{5,21},{6,22},{7,23},{8,24},{9,... | collective-permute-start | bytes 479240 | tf_op jit(solution)/shard_map/ppermute | solution.py:29
  (26 other events, 180.7 us)
where the time goes:
time: 311 us; the launch traced here: 305 us
  waiting for transfers between devices  135 us (43%)
  Pallas kernels  85.1 us (27%)
  starting transfers between devices  48.5 us (16%)
  other arithmetic  17.3 us (6%)
  local copies, waits for them, and re-layouts  17.1 us (5%)
    ppermute x46, waiting for transfers between devices, send(): return lax.ppermute(x, AXES, route)  135 us
    pallas_call x1, Pallas kernels, layer(): pl.pallas_call(functools.partial(layer_kernel, known), out_shape=[struct(...  81 us
    ppermute x46, starting transfers between devices, send(): return lax.ppermute(x, AXES, route)  48.5 us
    convert_element_type x10, other arithmetic, add_low(): return (a.astype(F32) + b.astype(F32)).astype(BF16)  9.05 us
  transfers between devices with their start and end apart: 46, of which 27 were waited for; matrix products, arithmetic and copies ran while one was open for 8% of the time, Pallas kernels for 1%

commit v1 on v0

v1 whole, which is shorter than its diff:
```python
import functools
import math

import jax
import jax.numpy as jnp
from jax import lax
from jax.experimental import pallas as pl
from jax.experimental.pallas import tpu as pltpu
from jax.sharding import PartitionSpec as P

HEAD_DIM = 64
PASSES = 3
EPSILON = 1e-05
AXES = ("dp", "fsdp")
F32 = jnp.float32
BF16 = jnp.bfloat16


def pairs(partner):
    return [(i, partner(i)) for i in range(32)]


TO_MATE = pairs(lambda i: i ^ 1)
TO_Z = [pairs(lambda i, k=k: i ^ (8 * k)) for k in range(4)]
TO_NEAR = pairs(lambda i: i ^ (2 if i & 1 else 4))
TO_FAR = pairs(lambda i: i ^ (4 if i & 1 else 2))


def send(x, route):
    return lax.ppermute(x, AXES, route)


def after(x, *earlier):
    earlier = tuple(e for e in earlier if e is not None)
    return lax.optimization_barrier((x, earlier))[0] if earlier else x


def in_core_order(core, mine, other, axis):
    return jnp.where(
        core == 0,
        jnp.concatenate([mine, other], axis=axis),
        jnp.concatenate([other, mine], axis=axis),
    )


def stack_kernel(*refs):
    for n, ref in enumerate(refs[:-1]):
        refs[-1][n] = ref[...]


def stack_blocks(blocks, weight):
    if not weight:
        return jnp.stack(blocks)
    return pl.pallas_call(
        stack_kernel,
        out_shape=jax.ShapeDtypeStruct((len(blocks), *blocks[0].shape), BF16),
        in_specs=[pl.BlockSpec(memory_space=pltpu.VMEM)] * len(blocks),
        out_specs=pl.BlockSpec(memory_space=pltpu.VMEM),
        compiler_params=pltpu.CompilerParams(vmem_limit_bytes=8 * 2**20),
        cost_estimate=pl.CostEstimate(flops=weight * 10**9, bytes_accessed=weight * 35 * 10**5, transcendentals=0),
        name="stack",
    )(*blocks)


STACK_WEIGHTS = (0, 0, 10)
BOTH_WEIGHTS = (10, 0, 0)


def gather_chunks(blocks):
    chunks, earlier = [], None
    for n, block in enumerate(blocks):
        block = after(block, earlier)
        earlier = [send(block, TO_Z[k]) for k in (1, 2, 3)]
        stack = stack_blocks([block] + earlier, STACK_WEIGHTS[n])
        both = stack_blocks([stack, send(stack, TO_NEAR)], BOTH_WEIGHTS[n])
        chunks.append([both, None, send(both, TO_MATE), None])
    return chunks, earlier


def far_pieces(pieces, *earlier):
    if pieces[1] is None:
        pieces[1] = send(after(pieces[0], *earlier), TO_FAR)


def mate_pieces(pieces, *earlier):
    if pieces[3] is None:
        pieces[3] = send(after(pieces[1], *earlier), TO_MATE)


def chip_of(place, swapped, far, near, z):
    chip, core = place
    order = core ^ swapped
    near_bit = 2 - order
    far_bit = 1 + order
    return chip ^ (far * far_bit) ^ (near * near_bit) ^ (z * 4)


def add_low(a, b):
    return (a.astype(F32) + b.astype(F32)).astype(BF16)


def add_kernel(got, keep, give_out, keep_out):
    for n in range(got.shape[1]):
        give_out[n] = (keep[1, n].astype(F32) + got[1, n].astype(F32)).astype(BF16)
        keep_out[n] = (keep[0, n].astype(F32) + got[0, n].astype(F32)).astype(BF16)


def add_halves(got, keep, weight):
    if not weight:
        return add_low(keep[1], got[1]), add_low(keep[0], got[0])
    shape, merged = keep.shape[1:], (2, -1, keep.shape[-2], keep.shape[-1])
    got, keep = got.reshape(merged), keep.reshape(merged)
    give, keep = pl.pallas_call(
        add_kernel,
        out_shape=[jax.ShapeDtypeStruct(keep.shape[1:], BF16)] * 2,
        in_specs=[pl.BlockSpec(memory_space=pltpu.VMEM)] * 2,
        out_specs=[pl.BlockSpec(memory_space=pltpu.VMEM)] * 2,
        compiler_params=pltpu.CompilerParams(vmem_limit_bytes=8 * 2**20),
        cost_estimate=pl.CostEstimate(flops=weight * 10**9, bytes_accessed=weight * 35 * 10**5, transcendentals=0),
        name="add",
    )(got, keep)
    return give.reshape(shape), keep.reshape(shape)


def begin_scatter(give, keep, weight):
    if not is_known_slice():
        return give, keep
    split = lambda a: a.reshape(2, 2, 4, *a.shape[1:])
    return add_halves(split(send(give, TO_MATE)), split(keep), weight)


def far_step(part):
    give, keep = part
    if not is_known_slice():
        return part
    return send(give, TO_FAR), keep


def near_step(part, weight):
    got, keep = part
    if not is_known_slice():
        return part
    give, keep = add_halves(got, keep, weight)
    return send(give, TO_NEAR), keep


def end_scatter(core, begun):
    begun = [begun[0]] + [near_step(begun[n], FAR_WEIGHTS[n]) for n in (1, 2)]
    results, earlier = [], None
    for n in range(len(begun)):
        near, keep = begun[n]
        z = [add_low(keep[k], near[k]) for k in (1, 2, 3)]
        z = [send(give, TO_Z[k + 1]) for k, give in enumerate(after(z, earlier))]
        earlier = z if n == 0 else None
        total = keep[0].astype(F32) + near[0].astype(F32)
        for part in z:
            total = total + part.astype(F32)
        total = total.reshape(2, total.shape[0] // 2, total.shape[1])
        mine = jnp.where(core == 0, total[0], total[1])
        other = send(jnp.where(core == 0, total[1], total[0]), TO_MATE)
        results.append((jnp.where(core == 0, mine, other), jnp.where(core == 0, other, mine)))
    return results


MATE_WEIGHTS = (0, 15, 0)
FAR_WEIGHTS = (0, 0, 0)
SMALL = 256


def pack_small(vectors, bias_up, pass_embed):
    rows = vectors[0].shape[0]
    first = jnp.stack(vectors, axis=1)
    second = jnp.concatenate([bias_up.reshape(rows, -1), pass_embed.T], axis=1)
    pad = lambda a: jnp.pad(a, ((0, 0), (0, SMALL // 2 - a.shape[1])))
    return jnp.concatenate([pad(first), pad(second)], axis=1)


def unpack_small(small):
    half = SMALL // 2
    vectors = [small[:, k] for k in range(8)]
    return vectors, small[:, half : half + 4].reshape(-1), small[:, half + 4 : half + 4 + PASSES].T


def is_known_slice():
    return lax.axis_size("dp") == 8 and lax.axis_size("fsdp") == 4


def place_of():
    if not is_known_slice():
        return jnp.zeros((2,), jnp.int32)
    index = lax.axis_index("dp") * 4 + lax.axis_index("fsdp")
    return jnp.stack([index >> 1, index & 1]).astype(jnp.int32)


def halves(*arrays):
    return [
        jnp.concatenate([a[:, h * (a.shape[1] // 2) : (h + 1) * (a.shape[1] // 2)] for a in arrays], axis=1)
        for h in range(2)
    ]


def slots(swapped):
    return [chip_of((0, 0), swapped, far, near, z) for far in range(2) for near in range(2) for z in range(4)]


def gather_all(w_qkv, w_out, small, w_up, w_down):
    place = place_of()
    groups = ((w_qkv, small), (w_up, w_out), (w_down,))
    if not is_known_slice():
        chunks = []
        for arrays in groups:
            whole = [lax.all_gather(a, AXES, axis=0, tiled=True) for a in arrays]
            pieces = []
            for swapped, part in enumerate(halves(*whole)):
                blocks = part.reshape(16, -1, part.shape[1])
                blocks = jnp.stack([blocks[chip] for chip in slots(swapped)])
                pieces += list(blocks.reshape(2, 2, 4, *blocks.shape[1:]))
            chunks.append(pieces)
        return place, chunks, ()
    core = place[1]
    blocks = []
    for arrays in groups:
        low, high = halves(*arrays)
        mine = jnp.where(core == 0, low, high)
        other = send(jnp.where(core == 0, high, low), TO_MATE)
        blocks.append(in_core_order(core, mine, other, 0))
    chunks, last_z = gather_chunks(blocks)
    return place, chunks, last_z


def scatter_all(parts):
    if is_known_slice():
        sums = end_scatter(place_of()[1], list(parts))
    else:
        sums = []
        for give, keep in parts:
            both = []
            for blocks, swapped in ((keep, 0), (give, 1)):
                order = slots(swapped)
                whole = jnp.concatenate([blocks[order.index(chip)] for chip in range(16)], axis=0)
                both.append(lax.psum_scatter(whole.astype(F32), AXES, scatter_dimension=0, tiled=True))
            sums.append(both)
    join = lambda n, first, width: jnp.concatenate([s[:, first : first + width] for s in sums[n]], axis=1)
    small_half = SMALL // 2
    qkv_half = sums[2][0].shape[1] - small_half
    out_half = qkv_half // 3
    up_half_ = sums[1][0].shape[1] - out_half
    return [
        join(2, 0, qkv_half),
        join(1, up_half_, out_half),
        join(1, 0, up_half_),
        join(0, 0, sums[0][0].shape[1]),
        join(2, qkv_half, small_half),
    ]


BIAS_Q, BIAS_V, BIAS_OUT, GAIN_ATTN, SHIFT_ATTN, GAIN_MLP, SHIFT_MLP, BIAS_DOWN, EMBED = range(9)
VECTORS = 16
PAIR = 2 * HEAD_DIM
SCALE = HEAD_DIM**-0.5
LOG2_E = 1.4426950408889634
GELU_A = 0.7978845608028654
GELU_B = 0.044715
LN_ROWS = 32
COST = (10 * 10**9, 35 * 2**20)
SOFT_ROWS = 64
WIDE = 256


def dot(a, b, a_dim, b_dim):
    return lax.dot_general(a, b, (((a_dim,), (b_dim,)), ((), ())), preferred_element_type=F32)


def nn(a, b):
    return dot(a, b, 1, 0)


def nt(a, b):
    return dot(a, b, 1, 1)


def tn(a, b):
    return dot(a, b, 0, 0)


def cols(n, size):
    return pl.ds(pl.multiple_of(n * size, size), size)


def row_mean(x):
    return jnp.sum(x, axis=1, keepdims=True) * (1.0 / x.shape[1])


def normalized(x):
    centred = x - row_mean(x)
    inverse = lax.rsqrt(row_mean(centred * centred) + EPSILON)
    return centred * inverse, inverse


def gelu_and_slope(v):
    square = v * v
    t = jnp.tanh(v * (GELU_A + (GELU_A * GELU_B) * square))
    half = 0.5 * (1.0 + t)
    slope = half + v * (1.0 - t * t) * (0.5 * GELU_A + (1.5 * GELU_A * GELU_B) * square)
    return v * half, slope


def iota(shape, dim):
    return lax.broadcasted_iota(jnp.int32, shape, dim)


def first_lanes():
    return iota((1, PAIR), 1) < HEAD_DIM


def stacked(x):
    low = first_lanes().astype(F32)
    return jnp.concatenate([x * low.astype(BF16), x * (1.0 - low).astype(BF16)], axis=0)


def unstacked(x):
    length = x.shape[0] // 2
    return jnp.where(first_lanes(), x[:length], x[length:])


def fetch(place_ref, pieces, targets, sems):
    place = (place_ref[0], place_ref[1])
    for source, swapped, far in zip(pieces, (0, 0, 1, 1), (0, 1, 0, 1)):
        half = place[1] ^ swapped
        rows = source.shape[2]
        for near in range(2):
            for z in range(4):
                chip = chip_of(place, swapped, far, near, z)
                first = 0
                for n, full in enumerate(targets):
                    width = full.shape[1] // 2
                    pltpu.make_async_copy(
                        source.at[near, z, :, pl.ds(first, width)],
                        full.at[
                            pl.ds(pl.multiple_of(chip * rows, 16), rows),
                            pl.ds(pl.multiple_of(half * width, 128), width),
                        ],
                        sems.at[n],
                    ).start()
                    first += width


def wait_whole(full, sem):
    pltpu.make_async_copy(full, full, sem).wait()


def slot_of(place_ref, swapped, chip):
    apart = chip ^ place_ref[0]
    order = place_ref[1] ^ swapped
    x, y = apart & 1, (apart >> 1) & 1
    far = x + order * (y - x)
    near = y + order * (x - y)
    return far * 8 + near * 4 + (apart >> 2)


def put_blocks(place_ref, swapped, target, value, first_chip, first_col):
    rows = target.shape[1]
    for n in range(value.shape[0] // rows):
        slot = slot_of(place_ref, swapped, first_chip + n)
        target[slot, :, first_col : first_col + value.shape[1]] = value[n * rows : (n + 1) * rows, :]


def half_start(place_ref, swapped, width):
    return pl.multiple_of((place_ref[1] ^ swapped) * width, 128)


def pick_vectors(offset, first, last):
    row, col = iota((VECTORS, SMALL // 2), 0), iota((VECTORS, SMALL // 2), 1)
    return ((col == row + offset) & (row >= first) & (row < last)).astype(F32).astype(BF16)


def spread_four():
    row, col = iota((SMALL // 2, WIDE), 0), iota((SMALL // 2, WIDE), 1)
    return ((row < 4) & ((col & 3) == row)).astype(F32).astype(BF16)


def own_lanes():
    return (iota((WIDE // 4, WIDE), 1) >> 2) == iota((WIDE // 4, WIDE), 0)


def norm_forward(source, at, length, vec, gain, shift, target, to):
    for b in range(0, length, LN_ROWS):
        n, _ = normalized(source[at + b : at + b + LN_ROWS, :])
        target[to + b : to + b + LN_ROWS, :] = (n * vec[gain : gain + 1, :] + vec[shift : shift + 1, :]).astype(BF16)


def norm_backward(source, at, extra, state, vec, gain, shift, g_vec, rounded, to, embed):
    for b in range(0, state.shape[0], LN_ROWS):
        part = slice(b, b + LN_ROWS)
        n, inverse = normalized(source[at + b : at + b + LN_ROWS, :])
        e = extra[part, :]
        g_vec[gain : gain + 1, :] += jnp.sum(e * n, axis=0, keepdims=True)
        g_vec[shift : shift + 1, :] += jnp.sum(e, axis=0, keepdims=True)
        eg = e * vec[gain : gain + 1, :]
        back = state[part, :] + inverse * (eg - row_mean(eg) - n * row_mean(eg * n))
        state[part, :] = back
        if rounded is not None:
            rounded[to + b : to + b + LN_ROWS, :] = back.astype(BF16)
        if embed is not None:
            g_vec[embed : embed + 1, :] += jnp.sum(back, axis=0, keepdims=True)


def attend(j, q, k, v, probs, scores, mask, context, at, seen):
    length = mask.shape[0]
    mine = pl.ds(at, length)
    c = cols(j, PAIR)
    scores[:, :seen] = nt(stacked(q[mine, c]), k[:seen, c])
    for b in range(0, 2 * length, SOFT_ROWS):
        part = slice(b, b + SOFT_ROWS)
        m = b % length
        s = scores[part, :seen] + mask[m : m + SOFT_ROWS, :seen]
        p = jnp.exp2((s - jnp.max(s, axis=1, keepdims=True)) * (SCALE * LOG2_E))
        p = p * (1.0 / jnp.sum(p, axis=1, keepdims=True))
        probs[j, part, :] = p.astype(BF16)
    context[mine, c] = unstacked(nn(probs[j], v[:seen, c])).astype(BF16)


def attend_back(j, q, k, v, probs, scores, d_scores, d_context, context, at, seen, d_query, k_grad, v_grad, fresh):
    length = d_context.shape[0]
    mine = pl.ds(at, length)
    c = cols(j, PAIR)
    dc = d_context[:, c]
    both = stacked(dc)
    scores[:, :seen] = nt(both, v[:seen, c])
    product = dc.astype(F32) * context[mine, c].astype(F32)
    inner_0 = jnp.sum(jnp.where(first_lanes(), product, 0.0), axis=1, keepdims=True)
    inner_1 = jnp.sum(jnp.where(first_lanes(), 0.0, product), axis=1, keepdims=True)
    for b in range(0, 2 * length, SOFT_ROWS):
        part = slice(b, b + SOFT_ROWS)
        m = b % length
        shift = (inner_0 if b < length else inner_1)[m : m + SOFT_ROWS]
        d_scores[part, :seen] = (probs[j, part, :].astype(F32) * (scores[part, :seen] - shift)).astype(BF16)
    ds = d_scores[:, :seen]
    d_query[mine, c] = (unstacked(nn(ds, k[:seen, c])) * SCALE).astype(BF16)
    k_more = tn(ds, stacked(q[mine, c]))
    v_more = tn(probs[j], both)
    if fresh:
        k_grad[:seen, c] = k_more
        v_grad[:seen, c] = v_more
    else:
        k_grad[:seen, c] += k_more
        v_grad[:seen, c] += v_more


def feed_up(x_mlp, at, length, w_up, bias_up, active, slope, to):
    def step(j, _):
        c = cols(j, WIDE)
        value, rise = gelu_and_slope(nn(x_mlp[pl.ds(at, length), :], w_up[:, c]) + bias_up[:, c])
        active[pl.ds(to, length), c] = value.astype(BF16)
        slope[pl.ds(to, length), c] = rise.astype(BF16)

    lax.fori_loop(0, w_up.shape[1] // WIDE, step, None, unroll=6)


def project_in(x_norm, at, length, w_qkv, vec, targets, to):
    width = w_qkv.shape[0]
    for part, (target, bias) in enumerate(zip(targets, (BIAS_Q, None, BIAS_V))):
        for c in range(0, width, WIDE):
            acc = nn(x_norm[at : at + length, :], w_qkv[:, part * width + c : part * width + c + WIDE])
            if bias is not None:
                acc = acc + vec[bias : bias + 1, c : c + WIDE]
            target[to[part] : to[part] + length, c : c + WIDE] = acc.astype(BF16)


def project_out(context, at, length, w_out, vec, entry, middle):
    for c in range(0, w_out.shape[1], WIDE):
        acc = nn(context[at : at + length, :], w_out[:, c : c + WIDE])
        middle[at : at + length, c : c + WIDE] = (
            entry[at : at + length, c : c + WIDE] + acc + vec[BIAS_OUT : BIAS_OUT + 1, c : c + WIDE]
        )


def feed_down(active, at, length, w_down, vec, middle, middle_at, state):
    for c in range(0, w_down.shape[1], WIDE):
        acc = nn(active[at : at + length, :], w_down[:, c : c + WIDE])
        state[:, c : c + WIDE] = (
            middle[middle_at : middle_at + length, c : c + WIDE] + acc + vec[BIAS_DOWN : BIAS_DOWN + 1, c : c + WIDE]
        )


def enter(state, r, vec, entry, at):
    for b in range(0, state.shape[0], LN_ROWS):
        entry[at + b : at + b + LN_ROWS, :] = state[b : b + LN_ROWS, :].astype(F32) + vec[EMBED + r : EMBED + r + 1, :]


def start_kernel(
    place_ref, lengths_ref, tokens, p0, p1, p2, p3,
    w_qkv, vec, bias_up, mask, x_norm, q, k, v, probs, context, entry,
    small, scores, sems,
):
    length, width = tokens.shape
    fetch(place_ref, (p0, p1, p2, p3), (w_qkv, small), sems)

    rows_at, keys_at = iota(mask.shape, 0), iota(mask.shape, 1)
    for _ in range(PASSES - 1):
        keys_at = jnp.where(keys_at >= length, keys_at - length, keys_at)
    same = keys_at <= rows_at
    end = 0
    for n in range(lengths_ref.shape[0]):
        end = end + lengths_ref[n]
        same = same & ((rows_at >= end) == (keys_at >= end))
    mask[...] = jnp.where(same, 0.0, -1e30)

    wait_whole(small, sems.at[1])
    side = SMALL // 2
    vec[...] = nt(pick_vectors(0, 0, EMBED), small[:, :side]) + nt(
        pick_vectors(4 - EMBED, EMBED, EMBED + PASSES), small[:, side:]
    )
    repeated = nn(small[:, side:], spread_four())
    for b in range(bias_up.shape[1] // WIDE):
        rows = repeated[b * (WIDE // 4) : (b + 1) * (WIDE // 4), :]
        bias_up[:, b * WIDE : (b + 1) * WIDE] = jnp.sum(jnp.where(own_lanes(), rows, 0.0), axis=0, keepdims=True)

    enter(tokens, 0, vec, entry, 0)
    norm_forward(entry, 0, length, vec, GAIN_ATTN, SHIFT_ATTN, x_norm, 0)
    wait_whole(w_qkv, sems.at[0])
    project_in(x_norm, 0, length, w_qkv, vec, (q, k, v), (0, 0, 0))

    def pair(j, _):
        attend(j, q, k, v, probs, scores, mask, context, 0, length)

    lax.fori_loop(0, width // PAIR, pair, None)


def up_kernel(
    place_ref, context, vec, bias_up, entry, p0, p1, p2, p3, w_up, w_out, middle, x_mlp, active, slope, sems
):
    length = context.shape[0]
    fetch(place_ref, (p0, p1, p2, p3), (w_up, w_out), sems)
    wait_whole(w_out, sems.at[1])
    project_out(context, 0, length, w_out, vec, entry, middle)
    norm_forward(middle, 0, length, vec, GAIN_MLP, SHIFT_MLP, x_mlp, 0)
    wait_whole(w_up, sems.at[0])
    feed_up(x_mlp, 0, length, w_up, bias_up, active, slope, 0)


def down_half(place_ref, swapped, active_0, active, d_z, target):
    length = active_0.shape[0]
    width = target.shape[2]
    step = 2 * target.shape[1]
    half = pl.ds(half_start(place_ref, swapped, width), width)

    def some(j, _):
        c = cols(j, step)
        grad = tn(active_0[:, c], d_z[:length, half]) + tn(active[:, c], d_z[length:, half])
        put_blocks(place_ref, swapped, target, grad.astype(BF16), 2 * j, 0)

    lax.fori_loop(0, active_0.shape[1] // step, some, None, unroll=2)


def main_kernel(
    place_ref, cotangent, vec, bias_up, mask, w_qkv, w_out, w_up, k_0, v_0, middle_0, active_0, slope_0, p0, p1, p2, p3,
    output, state, g_vec, x_norm, context, x_mlp, active, d_hidden_0, d_hidden, d_z, d_y, d_mixed, k_grad_0, v_grad_0,
    w_down, q, k_all, v_all, probs_1, probs_2, entry, middle, k_grad, v_grad, extra, d_context, scores, d_scores, sems,
):
    probs = (None, probs_1, probs_2)
    length, width = state.shape
    inner = w_up.shape[1]
    pair_count = width // PAIR
    fetch(place_ref, (p0, p1, p2, p3), (w_down,), sems)
    g_vec[...] = jnp.zeros(g_vec.shape, F32)
    k_all[:length, :] = k_0[...]
    v_all[:length, :] = v_0[...]
    wait_whole(w_down, sems.at[0])
    feed_down(active_0, 0, length, w_down, vec, middle_0, 0, state)

    for r in range(1, PASSES):
        at, seen = (r - 1) * length, (r + 1) * length
        enter(state, r, vec, entry, at)
        norm_forward(entry, at, length, vec, GAIN_ATTN, SHIFT_ATTN, x_norm, at)
        project_in(x_norm, at, length, w_qkv, vec, (q, k_all, v_all), (at, r * length, r * length))

        def pair(j, _):
            attend(j, q, k_all, v_all, probs[r], scores, mask, context, at, seen)

        lax.fori_loop(0, pair_count, pair, None)
        project_out(context, at, length, w_out, vec, entry, middle)
        norm_forward(middle, at, length, vec, GAIN_MLP, SHIFT_MLP, x_mlp, at)
        feed_up(x_mlp, at, length, w_up, bias_up, active, d_hidden, at)
        feed_down(active, at, length, w_down, vec, middle, at, state)

    for b in range(0, length, 64):
        output[b : b + 64, :] = state[b : b + 64, :].astype(BF16)
        state[b : b + 64, :] = cotangent[b : b + 64, :].astype(F32)

    def through_down(r, slope, target, to):
        for b in range(0, length, 64):
            d_z[r * length + b : r * length + b + 64, :] = state[b : b + 64, :].astype(BF16)

        def step(j, _):
            c = cols(j, WIDE)
            acc = nt(d_z[r * length : (r + 1) * length, :], w_down[c, :])
            rows = pl.ds(to, length)
            target[rows, c] = (acc * slope[rows, c].astype(F32)).astype(BF16)

        lax.fori_loop(0, inner // WIDE, step, None, unroll=6)

    for r in reversed(range(1, PASSES)):
        at, seen = (r - 1) * length, (r + 1) * length
        mine = pl.ds(at, length)
        through_down(r, d_hidden, d_hidden, at)
        for c in range(0, width, WIDE):
            extra[:, c : c + WIDE] = nt(d_hidden[mine, :], w_up[c : c + WIDE, :])
        norm_backward(middle, at, extra, state, vec, GAIN_MLP, SHIFT_MLP, g_vec, d_y, at, None)
        for c in range(0, width, WIDE):
            d_context[:, c : c + WIDE] = nt(d_y[mine, :], w_out[c : c + WIDE, :]).astype(BF16)

        def pair_back(j, _):
            attend_back(
                j, q, k_all, v_all, probs[r], scores, d_scores, d_context, context, at, seen, d_mixed, k_grad, v_grad,
                r == PASSES - 1,
            )

        lax.fori_loop(0, pair_count, pair_back, None)
        for b in range(0, length, 64):
            part = slice(at + b, at + b + 64)
            made = slice(r * length + b, r * length + b + 64)
            d_mixed[part, width : 2 * width] = (k_grad[made, :] * SCALE).astype(BF16)
            d_mixed[part, 2 * width :] = v_grad[made, :].astype(BF16)
        for c in range(0, width, WIDE):
            extra[:, c : c + WIDE] = nt(d_mixed[mine, :], w_qkv[c : c + WIDE, :])
        norm_backward(entry, at, extra, state, vec, GAIN_ATTN, SHIFT_ATTN, g_vec, None, 0, EMBED + r)

    k_grad_0[...] = k_grad[:length, :]
    v_grad_0[...] = v_grad[:length, :]
    through_down(0, slope_0, d_hidden_0, 0)
    g_vec[BIAS_DOWN : BIAS_DOWN + 1, :] = nn(jnp.ones((16, PASSES * length), BF16), d_z[...])[:1]


def give_down_kernel(place_ref, active_0, active, d_z, give):
    down_half(place_ref, 1, active_0, active, d_z, give)


def keep_down_kernel(place_ref, active_0, active, d_z, keep):
    down_half(place_ref, 0, active_0, active, d_z, keep)


def up_half(place_ref, swapped, x_0, x, d_0, d, target, first_col, source_col, width):
    size = 384 if width % 384 == 0 else width
    start = half_start(place_ref, swapped, width)
    for c in range(0, width, size):
        part = pl.ds(pl.multiple_of(start + (source_col + c), 128), size)
        grad = tn(x_0[...], d_0[:, part]) + tn(x[...], d[:, part])
        put_blocks(place_ref, swapped, target, grad.astype(BF16), 0, first_col + c)


def give_up_kernel(
    place_ref, vec, w_up, w_out, x_mlp_0, x_mlp, d_hidden_0, d_hidden, middle_0, state_in, g_vec_in, context_0, context, d_y_1,
    give, state, g_vec, d_y, d_context,
    extra,
):
    width, inner = state.shape[1], w_up.shape[1]
    up_half(place_ref, 1, x_mlp_0, x_mlp, d_hidden_0, d_hidden, give, 0, 0, inner // 2)
    for c in range(0, width, WIDE):
        extra[:, c : c + WIDE] = nt(d_hidden_0[...], w_up[c : c + WIDE, :])
    state[...] = state_in[...]
    g_vec[...] = g_vec_in[...]
    norm_backward(middle_0, 0, extra, state, vec, GAIN_MLP, SHIFT_MLP, g_vec, d_y, 0, None)
    for c in range(0, width, WIDE):
        d_context[:, c : c + WIDE] = nt(d_y[...], w_out[c : c + WIDE, :]).astype(BF16)
    up_half(place_ref, 1, context_0, context, d_y, d_y_1, give, inner // 2, 0, width // 2)


def keep_up_kernel(
    place_ref, x_mlp_0, x_mlp, d_hidden_0, d_hidden, context_0, context, d_y_0, d_y, keep, g_bias_up
):
    width, inner = x_mlp.shape[1], d_hidden.shape[1]
    up_half(place_ref, 0, x_mlp_0, x_mlp, d_hidden_0, d_hidden, keep, 0, 0, inner // 2)
    up_half(place_ref, 0, context_0, context, d_y_0, d_y, keep, inner // 2, 0, width // 2)
    ones = jnp.ones((16, x_mlp.shape[0]), BF16)
    length = x_mlp_0.shape[0]

    def step(j, _):
        c = cols(j, 768)
        g_bias_up[:, c] = (nn(ones[:, :length], d_hidden_0[:, c]) + nn(ones, d_hidden[:, c]))[:1]

    lax.fori_loop(0, g_bias_up.shape[1] // 768, step, None)


def last_kernel(
    place_ref, vec, w_qkv, q, k, v, probs, context_0, d_context, d_y_0, d_y, d_mixed, entry, k_grad_0, v_grad_0, state_in,
    g_vec_in, g_bias_up,
    token_grad, d_mixed_0, small,
    k_grad, v_grad, state, g_vec, extra, scores, d_scores,
):
    length, width = state.shape
    k_grad[...] = k_grad_0[...]
    v_grad[...] = v_grad_0[...]
    state[...] = state_in[...]
    g_vec[...] = g_vec_in[...]

    def pair_back(j, _):
        attend_back(
            j, q, k, v, probs, scores, d_scores, d_context, context_0, 0, length, d_mixed_0, k_grad, v_grad, False
        )

    lax.fori_loop(0, width // PAIR, pair_back, None)
    for b in range(0, length, 64):
        part = slice(b, b + 64)
        d_mixed_0[part, width : 2 * width] = (k_grad[part, :] * SCALE).astype(BF16)
        d_mixed_0[part, 2 * width :] = v_grad[part, :].astype(BF16)
    for c in range(0, width, WIDE):
        extra[:, c : c + WIDE] = nt(d_mixed_0[...], w_qkv[c : c + WIDE, :])
    norm_backward(entry, 0, extra, state, vec, GAIN_ATTN, SHIFT_ATTN, g_vec, None, 0, EMBED)
    for b in range(0, length, 64):
        token_grad[b : b + 64, :] = state[b : b + 64, :].astype(BF16)

    ones = jnp.ones((16, 2 * length), BF16)

    def sums(d_0, d):
        return (nn(ones[:, :length], d_0) + nn(ones, d))[:1]

    g_vec[BIAS_Q : BIAS_Q + 1, :] = sums(d_mixed_0[:, :width], d_mixed[:, :width])
    g_vec[BIAS_V : BIAS_V + 1, :] = sums(d_mixed_0[:, 2 * width :], d_mixed[:, 2 * width :])
    g_vec[BIAS_OUT : BIAS_OUT + 1, :] = sums(d_y_0[...], d_y[...])
    vectors = g_vec[...].astype(BF16)
    four = []
    for b in range(g_bias_up.shape[1] // WIDE):
        four.append(jnp.where(own_lanes(), g_bias_up[:, b * WIDE : (b + 1) * WIDE], 0.0).astype(BF16))
    second = tn(vectors, pick_vectors(4 - EMBED, EMBED, EMBED + PASSES)) + nt(
        jnp.concatenate(four, axis=0), spread_four()
    )
    small[:, : SMALL // 2] = tn(vectors, pick_vectors(0, 0, EMBED)).astype(BF16)
    small[:, SMALL // 2 :] = second.astype(BF16)


def qkv_kernel(swapped, place_ref, x_norm_0, x_norm, d_mixed_0, d_mixed, small, target):
    wide = d_mixed.shape[1] // 2
    up_half(place_ref, swapped, x_norm_0, x_norm, d_mixed_0, d_mixed, target, 0, 0, wide)
    side = SMALL // 2
    put_blocks(place_ref, swapped, target, small[:, pl.ds(half_start(place_ref, swapped, side), side)], 0, wide)


def call(kernel, name, inputs, outputs, scratch, flops, touched):
    size = lambda shape, dtype: math.prod(shape) * jnp.dtype(dtype).itemsize
    need = sum(size(*s) for s in scratch if isinstance(s, tuple))
    results = [pltpu.VMEM(shape, dtype) if stays else jax.ShapeDtypeStruct(shape, dtype) for shape, dtype, stays in outputs]
    extra = sum(size(shape, dtype) for shape, dtype, stays in outputs if not stays)
    return pl.pallas_call(
        kernel,
        out_shape=results,
        in_specs=[pl.BlockSpec(memory_space=memory) for _, memory in inputs],
        out_specs=[pl.BlockSpec(memory_space=pltpu.VMEM)] * len(outputs),
        scratch_shapes=[pltpu.VMEM(*s) if isinstance(s, tuple) else s for s in scratch],
        compiler_params=pltpu.CompilerParams(vmem_limit_bytes=need + extra + 13 * 2**20),
        cost_estimate=pl.CostEstimate(flops=flops, bytes_accessed=touched, transcendentals=0),
        name=name,
    )(*[array for array, _ in inputs])


def layer(place, lengths, tokens, cotangent, chunks):
    length, width = tokens.shape
    inner = 16 * chunks[2][0].shape[2]
    rest = (PASSES - 1) * length
    heads = width // PAIR
    anywhere, local, scalars = pl.ANY, pltpu.VMEM, pltpu.SMEM
    place = (place, scalars)
    L = lambda *arrays: [(a, local) for a in arrays]

    G = lambda n: [(a, anywhere) for a in chunks[n]]
    low = lambda *shape: (shape, BF16)
    full = lambda *shape: (shape, F32)
    kept = lambda *specs: [(*s, True) for s in specs]
    out = lambda *specs: [(*s, False) for s in specs]
    semaphores = lambda n: pltpu.SemaphoreType.DMA((n,))
    row, row32 = low(length, width), full(length, width)
    part = 2 * length * width

    far_pieces(chunks[0])
    mate_pieces(chunks[0])
    far_pieces(chunks[1])
    w_qkv, vec, bias_up, mask, x_norm_0, q_0, k_0, v_0, probs_0, context_0, entry_0 = call(
        start_kernel, "start",
        [place, (lengths, scalars)] + L(tokens) + G(0),
        kept(
            low(width, 3 * width), full(VECTORS, width), full(1, inner), full(length, PASSES * length), row, row, row, row,
            low(heads, 2 * length, length), row, row32,
        ),
        [low(width, SMALL), full(2 * length, length), semaphores(2)],
        20 * 10**9, 70 * 2**20,
    )
    far_pieces(chunks[2])
    mate_pieces(chunks[1])
    w_up, w_out, middle_0, x_mlp_0, active_0, slope_0 = call(
        up_kernel, "up",
        [place] + L(context_0, vec, bias_up, entry_0) + G(1),
        kept(low(width, inner), low(width, width), row32, row, low(length, inner), low(length, inner)),
        [semaphores(2)],
        12 * 10**9, 40 * 2**20,
    )
    mate_pieces(chunks[2], context_0)
    (
        output, state, g_vec, x_norm, context, x_mlp, active, d_hidden_0, d_hidden, d_z, d_y, d_mixed, k_grad, v_grad,
    ) = call(
        main_kernel, "main",
        [place] + L(cotangent, vec, bias_up, mask, w_qkv, w_out, w_up, k_0, v_0, middle_0, active_0, slope_0) + G(2),
        out(row) + kept(
            row32, full(VECTORS, width), low(rest, width), low(rest, width), low(rest, width), low(rest, inner),
            low(length, inner), low(rest, inner), low(rest + length, width), low(rest, width), low(rest, 3 * width),
            row32, row32,
        ),
        [
            low(inner, width), low(rest, width), low(rest + length, width), low(rest + length, width),
            low(heads, 2 * length, 2 * length), low(heads, 2 * length, 3 * length), full(rest, width), full(rest, width),
            full(rest + length, width), full(rest + length, width), row32, row, full(2 * length, PASSES * length),
            low(2 * length, PASSES * length), semaphores(1),
        ],
        40 * part * inner, 60 * 2**20,
    )
    halves_ = []
    for kernel, name in ((give_down_kernel, "give_down"), (keep_down_kernel, "keep_down")):
        halves_ += call(
            kernel, name, [place] + L(active_0, active, after(d_z, *halves_)), kept(low(16, inner // 16, width // 2)), [],
            *COST,
        )
    begun = [begin_scatter(*halves_, MATE_WEIGHTS[0])]
    state = after(state, begun[0][0])
    begun[0] = far_step(begun[0])
    up_shape = low(16, width // 16, inner // 2 + width // 2)
    give_up, state, g_vec, d_y_0, d_context = call(
        give_up_kernel, "give_up",
        [place]
        + L(vec, w_up, w_out, x_mlp_0, x_mlp, d_hidden_0, d_hidden, middle_0, state, g_vec, context_0, context, d_y),
        kept(up_shape, row32, full(VECTORS, width), row, row), [row32],
        *COST,
    )
    keep_up, g_bias_up = call(
        keep_up_kernel, "keep_up",
        [place] + L(x_mlp_0, x_mlp, d_hidden_0, d_hidden, context_0, context, d_y_0, d_y),
        kept(up_shape, full(1, inner)), [],
        *COST,
    )
    begun.append(begin_scatter(give_up, keep_up, MATE_WEIGHTS[1]))
    state = after(state, begun[0][0])
    token_grad, d_mixed_0, g_small = call(
        last_kernel, "last",
        [place]
        + L(
            vec, w_qkv, q_0, k_0, v_0, probs_0, context_0, d_context, d_y_0, d_y, d_mixed, entry_0, k_grad, v_grad, state,
            g_vec, g_bias_up,
        ),
        out(row) + kept(low(length, 3 * width), low(width, SMALL)),
        [
            row32, row32, row32, full(VECTORS, width), row32, full(2 * length, length), low(2 * length, length),
        ],
        *COST,
    )
    begun[1] = far_step((after(begun[1][0], g_small), begun[1][1]))
    near_0 = near_step(begun[0], FAR_WEIGHTS[0])
    last_shape = low(16, width // 16, 3 * width // 2 + SMALL // 2)
    ends = []
    for name, swapped in (("give_qkv", 1), ("keep_qkv", 0)):
        earlier = ends if ends else near_0[:1]
        ends += call(
            functools.partial(qkv_kernel, swapped), name,
            [place] + L(x_norm_0, x_norm, d_mixed_0, d_mixed, after(g_small, *earlier)), kept(last_shape), [], *COST,
        )
    return output, token_grad, (near_0, begun[1], far_step(begin_scatter(*ends, MATE_WEIGHTS[2])))


def per_device(
    tokens,
    lengths,
    cotangent,
    w_qkv,
    bias_q,
    bias_v,
    w_out,
    bias_out,
    gain_attn,
    shift_attn,
    gain_mlp,
    shift_mlp,
    w_up,
    bias_up,
    w_down,
    bias_down,
    pass_embed,
):
    small = pack_small(
        [bias_q, bias_v, bias_out, gain_attn, shift_attn, gain_mlp, shift_mlp, bias_down], bias_up, pass_embed
    )
    place, chunks, last_z = gather_all(w_qkv, w_out, small, w_up, w_down)
    output, token_grad, parts = layer(place, lengths[0], tokens, cotangent, chunks)
    g_qkv, g_out, g_up, g_down, g_small = scatter_all(parts)
    (g_bq, g_bv, g_bo, g_ga, g_sa, g_gm, g_sm, g_bd), g_bu, g_pe = unpack_small(g_small)
    return (
        output,
        token_grad,
        g_qkv,
        g_bq,
        g_bv,
        g_out,
        g_bo,
        g_ga,
        g_sa,
        g_gm,
        g_sm,
        g_up,
        g_bu,
        g_down,
        g_bd,
        g_pe,
    )


def solution(mesh):
    placed = (
        P(("dp", "fsdp"), None),
        P(("dp", "fsdp"), None),
        P(("dp", "fsdp"), None),
        P(("dp", "fsdp"), None),
        P(("dp", "fsdp")),
        P(("dp", "fsdp")),
        P(("dp", "fsdp"), None),
        P(("dp", "fsdp")),
        P(("dp", "fsdp")),
        P(("dp", "fsdp")),
        P(("dp", "fsdp")),
        P(("dp", "fsdp")),
        P(("dp", "fsdp"), None),
        P(("dp", "fsdp")),
        P(("dp", "fsdp"), None),
        P(("dp", "fsdp")),
        P(None, ("dp", "fsdp")),
    )
    return jax.shard_map(
        per_device,
        mesh=mesh,
        in_specs=placed,
        out_specs=(
            P(("dp", "fsdp"), None),
            P(("dp", "fsdp"), None),
            P(("dp", "fsdp"), None),
            P(("dp", "fsdp")),
            P(("dp", "fsdp")),
            P(("dp", "fsdp"), None),
            P(("dp", "fsdp")),
            P(("dp", "fsdp")),
            P(("dp", "fsdp")),
            P(("dp", "fsdp")),
            P(("dp", "fsdp")),
            P(("dp", "fsdp"), None),
            P(("dp", "fsdp")),
            P(("dp", "fsdp"), None),
            P(("dp", "fsdp")),
            P(None, ("dp", "fsdp")),
        ),
        check_vma=False,
    )
```

time: 311 us -> 274 us (0.88)
  waiting for transfers between devices: 135 us -> 108 us
  Pallas kernels: 85.1 us -> 95.3 us
  other arithmetic: 17.3 us -> 7.62 us
  local copies, waits for them, and re-layouts: 17.1 us -> 10.9 us
  starting transfers between devices: 48.5 us -> 45.3 us
    ppermute x46 -> x45, waiting for transfers between devices: 135 us -> 108 us  [send(): return lax.ppermute(x, AXES, route)]
    pallas_call x3 -> x13, Pallas kernels: 85.1 us -> 95.3 us  [the longest x10 93.5 us: call(): pl.pallas_call(kernel, out_shape=results, in_specs=[pl.BlockSpec(memory_s...]
    slice x5 -> x0, local copies, waits for them, and re-layouts: 6.69 us -> none  [the longest x3 4.62 us: gather_all(): p[..., first:]]
    convert_element_type x10 -> x8, other arithmetic: 9.05 us -> 2.47 us  [add_low(): return (a.astype(F32) + b.astype(F32)).astype(BF16)]
    ppermute x46 -> x45, starting transfers between devices: 48.5 us -> 45.3 us  [send(): return lax.ppermute(x, AXES, route)]
  transfers between devices with their start and end apart: 46 -> 45, of which waited for: 27 -> 19; matrix products, arithmetic and copies ran while one was open for 8% -> 3% of each run, Pallas kernels for 1% -> 15%
where the time goes in v1:
time: 274 us; the launch traced here: 269 us
  waiting for transfers between devices  108 us (39%)
  Pallas kernels  95.3 us (35%)
  starting transfers between devices  45.3 us (17%)
  local copies, waits for them, and re-layouts  10.9 us (4%)
  other arithmetic  7.62 us (3%)
    ppermute x45, waiting for transfers between devices, send(): return lax.ppermute(x, AXES, route)  108 us
    pallas_call x10, Pallas kernels, call(): pl.pallas_call(kernel, out_shape=results, in_specs=[pl.BlockSpec(memory_s...  93.5 us
    ppermute x45, starting transfers between devices, send(): return lax.ppermute(x, AXES, route)  45.3 us
  transfers between devices with their start and end apart: 45, of which 19 were waited for; matrix products, arithmetic and copies ran while one was open for 3% of the time, Pallas kernels for 15%

profile of v1, /device:TPU:0, one launch (start us, length us, event | category | flops | bytes accessed | tf_op | source)
XLA Modules:
  0.0 269.0 jit_solution(17712145982930149730)
XLA Ops:
  6.4 5.1 %collective-permute-start.3 = (bf16[48,1280]{1,0:T(8,128)(2,1)S(1)}, bf16[48,1280]{1,0:T(8,128)(2,1)S(1)}, u32[]{:S(2)}, u32[]{:S(2)}) collective-permute-start(bf16[48,1280]{1,0:T(8,128)(2,1)S(1)} %maximum_select_fusion.3), channel_id=1, source_target_pairs={{0,24},{1,25},{2,26},{3,27},{4,28},{5,29},{6,30},{7,31},{8,16},{9,... | collective-permute-start | bytes 368648 | tf_op jit(solution)/shard_map/ppermute | solution.py:30
  12.2 3.6 %collective-permute-done.3 = bf16[48,1280]{1,0:T(8,128)(2,1)S(1)} collective-permute-done((bf16[48,1280]{1,0:T(8,128)(2,1)S(1)}, bf16[48,1280]{1,0:T(8,128)(2,1)S(1)}, u32[]{:S(2)}, u32[]{:S(2)}) %collective-permute-start.3) | collective-permute-done | bytes 122912 | tf_op jit(solution)/shard_map/ppermute | solution.py:30
  15.8 6.3 %collective-permute-done.2 = bf16[48,1280]{1,0:T(8,128)(2,1)S(1)} collective-permute-done((bf16[48,1280]{1,0:T(8,128)(2,1)S(1)}, bf16[48,1280]{1,0:T(8,128)(2,1)S(1)}, u32[]{:S(2)}, u32[]{:S(2)}) %collective-permute-start.2) | collective-permute-done | bytes 122912 | tf_op jit(solution)/shard_map/ppermute | solution.py:30
  23.8 2.5 collective-permute-start.11
  28.3 5.0 %collective-permute-done.11 = bf16[48,1920]{1,0:T(8,128)(2,1)S(1)} collective-permute-done((bf16[48,1920]{1,0:T(8,128)(2,1)S(1)}, bf16[48,1920]{1,0:T(8,128)(2,1)S(1)}, u32[]{:S(2)}, u32[]{:S(2)}) %collective-permute-start.11) | collective-permute-done | bytes 184352 | tf_op jit(solution)/shard_map/ppermute | solution.py:30
  33.3 7.4 %collective-permute-done.10 = bf16[48,1920]{1,0:T(8,128)(2,1)S(1)} collective-permute-done((bf16[48,1920]{1,0:T(8,128)(2,1)S(1)}, bf16[48,1920]{1,0:T(8,128)(2,1)S(1)}, u32[]{:S(2)}, u32[]{:S(2)}) %collective-permute-start.10) | collective-permute-done | bytes 184352 | tf_op jit(solution)/shard_map/ppermute | solution.py:30
  46.8 3.0 %collective-permute-start.17 = (bf16[192,384]{1,0:T(8,128)(2,1)S(1)}, bf16[192,384]{1,0:T(8,128)(2,1)S(1)}, u32[]{:S(2)}, u32[]{:S(2)}) collective-permute-start(bf16[192,384]{1,0:T(8,128)(2,1)S(1)} %maximum_select_fusion.1.refs_0_), channel_id=1, source_target_pairs={{0,8},{1,9},{2,10},{3,11},{4,12},{5,13},{6,14},{7,15},{8,0},{9,1},... | collective-permute-start | bytes 442376 | tf_op jit(solution)/shard_map/ppermute | solution.py:30
  49.8 10.5 %collective-permute-done.12 = bf16[4,48,1920]{2,1,0:T(8,128)(2,1)S(1)} collective-permute-done((bf16[4,48,1920]{2,1,0:T(8,128)(2,1)S(1)}, bf16[4,48,1920]{2,1,0:T(8,128)(2,1)S(1)}, u32[]{:S(2)}, u32[]{:S(2)}) %collective-permute-start.12) | collective-permute-done | bytes 737312 | tf_op jit(solution)/shard_map/ppermute | solution.py:30
  63.8 14.8 %collective-permute-done.20 = bf16[4,192,384]{2,1,0:T(8,128)(2,1)} collective-permute-done((bf16[4,192,384]{2,1,0:T(8,128)(2,1)S(1)}, bf16[4,192,384]{2,1,0:T(8,128)(2,1)}, u32[]{:S(2)}, u32[]{:S(2)}) %collective-permute-start.20) | collective-permute-done | bytes 589856 | tf_op jit(solution)/shard_map/ppermute | solution.py:30
  81.6 4.6 %collective-permute-done.13.p1 = bf16[2,4,48,1920]{3,2,1,0:T(8,128)(2,1)S(1)} collective-permute-done((bf16[2,4,48,1920]{3,2,1,0:T(8,128)(2,1)S(1)}, bf16[2,4,48,1920]{3,2,1,0:T(8,128)(2,1)S(1)}, u32[]{:S(2)}, u32[]{:S(2)}) %collective-permute-start.13) | collective-permute-done | bytes 1474592 | tf_op jit(solution)/shard_map/ppermute | solution.py:30
  86.2 8.1 %start.1 = (bf16[768,2304]{1,0:T(8,128)(2,1)S(1)}, f32[16,768]{1,0:T(8,128)S(1)}, f32[1,3072]{1,0:T(1,128)S(1)}, f32[192,576]{1,0:T(8,128)S(1)}, bf16[192,768]{1...) custom-call(s32[2]{0:T(128)S(1)} %pad_add_fusion.place_ref, ...), custom_call_target="tpu_custom_call" | custom-call | flops 20000000000 | bytes 73400320 | tf_op jit(solution)/shard_map/start/pallas_call | solution.py:744
  94.4 4.4 %collective-permute-done.21.p1 = bf16[2,4,192,384]{3,2,1,0:T(8,128)(2,1)S(1)} collective-permute-done((bf16[2,4,192,384]{3,2,1,0:T(8,128)(2,1)S(1)}, bf16[2,4,192,384]{3,2,1,0:T(8,128)(2,1)S(1)}, u32[]{:S(2)}, u32[]{:S(2)}) %collective-permute-start.21) | collective-permute-done | bytes 1179680 | tf_op jit(solution)/shard_map/ppermute | solution.py:30
  98.9 5.1 %up.1 = (bf16[768,3072]{1,0:T(8,128)(2,1)S(1)}, bf16[768,768]{1,0:T(8,128)(2,1)S(1)}, f32[192,768]{1,0:T(8,128)S(1)}, bf16[192,768]{1,0:T(8,128)(2,1)S(1)}, bf16...) custom-call(s32[2]{0:T(128)S(1)} %pad_add_fusion.place_ref, ...), custom_call_target="tpu_custom_call" | custom-call | flops 12000000000 | bytes 41943040 | tf_op jit(solution)/shard_map/up/pallas_call | solution.py:744
  104.0 2.1 copy-done.3
  106.2 50.1 %main.1 = (bf16[192,768]{1,0:T(8,128)(2,1)}, f32[192,768]{1,0:T(8,128)S(1)}, f32[16,768]{1,0:T(8,128)S(1)}, bf16[384,768]{1,0:T(8,128)(2,1)S(1)}, bf16[384,768]{...) custom-call(s32[2]{0:T(128)S(1)} %pad_add_fusion.place_ref, ...), custom_call_target="tpu_custom_call" | custom-call | flops 36238786560 | bytes 62914560 | tf_op jit(solution)/shard_map/main/pallas_call | solution.py:744
  157.6 3.7 %give_down.1 = bf16[16,192,384]{2,1,0:T(8,128)(2,1)S(1)} custom-call(s32[2]{0:T(128)S(1)} %pad_add_fusion.place_ref, bf16[192,3072]{1,0:T(8,128)(2,1)S(1)} %copy-done.7, bf16[384,3072]{1,0:T(8,128)(2,1)S(1)} %get-tuple-element.95.active, bf16[576,768]{1,0:T(8,128)(2,1)S(1)} %get-tuple-element.97.d_z), custom_call_target="tpu_custom_call" | custom-call | flops 10000000000 | bytes 36700160 | tf_op jit(solution)/shard_map/give_down/pallas_call | solution.py:744
  161.8 4.1 %keep_down.1 = bf16[16,192,384]{2,1,0:T(8,128)(2,1)S(1)} custom-call(s32[2]{0:T(128)S(1)} %pad_add_fusion.place_ref, bf16[192,3072]{1,0:T(8,128)(2,1)S(1)} %copy-done.7, bf16[384,3072]{1,0:T(8,128)(2,1)S(1)} %get-tuple-element.95.active, bf16[576,768]{1,0:T(8,128)(2,1)S(1)} %get-tuple-element.97.d_z), custom_call_target="tpu_custom_call" | custom-call | flops 10000000000 | bytes 36700160 | tf_op jit(solution)/shard_map/keep_down/pallas_call | solution.py:744
  167.5 6.4 %give_up.1 = (bf16[16,48,1920]{2,1,0:T(8,128)(2,1)S(1)}, f32[192,768]{1,0:T(8,128)S(1)}, f32[16,768]{1,0:T(8,128)S(1)}, bf16[192,768]{1,0:T(8,128)(2,1)S(1)}, bf16[192,768]{1,0:T(8,128)(2,1)S(1)}) custom-call(s32[2]{0:T(128)S(1)} %pad_add_fusion.place_ref, f32[16,768]{1,0:T(8,128)S(1)} %get-tuple-element.71.vec, bf16[768,3072]{1,0:T(8,128)(2,1)S(1)} %bitcast.153, ...), custom_call_target="tpu_custom_call" | custom-call | flops 10000000000 | bytes 36700160 | tf_op jit(solution)/shard_map/give_up/pallas_call | solution.py:744
  174.6 4.5 %keep_up.1 = (bf16[16,48,1920]{2,1,0:T(8,128)(2,1)S(1)}, f32[1,3072]{1,0:T(1,128)S(1)}) custom-call(s32[2]{0:T(128)S(1)} %pad_add_fusion.place_ref, bf16[192,768]{1,0:T(8,128)(2,1)S(1)} %get-tuple-element.90.x_mlp_0, bf16[384,768]{1,0:T(8,128)(2,1)S(1)} %get-tuple-element.91.x_mlp, bf16[192,3072]{1,0:T(8,128)(2,1)S(1)} %get-tuple-element.92.d_hidden_0, ...), custom_call_target="tpu_custom_call" | custom-call | flops 10000000000 | bytes 36700160 | tf_op jit(solution)/shard_map/keep_up/pallas_call | solution.py:744
  179.2 3.7 %collective-permute-done.25 = bf16[2,4,192,384]{3,2,1,0:T(8,128)(2,1)S(1)} collective-permute-done((bf16[2,4,192,384]{3,2,1,0:T(8,128)(2,1)S(1)}, bf16[2,4,192,384]{3,2,1,0:T(8,128)(2,1)S(1)}, u32[]{:S(2)}, u32[]{:S(2)}) %collective-permute-start.25) | collective-permute-done | bytes 1179680 | tf_op jit(solution)/shard_map/ppermute | solution.py:30
  184.9 6.7 %last.1 = (bf16[192,768]{1,0:T(8,128)(2,1)}, bf16[192,2304]{1,0:T(8,128)(2,1)S(1)}, bf16[768,256]{1,0:T(8,128)(2,1)S(1)}) custom-call(s32[2]{0:T(128)S(1)} %pad_add_fusion.place_ref, f32[16,768]{1,0:T(8,128)S(1)} %copy-done.19, bf16[768,2304]{1,0:T(8,128)(2,1)S(1)} %copy-done.5, bf16[192,768]{1,0:T(8,128)(2,1)S(1)} %copy-done.11, ...), custom_call_target="tpu_custom_call" | custom-call | flops 10000000000 | bytes 36700160 | tf_op jit(solution)/shard_map/last/pallas_call | solution.py:744
  193.2 2.5 give_qkv.1
  195.7 2.5 keep_qkv.1
  204.4 3.2 %collective-permute-start.37 = (bf16[192,384]{1,0:T(8,128)(2,1)S(1)}, bf16[192,384]{1,0:T(8,128)(2,1)S(1)}, u32[]{:S(2)}, u32[]{:S(2)}) collective-permute-start(bf16[192,384]{1,0:T(8,128)(2,1)S(1)} %get-tuple-element.213), channel_id=1, source_target_pairs={{0,8},{1,9},{2,10},{3,11},{4,12},{5,13},{6,14},{7,15},{8,0},{9,1},... | collective-permute-start | bytes 442376 | tf_op jit(solution)/shard_map/ppermute | solution.py:30
  207.6 4.3 %collective-permute-done.39 = bf16[192,384]{1,0:T(8,128)(2,1)S(1)} collective-permute-done((bf16[192,384]{1,0:T(8,128)(2,1)S(1)}, bf16[192,384]{1,0:T(8,128)(2,1)S(1)}, u32[]{:S(2)}, u32[]{:S(2)}) %collective-permute-start.39) | collective-permute-done | bytes 147488 | tf_op jit(solution)/shard_map/ppermute | solution.py:30
  211.9 4.8 %collective-permute-done.38 = bf16[192,384]{1,0:T(8,128)(2,1)S(1)} collective-permute-done((bf16[192,384]{1,0:T(8,128)(2,1)S(1)}, bf16[192,384]{1,0:T(8,128)(2,1)S(1)}, u32[]{:S(2)}, u32[]{:S(2)}) %collective-permute-start.38) | collective-permute-done | bytes 147488 | tf_op jit(solution)/shard_map/ppermute | solution.py:30
  218.6 16.8 %collective-permute-done.35 = bf16[2,4,48,1920]{3,2,1,0:T(8,128)(2,1)S(1)} collective-permute-done((bf16[2,4,48,1920]{3,2,1,0:T(8,128)(2,1)S(1)}, bf16[2,4,48,1920]{3,2,1,0:T(8,128)(2,1)S(1)}, u32[]{:S(2)}, u32[]{:S(2)}) %collective-permute-start.35) | collective-permute-done | bytes 1474592 | tf_op jit(solution)/shard_map/ppermute | solution.py:30
  239.1 2.5 collective-permute-start.31
  241.6 5.7 %collective-permute-done.36 = bf16[4,48,1920]{2,1,0:T(8,128)(2,1)S(1)} collective-permute-done((bf16[4,48,1920]{2,1,0:T(8,128)(2,1)S(1)}, bf16[4,48,1920]{2,1,0:T(8,128)(2,1)S(1)}, u32[]{:S(2)}, u32[]{:S(2)}) %collective-permute-start.36) | collective-permute-done | bytes 737312 | tf_op jit(solution)/shard_map/ppermute | solution.py:30
  249.3 2.6 collective-permute-start.42
  251.9 8.2 %collective-permute-done.31 = bf16[48,1280]{1,0:T(8,128)(2,1)S(1)} collective-permute-done((bf16[48,1280]{1,0:T(8,128)(2,1)S(1)}, bf16[48,1280]{1,0:T(8,128)(2,1)S(1)}, u32[]{:S(2)}, u32[]{:S(2)}) %collective-permute-start.31) | collective-permute-done | bytes 122912 | tf_op jit(solution)/shard_map/ppermute | solution.py:30
  260.4 3.8 %collective-permute-done.41 = bf16[48,1920]{1,0:T(8,128)(2,1)S(1)} collective-permute-done((bf16[48,1920]{1,0:T(8,128)(2,1)S(1)}, bf16[48,1920]{1,0:T(8,128)(2,1)S(1)}, u32[]{:S(2)}, u32[]{:S(2)}) %collective-permute-start.41) | collective-permute-done | bytes 184352 | tf_op jit(solution)/shard_map/ppermute | solution.py:30
  (170 shorter events, 48.8 us)
Async XLA Ops:
  6.3 17.5 %collective-permute-start.8 = (bf16[24,1920]{1,0:T(8,128)(2,1)S(1)}, bf16[24,1920]{1,0:T(8,128)(2,1)S(1)}, u32[]{:S(2)}, u32[]{:S(2)}) collective-permute-start(bf16[24,1920]{1,0:T(8,128)(2,1)S(1)} %get-tuple-element.226), channel_id=1, source_target_pairs={{0,1},{1,0},{2,3},{3,2},{4,5},{5,4},{6,7},{7,6},{8,9},{9,8},{10,11... | collective-permute-start | bytes 276488 | tf_op jit(solution)/shard_map/ppermute | solution.py:30
  22.2 20.1 %collective-permute-start.4 = (bf16[4,48,1280]{2,1,0:T(8,128)(2,1)S(1)}, bf16[4,48,1280]{2,1,0:T(8,128)(2,1)S(1)}, u32[]{:S(2)}, u32[]{:S(2)}) collective-permute-start(bf16[4,48,1280]{2,1,0:T(8,128)(2,1)S(1)} %pad_maximum_fusion.3.refs_0_), channel_id=1, source_target_pairs={{0,4},{1,3},{2,6},{3,1},{4,0},{5,7},{6,2},{7,5},{8,12},{9,11},{10,... | collective-permute-start | bytes 1474568 | tf_op jit(solution)/shard_map/ppermute | solution.py:30
  26.4 14.4 %collective-permute-start.10 = (bf16[48,1920]{1,0:T(8,128)(2,1)S(1)}, bf16[48,1920]{1,0:T(8,128)(2,1)S(1)}, u32[]{:S(2)}, u32[]{:S(2)}) collective-permute-start(bf16[48,1920]{1,0:T(8,128)(2,1)S(1)} %maximum_select_fusion), channel_id=1, source_target_pairs={{0,16},{1,17},{2,18},{3,19},{4,20},{5,21},{6,22},{7,23},{8,24},{9,... | collective-permute-start | bytes 552968 | tf_op jit(solution)/shard_map/ppermute | solution.py:30
  26.4 14.4 %collective-permute-start.9 = (bf16[48,1920]{1,0:T(8,128)(2,1)S(1)}, bf16[48,1920]{1,0:T(8,128)(2,1)S(1)}, u32[]{:S(2)}, u32[]{:S(2)}) collective-permute-start(bf16[48,1920]{1,0:T(8,128)(2,1)S(1)} %maximum_select_fusion), channel_id=1, source_target_pairs={{0,8},{1,9},{2,10},{3,11},{4,12},{5,13},{6,14},{7,15},{8,0},{9,1},... | collective-permute-start | bytes 552968 | tf_op jit(solution)/shard_map/ppermute | solution.py:30
  40.9 19.4 %collective-permute-start.12 = (bf16[4,48,1920]{2,1,0:T(8,128)(2,1)S(1)}, bf16[4,48,1920]{2,1,0:T(8,128)(2,1)S(1)}, u32[]{:S(2)}, u32[]{:S(2)}) collective-permute-start(bf16[4,48,1920]{2,1,0:T(8,128)(2,1)S(1)} %get-tuple-element.218), channel_id=1, source_target_pairs={{0,4},{1,3},{2,6},{3,1},{4,0},{5,7},{6,2},{7,5},{8,12},{9,11},{10,... | collective-permute-start | bytes 2211848 | tf_op jit(solution)/shard_map/ppermute | solution.py:30
  43.4 17.9 %collective-permute-start.5 = (bf16[2,4,48,1280]{3,2,1,0:T(8,128)(2,1)}, bf16[2,4,48,1280]{3,2,1,0:T(8,128)(2,1)}, u32[]{:S(2)}, u32[]{:S(2)}) collective-permute-start(bf16[2,4,48,1280]{3,2,1,0:T(8,128)(2,1)} %stack.111.p0), channel_id=1, source_target_pairs={{0,2},{1,5},{2,0},{3,7},{4,6},{5,1},{6,4},{7,3},{8,10},{9,13},{10,... | collective-permute-start | bytes 2949128 | tf_op jit(solution)/shard_map/ppermute | solution.py:30
  45.4 15.1 %collective-permute-start.19 = (bf16[192,384]{1,0:T(8,128)(2,1)S(1)}, bf16[192,384]{1,0:T(8,128)(2,1)S(1)}, u32[]{:S(2)}, u32[]{:S(2)}) collective-permute-start(bf16[192,384]{1,0:T(8,128)(2,1)S(1)} %maximum_select_fusion.1.refs_0_), channel_id=1, source_target_pairs={{0,24},{1,25},{2,26},{3,27},{4,28},{5,29},{6,30},{7,31},{8,16},{9,... | collective-permute-start | bytes 442376 | tf_op jit(solution)/shard_map/ppermute | solution.py:30
  46.8 15.3 %collective-permute-start.18 = (bf16[192,384]{1,0:T(8,128)(2,1)S(1)}, bf16[192,384]{1,0:T(8,128)(2,1)S(1)}, u32[]{:S(2)}, u32[]{:S(2)}) collective-permute-start(bf16[192,384]{1,0:T(8,128)(2,1)S(1)} %maximum_select_fusion.1.refs_0_), channel_id=1, source_target_pairs={{0,16},{1,17},{2,18},{3,19},{4,20},{5,21},{6,22},{7,23},{8,24},{9,... | collective-permute-start | bytes 442376 | tf_op jit(solution)/shard_map/ppermute | solution.py:30
  46.8 15.3 %collective-permute-start.17 = (bf16[192,384]{1,0:T(8,128)(2,1)S(1)}, bf16[192,384]{1,0:T(8,128)(2,1)S(1)}, u32[]{:S(2)}, u32[]{:S(2)}) collective-permute-start(bf16[192,384]{1,0:T(8,128)(2,1)S(1)} %maximum_select_fusion.1.refs_0_), channel_id=1, source_target_pairs={{0,8},{1,9},{2,10},{3,11},{4,12},{5,13},{6,14},{7,15},{8,0},{9,1},... | collective-permute-start | bytes 442376 | tf_op jit(solution)/shard_map/ppermute | solution.py:30
  60.3 21.1 %collective-permute-start.6 = (bf16[2,4,48,1280]{3,2,1,0:T(8,128)(2,1)}, bf16[2,4,48,1280]{3,2,1,0:T(8,128)(2,1)}, u32[]{:S(2)}, u32[]{:S(2)}) collective-permute-start(bf16[2,4,48,1280]{3,2,1,0:T(8,128)(2,1)} %stack.111.p0), channel_id=1, source_target_pairs={{0,1},{1,0},{2,3},{3,2},{4,5},{5,4},{6,7},{7,6},{8,9},{9,8},{10,11... | collective-permute-start | bytes 2949128 | tf_op jit(solution)/shard_map/ppermute | solution.py:30
  60.5 25.7 %collective-permute-start.13 = (bf16[2,4,48,1920]{3,2,1,0:T(8,128)(2,1)S(1)}, bf16[2,4,48,1920]{3,2,1,0:T(8,128)(2,1)S(1)}, u32[]{:S(2)}, u32[]{:S(2)}) collective-permute-start(bf16[2,4,48,1920]{3,2,1,0:T(8,128)(2,1)S(1)} %pad_maximum_fusion.p0), channel_id=1, source_target_pairs={{0,2},{1,5},{2,0},{3,7},{4,6},{5,1},{6,4},{7,3},{8,10},{9,13},{10,... | collective-permute-start | bytes 4423688 | tf_op jit(solution)/shard_map/ppermute | solution.py:30
  61.3 24.9 %collective-permute-start.7 = (bf16[2,4,48,1280]{3,2,1,0:T(8,128)(2,1)}, bf16[2,4,48,1280]{3,2,1,0:T(8,128)(2,1)}, u32[]{:S(2)}, u32[]{:S(2)}) collective-permute-start(bf16[2,4,48,1280]{3,2,1,0:T(8,128)(2,1)} %collective-permute-done.5.p1), channel_id=1, source_target_pairs={{0,1},{1,0},{2,3},{3,2},{4,5},{5,4},{6,7},{7,6},{8,9},{9,8},{10,11... | collective-permute-start | bytes 2949128 | tf_op jit(solution)/shard_map/ppermute | solution.py:30
  62.2 16.4 %collective-permute-start.20 = (bf16[4,192,384]{2,1,0:T(8,128)(2,1)S(1)}, bf16[4,192,384]{2,1,0:T(8,128)(2,1)}, u32[]{:S(2)}, u32[]{:S(2)}) collective-permute-start(bf16[4,192,384]{2,1,0:T(8,128)(2,1)S(1)} %stack.112), channel_id=1, source_target_pairs={{0,4},{1,3},{2,6},{3,1},{4,0},{5,7},{6,2},{7,5},{8,12},{9,11},{10,... | collective-permute-start | bytes 1769480 | tf_op jit(solution)/shard_map/ppermute | solution.py:30
  79.8 26.3 %collective-permute-start.22 = (bf16[2,4,192,384]{3,2,1,0:T(8,128)(2,1)S(1)}, bf16[2,4,192,384]{3,2,1,0:T(8,128)(2,1)S(1)}, u32[]{:S(2)}, u32[]{:S(2)}) collective-permute-start(bf16[2,4,192,384]{3,2,1,0:T(8,128)(2,1)S(1)} %pad_maximum_fusion.1.p0), channel_id=1, source_target_pairs={{0,1},{1,0},{2,3},{3,2},{4,5},{5,4},{6,7},{7,6},{8,9},{9,8},{10,11... | collective-permute-start | bytes 3538952 | tf_op jit(solution)/shard_map/ppermute | solution.py:30
  79.9 19.0 %collective-permute-start.21 = (bf16[2,4,192,384]{3,2,1,0:T(8,128)(2,1)S(1)}, bf16[2,4,192,384]{3,2,1,0:T(8,128)(2,1)S(1)}, u32[]{:S(2)}, u32[]{:S(2)}) collective-permute-start(bf16[2,4,192,384]{3,2,1,0:T(8,128)(2,1)S(1)} %pad_maximum_fusion.1.p0), channel_id=1, source_target_pairs={{0,2},{1,5},{2,0},{3,7},{4,6},{5,1},{6,4},{7,3},{8,10},{9,13},{10,... | collective-permute-start | bytes 3538952 | tf_op jit(solution)/shard_map/ppermute | solution.py:30
  81.4 17.4 %collective-permute-start.14 = (bf16[2,4,48,1920]{3,2,1,0:T(8,128)(2,1)S(1)}, bf16[2,4,48,1920]{3,2,1,0:T(8,128)(2,1)S(1)}, u32[]{:S(2)}, u32[]{:S(2)}) collective-permute-start(bf16[2,4,48,1920]{3,2,1,0:T(8,128)(2,1)S(1)} %pad_maximum_fusion.p0), channel_id=1, source_target_pairs={{0,1},{1,0},{2,3},{3,2},{4,5},{5,4},{6,7},{7,6},{8,9},{9,8},{10,11... | collective-permute-start | bytes 4423688 | tf_op jit(solution)/shard_map/ppermute | solution.py:30
  86.2 12.6 %collective-permute-start.15 = (bf16[2,4,48,1920]{3,2,1,0:T(8,128)(2,1)S(1)}, bf16[2,4,48,1920]{3,2,1,0:T(8,128)(2,1)S(1)}, u32[]{:S(2)}, u32[]{:S(2)}) collective-permute-start(bf16[2,4,48,1920]{3,2,1,0:T(8,128)(2,1)S(1)} %collective-permute-done.13.p1), channel_id=1, source_target_pairs={{0,1},{1,0},{2,3},{3,2},{4,5},{5,4},{6,7},{7,6},{8,9},{9,8},{10,11... | collective-permute-start | bytes 4423688 | tf_op jit(solution)/shard_map/ppermute | solution.py:30
  166.6 16.3 %collective-permute-start.25 = (bf16[2,4,192,384]{3,2,1,0:T(8,128)(2,1)S(1)}, bf16[2,4,192,384]{3,2,1,0:T(8,128)(2,1)S(1)}, u32[]{:S(2)}, u32[]{:S(2)}) collective-permute-start(bf16[2,4,192,384]{3,2,1,0:T(8,128)(2,1)S(1)} %bitcast.154), channel_id=1, source_target_pairs={{0,2},{1,5},{2,0},{3,7},{4,6},{5,1},{6,4},{7,3},{8,10},{9,13},{10,... | collective-permute-start | bytes 3538952 | tf_op jit(solution)/shard_map/ppermute | solution.py:30
  173.9 27.1 %collective-permute-start.34 = (bf16[16,48,1920]{2,1,0:T(8,128)(2,1)S(1)}, bf16[16,48,1920]{2,1,0:T(8,128)(2,1)S(1)}, u32[]{:S(2)}, u32[]{:S(2)}) collective-permute-start(bf16[16,48,1920]{2,1,0:T(8,128)(2,1)S(1)} %get-tuple-element.118), channel_id=1, source_target_pairs={{0,1},{1,0},{2,3},{3,2},{4,5},{5,4},{6,7},{7,6},{8,9},{9,8},{10,11... | collective-permute-start | bytes 8847368 | tf_op jit(solution)/shard_map/ppermute | solution.py:30
  200.2 16.7 %collective-permute-start.28 = (bf16[2,4,48,1280]{3,2,1,0:T(8,128)(2,1)S(1)}, bf16[2,4,48,1280]{3,2,1,0:T(8,128)(2,1)S(1)}, u32[]{:S(2)}, u32[]{:S(2)}) collective-permute-start(bf16[2,4,48,1280]{3,2,1,0:T(8,128)(2,1)S(1)} %bitcast.155), channel_id=1, source_target_pairs={{0,2},{1,5},{2,0},{3,7},{4,6},{5,1},{6,4},{7,3},{8,10},{9,13},{10,... | collective-permute-start | bytes 2949128 | tf_op jit(solution)/shard_map/ppermute | solution.py:30
  201.8 33.7 %collective-permute-start.35 = (bf16[2,4,48,1920]{3,2,1,0:T(8,128)(2,1)S(1)}, bf16[2,4,48,1920]{3,2,1,0:T(8,128)(2,1)S(1)}, u32[]{:S(2)}, u32[]{:S(2)}) collective-permute-start(bf16[2,4,48,1920]{3,2,1,0:T(8,128)(2,1)S(1)} %bitcast.149), channel_id=1, source_target_pairs={{0,2},{1,5},{2,0},{3,7},{4,6},{5,1},{6,4},{7,3},{8,10},{9,13},{10,... | collective-permute-start | bytes 4423688 | tf_op jit(solution)/shard_map/ppermute | solution.py:30
  204.4 12.3 %collective-permute-start.38 = (bf16[192,384]{1,0:T(8,128)(2,1)S(1)}, bf16[192,384]{1,0:T(8,128)(2,1)S(1)}, u32[]{:S(2)}, u32[]{:S(2)}) collective-permute-start(bf16[192,384]{1,0:T(8,128)(2,1)S(1)} %get-tuple-element.212), channel_id=1, source_target_pairs={{0,16},{1,17},{2,18},{3,19},{4,20},{5,21},{6,22},{7,23},{8,24},{9,... | collective-permute-start | bytes 442376 | tf_op jit(solution)/shard_map/ppermute | solution.py:30
  204.4 12.3 %collective-permute-start.37 = (bf16[192,384]{1,0:T(8,128)(2,1)S(1)}, bf16[192,384]{1,0:T(8,128)(2,1)S(1)}, u32[]{:S(2)}, u32[]{:S(2)}) collective-permute-start(bf16[192,384]{1,0:T(8,128)(2,1)S(1)} %get-tuple-element.213), channel_id=1, source_target_pairs={{0,8},{1,9},{2,10},{3,11},{4,12},{5,13},{6,14},{7,15},{8,0},{9,1},... | collective-permute-start | bytes 442376 | tf_op jit(solution)/shard_map/ppermute | solution.py:30
  216.8 20.4 %collective-permute-start.44 = (f32[96,384]{1,0:T(8,128)S(1)}, f32[96,384]{1,0:T(8,128)S(1)}, u32[]{:S(2)}, u32[]{:S(2)}) collective-permute-start(f32[96,384]{1,0:T(8,128)S(1)} %slice_select_fusion.2), channel_id=1, source_target_pairs={{0,1},{1,0},{2,3},{3,2},{4,5},{5,4},{6,7},{7,6},{8,9},{9,8},{10,11... | collective-permute-start | bytes 442376 | tf_op jit(solution)/shard_map/ppermute | solution.py:30
  217.2 20.8 %collective-permute-start.29 = (bf16[4,48,1280]{2,1,0:T(8,128)(2,1)S(1)}, bf16[4,48,1280]{2,1,0:T(8,128)(2,1)S(1)}, u32[]{:S(2)}, u32[]{:S(2)}) collective-permute-start(bf16[4,48,1280]{2,1,0:T(8,128)(2,1)S(1)} %get-tuple-element.207), channel_id=1, source_target_pairs={{0,4},{1,3},{2,6},{3,1},{4,0},{5,7},{6,2},{7,5},{8,12},{9,11},{10,... | collective-permute-start | bytes 1474568 | tf_op jit(solution)/shard_map/ppermute | solution.py:30
  235.8 11.5 %collective-permute-start.36 = (bf16[4,48,1920]{2,1,0:T(8,128)(2,1)S(1)}, bf16[4,48,1920]{2,1,0:T(8,128)(2,1)S(1)}, u32[]{:S(2)}, u32[]{:S(2)}) collective-permute-start(bf16[4,48,1920]{2,1,0:T(8,128)(2,1)S(1)} %get-tuple-element.203), channel_id=1, source_target_pairs={{0,4},{1,3},{2,6},{3,1},{4,0},{5,7},{6,2},{7,5},{8,12},{9,11},{10,... | collective-permute-start | bytes 2211848 | tf_op jit(solution)/shard_map/ppermute | solution.py:30
  238.1 11.2 %collective-permute-start.30 = (bf16[48,1280]{1,0:T(8,128)(2,1)S(1)}, bf16[48,1280]{1,0:T(8,128)(2,1)S(1)}, u32[]{:S(2)}, u32[]{:S(2)}) collective-permute-start(bf16[48,1280]{1,0:T(8,128)(2,1)S(1)} %get-tuple-element.214), channel_id=1, source_target_pairs={{0,8},{1,9},{2,10},{3,11},{4,12},{5,13},{6,14},{7,15},{8,0},{9,1},... | collective-permute-start | bytes 368648 | tf_op jit(solution)/shard_map/ppermute | solution.py:30
  238.2 13.8 %collective-permute-start.32 = (bf16[48,1280]{1,0:T(8,128)(2,1)S(1)}, bf16[48,1280]{1,0:T(8,128)(2,1)S(1)}, u32[]{:S(2)}, u32[]{:S(2)}) collective-permute-start(bf16[48,1280]{1,0:T(8,128)(2,1)S(1)} %get-tuple-element.215), channel_id=1, source_target_pairs={{0,24},{1,25},{2,26},{3,27},{4,28},{5,29},{6,30},{7,31},{8,16},{9,... | collective-permute-start | bytes 368648 | tf_op jit(solution)/shard_map/ppermute | solution.py:30
  239.1 21.0 %collective-permute-start.31 = (bf16[48,1280]{1,0:T(8,128)(2,1)S(1)}, bf16[48,1280]{1,0:T(8,128)(2,1)S(1)}, u32[]{:S(2)}, u32[]{:S(2)}) collective-permute-start(bf16[48,1280]{1,0:T(8,128)(2,1)S(1)} %get-tuple-element.216), channel_id=1, source_target_pairs={{0,16},{1,17},{2,18},{3,19},{4,20},{5,21},{6,22},{7,23},{8,24},{9,... | collective-permute-start | bytes 368648 | tf_op jit(solution)/shard_map/ppermute | solution.py:30
  247.5 12.9 %collective-permute-start.40 = (bf16[48,1920]{1,0:T(8,128)(2,1)S(1)}, bf16[48,1920]{1,0:T(8,128)(2,1)S(1)}, u32[]{:S(2)}, u32[]{:S(2)}) collective-permute-start(bf16[48,1920]{1,0:T(8,128)(2,1)S(1)} %get-tuple-element.123), channel_id=1, source_target_pairs={{0,8},{1,9},{2,10},{3,11},{4,12},{5,13},{6,14},{7,15},{8,0},{9,1},... | collective-permute-start | bytes 552968 | tf_op jit(solution)/shard_map/ppermute | solution.py:30
  247.6 16.6 %collective-permute-start.41 = (bf16[48,1920]{1,0:T(8,128)(2,1)S(1)}, bf16[48,1920]{1,0:T(8,128)(2,1)S(1)}, u32[]{:S(2)}, u32[]{:S(2)}) collective-permute-start(bf16[48,1920]{1,0:T(8,128)(2,1)S(1)} %get-tuple-element.124), channel_id=1, source_target_pairs={{0,16},{1,17},{2,18},{3,19},{4,20},{5,21},{6,22},{7,23},{8,24},{9,... | collective-permute-start | bytes 552968 | tf_op jit(solution)/shard_map/ppermute | solution.py:30
  249.3 14.8 %collective-permute-start.42 = (bf16[48,1920]{1,0:T(8,128)(2,1)S(1)}, bf16[48,1920]{1,0:T(8,128)(2,1)S(1)}, u32[]{:S(2)}, u32[]{:S(2)}) collective-permute-start(bf16[48,1920]{1,0:T(8,128)(2,1)S(1)} %get-tuple-element.125), channel_id=1, source_target_pairs={{0,24},{1,25},{2,26},{3,27},{4,28},{5,29},{6,30},{7,31},{8,16},{9,... | collective-permute-start | bytes 552968 | tf_op jit(solution)/shard_map/ppermute | solution.py:30
  (36 other events, 408.0 us)

commit v2 on v1

--- a/solution.py
+++ b/solution.py
@@ -122,11 +122,15 @@
     return give.reshape(shape), keep.reshape(shape)
 
 
-def begin_scatter(give, keep, weight):
+def mate_step(give):
+    return send(give, TO_MATE) if is_known_slice() else give
+
+
+def begin_scatter(got, give, keep, weight):
     if not is_known_slice():
         return give, keep
     split = lambda a: a.reshape(2, 2, 4, *a.shape[1:])
-    return add_halves(split(send(give, TO_MATE)), split(keep), weight)
+    return add_halves(split(got), split(keep), weight)
 
 
 def far_step(part):
@@ -263,6 +267,7 @@
 GELU_B = 0.044715
 LN_ROWS = 32
 COST = (10 * 10**9, 35 * 2**20)
+TINY = 1000
 SOFT_ROWS = 64
 WIDE = 256
 
@@ -524,7 +529,7 @@
     def pair(j, _):
         attend(j, q, k, v, probs, scores, mask, context, 0, length)
 
-    lax.fori_loop(0, width // PAIR, pair, None)
+    lax.fori_loop(0, width // PAIR, pair, None, unroll=2)
 
 
 def up_kernel(
@@ -578,7 +583,7 @@
         def pair(j, _):
             attend(j, q, k_all, v_all, probs[r], scores, mask, context, at, seen)
 
-        lax.fori_loop(0, pair_count, pair, None)
+        lax.fori_loop(0, pair_count, pair, None, unroll=2)
         project_out(context, at, length, w_out, vec, entry, middle)
         norm_forward(middle, at, length, vec, GAIN_MLP, SHIFT_MLP, x_mlp, at)
         feed_up(x_mlp, at, length, w_up, bias_up, active, d_hidden, at)
@@ -616,7 +621,7 @@
                 r == PASSES - 1,
             )
 
-        lax.fori_loop(0, pair_count, pair_back, None)
+        lax.fori_loop(0, pair_count, pair_back, None, unroll=2)
         for b in range(0, length, 64):
             part = slice(at + b, at + b + 64)
             made = slice(r * length + b, r * length + b + 64)
@@ -699,7 +704,7 @@
             j, q, k, v, probs, scores, d_scores, d_context, context_0, 0, length, d_mixed_0, k_grad, v_grad, False
         )
 
-    lax.fori_loop(0, width // PAIR, pair_back, None)
+    lax.fori_loop(0, width // PAIR, pair_back, None, unroll=2)
     for b in range(0, length, 64):
         part = slice(b, b + 64)
         d_mixed_0[part, width : 2 * width] = (k_grad[part, :] * SCALE).astype(BF16)
@@ -747,7 +752,7 @@
         in_specs=[pl.BlockSpec(memory_space=memory) for _, memory in inputs],
         out_specs=[pl.BlockSpec(memory_space=pltpu.VMEM)] * len(outputs),
         scratch_shapes=[pltpu.VMEM(*s) if isinstance(s, tuple) else s for s in scratch],
-        compiler_params=pltpu.CompilerParams(vmem_limit_bytes=need + extra + 13 * 2**20),
+        compiler_params=pltpu.CompilerParams(vmem_limit_bytes=need + extra + 4 * 2**20),
         cost_estimate=pl.CostEstimate(flops=flops, bytes_accessed=touched, transcendentals=0),
         name=name,
     )(*[array for array, _ in inputs])
@@ -818,7 +823,7 @@
             kernel, name, [place] + L(active_0, active, after(d_z, *halves_)), kept(low(16, inner // 16, width // 2)), [],
             *COST,
         )
-    begun = [begin_scatter(*halves_, MATE_WEIGHTS[0])]
+    begun = [begin_scatter(mate_step(halves_[0]), *halves_, MATE_WEIGHTS[0])]
     state = after(state, begun[0][0])
     begun[0] = far_step(begun[0])
     up_shape = low(16, width // 16, inner // 2 + width // 2)
@@ -835,7 +840,7 @@
         kept(up_shape, full(1, inner)), [],
         *COST,
     )
-    begun.append(begin_scatter(give_up, keep_up, MATE_WEIGHTS[1]))
+    up_got = mate_step(give_up)
     state = after(state, begun[0][0])
     token_grad, d_mixed_0, g_small = call(
         last_kernel, "last",
@@ -848,9 +853,11 @@
         [
             row32, row32, row32, full(VECTORS, width), row32, full(2 * length, length), low(2 * length, length),
         ],
-        *COST,
-    )
-    begun[1] = far_step((after(begun[1][0], g_small), begun[1][1]))
+        40 * 10**9, 140 * 2**20,
+    )
+    begun.append(begin_scatter(after(up_got, g_small), give_up, keep_up, MATE_WEIGHTS[1]))
+    g_small = after(g_small, begun[1][0])
+    begun[1] = far_step(begun[1])
     near_0 = near_step(begun[0], FAR_WEIGHTS[0])
     last_shape = low(16, width // 16, 3 * width // 2 + SMALL // 2)
     ends = []
@@ -858,9 +865,10 @@
         earlier = ends if ends else near_0[:1]
         ends += call(
             functools.partial(qkv_kernel, swapped), name,
-            [place] + L(x_norm_0, x_norm, d_mixed_0, d_mixed, after(g_small, *earlier)), kept(last_shape), [], *COST,
+            [place] + L(x_norm_0, x_norm, d_mixed_0, d_mixed, after(g_small, *earlier)), kept(last_shape), [], TINY, TINY,
         )
-    return output, token_grad, (near_0, begun[1], far_step(begin_scatter(*ends, MATE_WEIGHTS[2])))
+    near_0 = (near_0[0], after(near_0[1], ends[1]))
+    return output, token_grad, (near_0, begun[1], far_step(begin_scatter(mate_step(ends[0]), *ends, MATE_WEIGHTS[2])))
 
 
 def per_device(

time: 274 us -> 264 us (0.964)
  Pallas kernels: 95.3 us -> 88.3 us
  local copies, waits for them, and re-layouts: 10.9 us -> 7.46 us
    pallas_call x10, Pallas kernels: 93.5 us -> 86.5 us  [call(): pl.pallas_call(kernel, out_shape=results, in_specs=[pl.BlockSpec(memory_s...]
    unnamed x48 -> x14, local copies, waits for them, and re-layouts: 5.19 us -> 1.76 us
  transfers between devices with their start and end apart: 45 -> 45, of which waited for: 19 -> 21; matrix products, arithmetic and copies ran while one was open for 3% -> 3% of each run, Pallas kernels for 15% -> 16%
where the time goes in v2:
time: 264 us; the launch traced here: 260 us
  waiting for transfers between devices  107 us (41%)
  Pallas kernels  88.3 us (33%)
  starting transfers between devices  46.4 us (18%)
  other arithmetic  9.16 us (3%)
  local copies, waits for them, and re-layouts  7.46 us (3%)
    ppermute x45, waiting for transfers between devices, send(): return lax.ppermute(x, AXES, route)  107 us
    pallas_call x10, Pallas kernels, call(): pl.pallas_call(kernel, out_shape=results, in_specs=[pl.BlockSpec(memory_s...  86.5 us
    ppermute x45, starting transfers between devices, send(): return lax.ppermute(x, AXES, route)  46.4 us
  transfers between devices with their start and end apart: 45, of which 21 were waited for; matrix products, arithmetic and copies ran while one was open for 3% of the time, Pallas kernels for 16%

profile of v2, /device:TPU:0, one launch (start us, length us, event | category | flops | bytes accessed | tf_op | source)
XLA Modules:
  0.0 259.9 jit_solution(7305080576111085631)
XLA Ops:
  6.4 5.1 %collective-permute-start.3 = (bf16[48,1280]{1,0:T(8,128)(2,1)S(1)}, bf16[48,1280]{1,0:T(8,128)(2,1)S(1)}, u32[]{:S(2)}, u32[]{:S(2)}) collective-permute-start(bf16[48,1280]{1,0:T(8,128)(2,1)S(1)} %maximum_select_fusion.3), channel_id=1, source_target_pairs={{0,24},{1,25},{2,26},{3,27},{4,28},{5,29},{6,30},{7,31},{8,16},{9,... | collective-permute-start | bytes 368648 | tf_op jit(solution)/shard_map/ppermute | solution.py:30
  12.2 3.6 %collective-permute-done.3 = bf16[48,1280]{1,0:T(8,128)(2,1)S(1)} collective-permute-done((bf16[48,1280]{1,0:T(8,128)(2,1)S(1)}, bf16[48,1280]{1,0:T(8,128)(2,1)S(1)}, u32[]{:S(2)}, u32[]{:S(2)}) %collective-permute-start.3) | collective-permute-done | bytes 122912 | tf_op jit(solution)/shard_map/ppermute | solution.py:30
  15.8 6.3 %collective-permute-done.2 = bf16[48,1280]{1,0:T(8,128)(2,1)S(1)} collective-permute-done((bf16[48,1280]{1,0:T(8,128)(2,1)S(1)}, bf16[48,1280]{1,0:T(8,128)(2,1)S(1)}, u32[]{:S(2)}, u32[]{:S(2)}) %collective-permute-start.2) | collective-permute-done | bytes 122912 | tf_op jit(solution)/shard_map/ppermute | solution.py:30
  23.8 2.5 collective-permute-start.11
  28.3 5.0 %collective-permute-done.11 = bf16[48,1920]{1,0:T(8,128)(2,1)S(1)} collective-permute-done((bf16[48,1920]{1,0:T(8,128)(2,1)S(1)}, bf16[48,1920]{1,0:T(8,128)(2,1)S(1)}, u32[]{:S(2)}, u32[]{:S(2)}) %collective-permute-start.11) | collective-permute-done | bytes 184352 | tf_op jit(solution)/shard_map/ppermute | solution.py:30
  33.3 7.4 %collective-permute-done.10 = bf16[48,1920]{1,0:T(8,128)(2,1)S(1)} collective-permute-done((bf16[48,1920]{1,0:T(8,128)(2,1)S(1)}, bf16[48,1920]{1,0:T(8,128)(2,1)S(1)}, u32[]{:S(2)}, u32[]{:S(2)}) %collective-permute-start.10) | collective-permute-done | bytes 184352 | tf_op jit(solution)/shard_map/ppermute | solution.py:30
  46.8 3.0 %collective-permute-start.17 = (bf16[192,384]{1,0:T(8,128)(2,1)S(1)}, bf16[192,384]{1,0:T(8,128)(2,1)S(1)}, u32[]{:S(2)}, u32[]{:S(2)}) collective-permute-start(bf16[192,384]{1,0:T(8,128)(2,1)S(1)} %maximum_select_fusion.1.refs_0_), channel_id=1, source_target_pairs={{0,8},{1,9},{2,10},{3,11},{4,12},{5,13},{6,14},{7,15},{8,0},{9,1},... | collective-permute-start | bytes 442376 | tf_op jit(solution)/shard_map/ppermute | solution.py:30
  49.8 10.5 %collective-permute-done.12 = bf16[4,48,1920]{2,1,0:T(8,128)(2,1)S(1)} collective-permute-done((bf16[4,48,1920]{2,1,0:T(8,128)(2,1)S(1)}, bf16[4,48,1920]{2,1,0:T(8,128)(2,1)S(1)}, u32[]{:S(2)}, u32[]{:S(2)}) %collective-permute-start.12) | collective-permute-done | bytes 737312 | tf_op jit(solution)/shard_map/ppermute | solution.py:30
  63.8 14.8 %collective-permute-done.20 = bf16[4,192,384]{2,1,0:T(8,128)(2,1)} collective-permute-done((bf16[4,192,384]{2,1,0:T(8,128)(2,1)S(1)}, bf16[4,192,384]{2,1,0:T(8,128)(2,1)}, u32[]{:S(2)}, u32[]{:S(2)}) %collective-permute-start.20) | collective-permute-done | bytes 589856 | tf_op jit(solution)/shard_map/ppermute | solution.py:30
  81.6 4.6 %collective-permute-done.13.p1 = bf16[2,4,48,1920]{3,2,1,0:T(8,128)(2,1)S(1)} collective-permute-done((bf16[2,4,48,1920]{3,2,1,0:T(8,128)(2,1)S(1)}, bf16[2,4,48,1920]{3,2,1,0:T(8,128)(2,1)S(1)}, u32[]{:S(2)}, u32[]{:S(2)}) %collective-permute-start.13) | collective-permute-done | bytes 1474592 | tf_op jit(solution)/shard_map/ppermute | solution.py:30
  86.2 7.8 %start.1 = (bf16[768,2304]{1,0:T(8,128)(2,1)S(1)}, f32[16,768]{1,0:T(8,128)S(1)}, f32[1,3072]{1,0:T(1,128)S(1)}, f32[192,576]{1,0:T(8,128)S(1)}, bf16[192,768]{1...) custom-call(s32[2]{0:T(128)S(1)} %pad_add_fusion.place_ref, ...), custom_call_target="tpu_custom_call" | custom-call | flops 20000000000 | bytes 73400320 | tf_op jit(solution)/shard_map/start/pallas_call | solution.py:749
  94.1 4.8 %collective-permute-done.21.p1 = bf16[2,4,192,384]{3,2,1,0:T(8,128)(2,1)S(1)} collective-permute-done((bf16[2,4,192,384]{3,2,1,0:T(8,128)(2,1)S(1)}, bf16[2,4,192,384]{3,2,1,0:T(8,128)(2,1)S(1)}, u32[]{:S(2)}, u32[]{:S(2)}) %collective-permute-start.21) | collective-permute-done | bytes 1179680 | tf_op jit(solution)/shard_map/ppermute | solution.py:30
  98.9 5.1 %up.1 = (bf16[768,3072]{1,0:T(8,128)(2,1)S(1)}, bf16[768,768]{1,0:T(8,128)(2,1)S(1)}, f32[192,768]{1,0:T(8,128)S(1)}, bf16[192,768]{1,0:T(8,128)(2,1)S(1)}, bf16...) custom-call(s32[2]{0:T(128)S(1)} %pad_add_fusion.place_ref, ...), custom_call_target="tpu_custom_call" | custom-call | flops 12000000000 | bytes 41943040 | tf_op jit(solution)/shard_map/up/pallas_call | solution.py:749
  104.0 44.0 %main.1 = (bf16[192,768]{1,0:T(8,128)(2,1)}, f32[192,768]{1,0:T(8,128)S(1)}, f32[16,768]{1,0:T(8,128)S(1)}, bf16[384,768]{1,0:T(8,128)(2,1)S(1)}, bf16[384,768]{...) custom-call(s32[2]{0:T(128)S(1)} %pad_add_fusion.place_ref, ...), custom_call_target="tpu_custom_call" | custom-call | flops 36238786560 | bytes 62914560 | tf_op jit(solution)/shard_map/main/pallas_call | solution.py:749
  148.0 3.9 %give_down.1 = bf16[16,192,384]{2,1,0:T(8,128)(2,1)S(1)} custom-call(s32[2]{0:T(128)S(1)} %pad_add_fusion.place_ref, bf16[192,3072]{1,0:T(8,128)(2,1)S(1)} %get-tuple-element.85.active_0, bf16[384,3072]{1,0:T(8,128)(2,1)S(1)} %get-tuple-element.97.active, bf16[576,768]{1,0:T(8,128)(2,1)S(1)} %get-tuple-element.99.d_z), custom_call_target="tpu_custom_call" | custom-call | flops 10000000000 | bytes 36700160 | tf_op jit(solution)/shard_map/give_down/pallas_call | solution.py:749
  152.4 3.6 %keep_down.1 = bf16[16,192,384]{2,1,0:T(8,128)(2,1)S(1)} custom-call(s32[2]{0:T(128)S(1)} %pad_add_fusion.place_ref, bf16[192,3072]{1,0:T(8,128)(2,1)S(1)} %get-tuple-element.85.active_0, bf16[384,3072]{1,0:T(8,128)(2,1)S(1)} %get-tuple-element.97.active, bf16[576,768]{1,0:T(8,128)(2,1)S(1)} %get-tuple-element.99.d_z), custom_call_target="tpu_custom_call" | custom-call | flops 10000000000 | bytes 36700160 | tf_op jit(solution)/shard_map/keep_down/pallas_call | solution.py:749
  159.9 6.3 %give_up.1 = (bf16[16,48,1920]{2,1,0:T(8,128)(2,1)S(1)}, f32[192,768]{1,0:T(8,128)S(1)}, f32[16,768]{1,0:T(8,128)S(1)}, bf16[192,768]{1,0:T(8,128)(2,1)S(1)}, bf16[192,768]{1,0:T(8,128)(2,1)S(1)}) custom-call(s32[2]{0:T(128)S(1)} %pad_add_fusion.place_ref, f32[16,768]{1,0:T(8,128)S(1)} %get-tuple-element.73.vec, ...), custom_call_target="tpu_custom_call" | custom-call | flops 10000000000 | bytes 36700160 | tf_op jit(solution)/shard_map/give_up/pallas_call | solution.py:749
  166.9 4.5 %keep_up.1 = (bf16[16,48,1920]{2,1,0:T(8,128)(2,1)S(1)}, f32[1,3072]{1,0:T(1,128)S(1)}) custom-call(s32[2]{0:T(128)S(1)} %pad_add_fusion.place_ref, bf16[192,768]{1,0:T(8,128)(2,1)S(1)} %get-tuple-element.92.x_mlp_0, bf16[384,768]{1,0:T(8,128)(2,1)S(1)} %get-tuple-element.93.x_mlp, bf16[192,3072]{1,0:T(8,128)(2,1)S(1)} %get-tuple-element.94.d_hidden_0, ...), custom_call_target="tpu_custom_call" | custom-call | flops 10000000000 | bytes 36700160 | tf_op jit(solution)/shard_map/keep_up/pallas_call | solution.py:749
  171.4 3.9 %collective-permute-done.25 = bf16[2,4,192,384]{3,2,1,0:T(8,128)(2,1)S(1)} collective-permute-done((bf16[2,4,192,384]{3,2,1,0:T(8,128)(2,1)S(1)}, bf16[2,4,192,384]{3,2,1,0:T(8,128)(2,1)S(1)}, u32[]{:S(2)}, u32[]{:S(2)}) %collective-permute-start.25) | collective-permute-done | bytes 1179680 | tf_op jit(solution)/shard_map/ppermute | solution.py:30
  177.3 6.4 %last.1 = (bf16[192,768]{1,0:T(8,128)(2,1)}, bf16[192,2304]{1,0:T(8,128)(2,1)S(1)}, bf16[768,256]{1,0:T(8,128)(2,1)S(1)}) custom-call(s32[2]{0:T(128)S(1)} %pad_add_fusion.place_ref, f32[16,768]{1,0:T(8,128)S(1)} %get-tuple-element.73.vec, bf16[768,2304]{1,0:T(8,128)(2,1)S(1)} %copy-done.4, bf16[192,768]{1,0:T(8,128)(2,1)S(1)} %get-tuple-element.90.q, ...), custom_call_target="tpu_custom_call" | custom-call | flops 40000000000 | bytes 146800640 | tf_op jit(solution)/shard_map/last/pallas_call | solution.py:749
  185.5 2.5 give_qkv.1
  188.1 2.5 keep_qkv.1
  192.3 2.8 %collective-permute-start.37 = (bf16[192,384]{1,0:T(8,128)(2,1)S(1)}, bf16[192,384]{1,0:T(8,128)(2,1)S(1)}, u32[]{:S(2)}, u32[]{:S(2)}) collective-permute-start(bf16[192,384]{1,0:T(8,128)(2,1)S(1)} %get-tuple-element.217), channel_id=1, source_target_pairs={{0,8},{1,9},{2,10},{3,11},{4,12},{5,13},{6,14},{7,15},{8,0},{9,1},... | collective-permute-start | bytes 442376 | tf_op jit(solution)/shard_map/ppermute | solution.py:30
  195.1 4.2 %collective-permute-done.39 = bf16[192,384]{1,0:T(8,128)(2,1)S(1)} collective-permute-done((bf16[192,384]{1,0:T(8,128)(2,1)S(1)}, bf16[192,384]{1,0:T(8,128)(2,1)S(1)}, u32[]{:S(2)}, u32[]{:S(2)}) %collective-permute-start.39) | collective-permute-done | bytes 147488 | tf_op jit(solution)/shard_map/ppermute | solution.py:30
  199.3 5.8 %collective-permute-done.38 = bf16[192,384]{1,0:T(8,128)(2,1)S(1)} collective-permute-done((bf16[192,384]{1,0:T(8,128)(2,1)S(1)}, bf16[192,384]{1,0:T(8,128)(2,1)S(1)}, u32[]{:S(2)}, u32[]{:S(2)}) %collective-permute-start.38) | collective-permute-done | bytes 147488 | tf_op jit(solution)/shard_map/ppermute | solution.py:30
  210.7 14.0 %collective-permute-done.36 = bf16[4,48,1920]{2,1,0:T(8,128)(2,1)S(1)} collective-permute-done((bf16[4,48,1920]{2,1,0:T(8,128)(2,1)S(1)}, bf16[4,48,1920]{2,1,0:T(8,128)(2,1)S(1)}, u32[]{:S(2)}, u32[]{:S(2)}) %collective-permute-start.36) | collective-permute-done | bytes 737312 | tf_op jit(solution)/shard_map/ppermute | solution.py:30
  224.9 2.3 collective-permute-start.41
  231.3 2.5 collective-permute-done.40
  233.8 4.6 %collective-permute-done.41 = bf16[48,1920]{1,0:T(8,128)(2,1)S(1)} collective-permute-done((bf16[48,1920]{1,0:T(8,128)(2,1)S(1)}, bf16[48,1920]{1,0:T(8,128)(2,1)S(1)}, u32[]{:S(2)}, u32[]{:S(2)}) %collective-permute-start.41) | collective-permute-done | bytes 184352 | tf_op jit(solution)/shard_map/ppermute | solution.py:30
  238.8 3.1 %collective-permute-start.31 = (bf16[48,1280]{1,0:T(8,128)(2,1)S(1)}, bf16[48,1280]{1,0:T(8,128)(2,1)S(1)}, u32[]{:S(2)}, u32[]{:S(2)}) collective-permute-start(bf16[48,1280]{1,0:T(8,128)(2,1)S(1)} %get-tuple-element.218), channel_id=1, source_target_pairs={{0,8},{1,9},{2,10},{3,11},{4,12},{5,13},{6,14},{7,15},{8,0},{9,1},... | collective-permute-start | bytes 368648 | tf_op jit(solution)/shard_map/ppermute | solution.py:30
  245.9 4.5 %collective-permute-done.33 = bf16[48,1280]{1,0:T(8,128)(2,1)S(1)} collective-permute-done((bf16[48,1280]{1,0:T(8,128)(2,1)S(1)}, bf16[48,1280]{1,0:T(8,128)(2,1)S(1)}, u32[]{:S(2)}, u32[]{:S(2)}) %collective-permute-start.33) | collective-permute-done | bytes 122912 | tf_op jit(solution)/shard_map/ppermute | solution.py:30
  250.4 4.6 %collective-permute-done.32 = bf16[48,1280]{1,0:T(8,128)(2,1)S(1)} collective-permute-done((bf16[48,1280]{1,0:T(8,128)(2,1)S(1)}, bf16[48,1280]{1,0:T(8,128)(2,1)S(1)}, u32[]{:S(2)}, u32[]{:S(2)}) %collective-permute-start.32) | collective-permute-done | bytes 122912 | tf_op jit(solution)/shard_map/ppermute | solution.py:30
  (135 shorter events, 51.6 us)
Async XLA Ops:
  6.3 17.5 %collective-permute-start.8 = (bf16[24,1920]{1,0:T(8,128)(2,1)S(1)}, bf16[24,1920]{1,0:T(8,128)(2,1)S(1)}, u32[]{:S(2)}, u32[]{:S(2)}) collective-permute-start(bf16[24,1920]{1,0:T(8,128)(2,1)S(1)} %get-tuple-element.230), channel_id=1, source_target_pairs={{0,1},{1,0},{2,3},{3,2},{4,5},{5,4},{6,7},{7,6},{8,9},{9,8},{10,11... | collective-permute-start | bytes 276488 | tf_op jit(solution)/shard_map/ppermute | solution.py:30
  11.6 10.6 %collective-permute-start.2 = (bf16[48,1280]{1,0:T(8,128)(2,1)S(1)}, bf16[48,1280]{1,0:T(8,128)(2,1)S(1)}, u32[]{:S(2)}, u32[]{:S(2)}) collective-permute-start(bf16[48,1280]{1,0:T(8,128)(2,1)S(1)} %maximum_select_fusion.3), channel_id=1, source_target_pairs={{0,16},{1,17},{2,18},{3,19},{4,20},{5,21},{6,22},{7,23},{8,24},{9,... | collective-permute-start | bytes 368648 | tf_op jit(solution)/shard_map/ppermute | solution.py:30
  11.6 10.6 %collective-permute-start.1 = (bf16[48,1280]{1,0:T(8,128)(2,1)S(1)}, bf16[48,1280]{1,0:T(8,128)(2,1)S(1)}, u32[]{:S(2)}, u32[]{:S(2)}) collective-permute-start(bf16[48,1280]{1,0:T(8,128)(2,1)S(1)} %maximum_select_fusion.3), channel_id=1, source_target_pairs={{0,8},{1,9},{2,10},{3,11},{4,12},{5,13},{6,14},{7,15},{8,0},{9,1},... | collective-permute-start | bytes 368648 | tf_op jit(solution)/shard_map/ppermute | solution.py:30
  22.2 20.1 %collective-permute-start.4 = (bf16[4,48,1280]{2,1,0:T(8,128)(2,1)S(1)}, bf16[4,48,1280]{2,1,0:T(8,128)(2,1)S(1)}, u32[]{:S(2)}, u32[]{:S(2)}) collective-permute-start(bf16[4,48,1280]{2,1,0:T(8,128)(2,1)S(1)} %pad_maximum_fusion.3.refs_0_), channel_id=1, source_target_pairs={{0,4},{1,3},{2,6},{3,1},{4,0},{5,7},{6,2},{7,5},{8,12},{9,11},{10,... | collective-permute-start | bytes 1474568 | tf_op jit(solution)/shard_map/ppermute | solution.py:30
  23.8 9.5 %collective-permute-start.11 = (bf16[48,1920]{1,0:T(8,128)(2,1)S(1)}, bf16[48,1920]{1,0:T(8,128)(2,1)S(1)}, u32[]{:S(2)}, u32[]{:S(2)}) collective-permute-start(bf16[48,1920]{1,0:T(8,128)(2,1)S(1)} %maximum_select_fusion), channel_id=1, source_target_pairs={{0,24},{1,25},{2,26},{3,27},{4,28},{5,29},{6,30},{7,31},{8,16},{9,... | collective-permute-start | bytes 552968 | tf_op jit(solution)/shard_map/ppermute | solution.py:30
  26.4 14.4 %collective-permute-start.10 = (bf16[48,1920]{1,0:T(8,128)(2,1)S(1)}, bf16[48,1920]{1,0:T(8,128)(2,1)S(1)}, u32[]{:S(2)}, u32[]{:S(2)}) collective-permute-start(bf16[48,1920]{1,0:T(8,128)(2,1)S(1)} %maximum_select_fusion), channel_id=1, source_target_pairs={{0,16},{1,17},{2,18},{3,19},{4,20},{5,21},{6,22},{7,23},{8,24},{9,... | collective-permute-start | bytes 552968 | tf_op jit(solution)/shard_map/ppermute | solution.py:30
  26.4 14.4 %collective-permute-start.9 = (bf16[48,1920]{1,0:T(8,128)(2,1)S(1)}, bf16[48,1920]{1,0:T(8,128)(2,1)S(1)}, u32[]{:S(2)}, u32[]{:S(2)}) collective-permute-start(bf16[48,1920]{1,0:T(8,128)(2,1)S(1)} %maximum_select_fusion), channel_id=1, source_target_pairs={{0,8},{1,9},{2,10},{3,11},{4,12},{5,13},{6,14},{7,15},{8,0},{9,1},... | collective-permute-start | bytes 552968 | tf_op jit(solution)/shard_map/ppermute | solution.py:30
  40.9 19.4 %collective-permute-start.12 = (bf16[4,48,1920]{2,1,0:T(8,128)(2,1)S(1)}, bf16[4,48,1920]{2,1,0:T(8,128)(2,1)S(1)}, u32[]{:S(2)}, u32[]{:S(2)}) collective-permute-start(bf16[4,48,1920]{2,1,0:T(8,128)(2,1)S(1)} %get-tuple-element.222), channel_id=1, source_target_pairs={{0,4},{1,3},{2,6},{3,1},{4,0},{5,7},{6,2},{7,5},{8,12},{9,11},{10,... | collective-permute-start | bytes 2211848 | tf_op jit(solution)/shard_map/ppermute | solution.py:30
  43.4 18.0 %collective-permute-start.5 = (bf16[2,4,48,1280]{3,2,1,0:T(8,128)(2,1)}, bf16[2,4,48,1280]{3,2,1,0:T(8,128)(2,1)}, u32[]{:S(2)}, u32[]{:S(2)}) collective-permute-start(bf16[2,4,48,1280]{3,2,1,0:T(8,128)(2,1)} %stack.111.p0), channel_id=1, source_target_pairs={{0,2},{1,5},{2,0},{3,7},{4,6},{5,1},{6,4},{7,3},{8,10},{9,13},{10,... | collective-permute-start | bytes 2949128 | tf_op jit(solution)/shard_map/ppermute | solution.py:30
  45.4 15.1 %collective-permute-start.19 = (bf16[192,384]{1,0:T(8,128)(2,1)S(1)}, bf16[192,384]{1,0:T(8,128)(2,1)S(1)}, u32[]{:S(2)}, u32[]{:S(2)}) collective-permute-start(bf16[192,384]{1,0:T(8,128)(2,1)S(1)} %maximum_select_fusion.1.refs_0_), channel_id=1, source_target_pairs={{0,24},{1,25},{2,26},{3,27},{4,28},{5,29},{6,30},{7,31},{8,16},{9,... | collective-permute-start | bytes 442376 | tf_op jit(solution)/shard_map/ppermute | solution.py:30
  46.8 15.3 %collective-permute-start.18 = (bf16[192,384]{1,0:T(8,128)(2,1)S(1)}, bf16[192,384]{1,0:T(8,128)(2,1)S(1)}, u32[]{:S(2)}, u32[]{:S(2)}) collective-permute-start(bf16[192,384]{1,0:T(8,128)(2,1)S(1)} %maximum_select_fusion.1.refs_0_), channel_id=1, source_target_pairs={{0,16},{1,17},{2,18},{3,19},{4,20},{5,21},{6,22},{7,23},{8,24},{9,... | collective-permute-start | bytes 442376 | tf_op jit(solution)/shard_map/ppermute | solution.py:30
  46.8 15.3 %collective-permute-start.17 = (bf16[192,384]{1,0:T(8,128)(2,1)S(1)}, bf16[192,384]{1,0:T(8,128)(2,1)S(1)}, u32[]{:S(2)}, u32[]{:S(2)}) collective-permute-start(bf16[192,384]{1,0:T(8,128)(2,1)S(1)} %maximum_select_fusion.1.refs_0_), channel_id=1, source_target_pairs={{0,8},{1,9},{2,10},{3,11},{4,12},{5,13},{6,14},{7,15},{8,0},{9,1},... | collective-permute-start | bytes 442376 | tf_op jit(solution)/shard_map/ppermute | solution.py:30
  60.3 21.1 %collective-permute-start.6 = (bf16[2,4,48,1280]{3,2,1,0:T(8,128)(2,1)}, bf16[2,4,48,1280]{3,2,1,0:T(8,128)(2,1)}, u32[]{:S(2)}, u32[]{:S(2)}) collective-permute-start(bf16[2,4,48,1280]{3,2,1,0:T(8,128)(2,1)} %stack.111.p0), channel_id=1, source_target_pairs={{0,1},{1,0},{2,3},{3,2},{4,5},{5,4},{6,7},{7,6},{8,9},{9,8},{10,11... | collective-permute-start | bytes 2949128 | tf_op jit(solution)/shard_map/ppermute | solution.py:30
  60.5 25.7 %collective-permute-start.13 = (bf16[2,4,48,1920]{3,2,1,0:T(8,128)(2,1)S(1)}, bf16[2,4,48,1920]{3,2,1,0:T(8,128)(2,1)S(1)}, u32[]{:S(2)}, u32[]{:S(2)}) collective-permute-start(bf16[2,4,48,1920]{3,2,1,0:T(8,128)(2,1)S(1)} %pad_maximum_fusion.p0), channel_id=1, source_target_pairs={{0,2},{1,5},{2,0},{3,7},{4,6},{5,1},{6,4},{7,3},{8,10},{9,13},{10,... | collective-permute-start | bytes 4423688 | tf_op jit(solution)/shard_map/ppermute | solution.py:30
  61.3 24.9 %collective-permute-start.7 = (bf16[2,4,48,1280]{3,2,1,0:T(8,128)(2,1)}, bf16[2,4,48,1280]{3,2,1,0:T(8,128)(2,1)}, u32[]{:S(2)}, u32[]{:S(2)}) collective-permute-start(bf16[2,4,48,1280]{3,2,1,0:T(8,128)(2,1)} %collective-permute-done.5.p1), channel_id=1, source_target_pairs={{0,1},{1,0},{2,3},{3,2},{4,5},{5,4},{6,7},{7,6},{8,9},{9,8},{10,11... | collective-permute-start | bytes 2949128 | tf_op jit(solution)/shard_map/ppermute | solution.py:30
  62.2 16.4 %collective-permute-start.20 = (bf16[4,192,384]{2,1,0:T(8,128)(2,1)S(1)}, bf16[4,192,384]{2,1,0:T(8,128)(2,1)}, u32[]{:S(2)}, u32[]{:S(2)}) collective-permute-start(bf16[4,192,384]{2,1,0:T(8,128)(2,1)S(1)} %stack.112), channel_id=1, source_target_pairs={{0,4},{1,3},{2,6},{3,1},{4,0},{5,7},{6,2},{7,5},{8,12},{9,11},{10,... | collective-permute-start | bytes 1769480 | tf_op jit(solution)/shard_map/ppermute | solution.py:30
  79.8 24.2 %collective-permute-start.22 = (bf16[2,4,192,384]{3,2,1,0:T(8,128)(2,1)S(1)}, bf16[2,4,192,384]{3,2,1,0:T(8,128)(2,1)S(1)}, u32[]{:S(2)}, u32[]{:S(2)}) collective-permute-start(bf16[2,4,192,384]{3,2,1,0:T(8,128)(2,1)S(1)} %pad_maximum_fusion.1.p0), channel_id=1, source_target_pairs={{0,1},{1,0},{2,3},{3,2},{4,5},{5,4},{6,7},{7,6},{8,9},{9,8},{10,11... | collective-permute-start | bytes 3538952 | tf_op jit(solution)/shard_map/ppermute | solution.py:30
  79.9 19.0 %collective-permute-start.21 = (bf16[2,4,192,384]{3,2,1,0:T(8,128)(2,1)S(1)}, bf16[2,4,192,384]{3,2,1,0:T(8,128)(2,1)S(1)}, u32[]{:S(2)}, u32[]{:S(2)}) collective-permute-start(bf16[2,4,192,384]{3,2,1,0:T(8,128)(2,1)S(1)} %pad_maximum_fusion.1.p0), channel_id=1, source_target_pairs={{0,2},{1,5},{2,0},{3,7},{4,6},{5,1},{6,4},{7,3},{8,10},{9,13},{10,... | collective-permute-start | bytes 3538952 | tf_op jit(solution)/shard_map/ppermute | solution.py:30
  81.4 17.4 %collective-permute-start.14 = (bf16[2,4,48,1920]{3,2,1,0:T(8,128)(2,1)S(1)}, bf16[2,4,48,1920]{3,2,1,0:T(8,128)(2,1)S(1)}, u32[]{:S(2)}, u32[]{:S(2)}) collective-permute-start(bf16[2,4,48,1920]{3,2,1,0:T(8,128)(2,1)S(1)} %pad_maximum_fusion.p0), channel_id=1, source_target_pairs={{0,1},{1,0},{2,3},{3,2},{4,5},{5,4},{6,7},{7,6},{8,9},{9,8},{10,11... | collective-permute-start | bytes 4423688 | tf_op jit(solution)/shard_map/ppermute | solution.py:30
  86.2 12.6 %collective-permute-start.15 = (bf16[2,4,48,1920]{3,2,1,0:T(8,128)(2,1)S(1)}, bf16[2,4,48,1920]{3,2,1,0:T(8,128)(2,1)S(1)}, u32[]{:S(2)}, u32[]{:S(2)}) collective-permute-start(bf16[2,4,48,1920]{3,2,1,0:T(8,128)(2,1)S(1)} %collective-permute-done.13.p1), channel_id=1, source_target_pairs={{0,1},{1,0},{2,3},{3,2},{4,5},{5,4},{6,7},{7,6},{8,9},{9,8},{10,11... | collective-permute-start | bytes 4423688 | tf_op jit(solution)/shard_map/ppermute | solution.py:30
  159.0 16.3 %collective-permute-start.25 = (bf16[2,4,192,384]{3,2,1,0:T(8,128)(2,1)S(1)}, bf16[2,4,192,384]{3,2,1,0:T(8,128)(2,1)S(1)}, u32[]{:S(2)}, u32[]{:S(2)}) collective-permute-start(bf16[2,4,192,384]{3,2,1,0:T(8,128)(2,1)S(1)} %bitcast.132), channel_id=1, source_target_pairs={{0,2},{1,5},{2,0},{3,7},{4,6},{5,1},{6,4},{7,3},{8,10},{9,13},{10,... | collective-permute-start | bytes 3538952 | tf_op jit(solution)/shard_map/ppermute | solution.py:30
  166.2 17.5 %collective-permute-start.26 = (bf16[16,48,1920]{2,1,0:T(8,128)(2,1)S(1)}, bf16[16,48,1920]{2,1,0:T(8,128)(2,1)S(1)}, u32[]{:S(2)}, u32[]{:S(2)}) collective-permute-start(bf16[16,48,1920]{2,1,0:T(8,128)(2,1)S(1)} %get-tuple-element.118), channel_id=1, source_target_pairs={{0,1},{1,0},{2,3},{3,2},{4,5},{5,4},{6,7},{7,6},{8,9},{9,8},{10,11... | collective-permute-start | bytes 8847368 | tf_op jit(solution)/shard_map/ppermute | solution.py:30
  175.6 9.9 %collective-permute-start.27 = (bf16[4,192,384]{2,1,0:T(8,128)(2,1)S(1)}, bf16[4,192,384]{2,1,0:T(8,128)(2,1)S(1)}, u32[]{:S(2)}, u32[]{:S(2)}) collective-permute-start(bf16[4,192,384]{2,1,0:T(8,128)(2,1)S(1)} %get-tuple-element.209), channel_id=1, source_target_pairs={{0,4},{1,3},{2,6},{3,1},{4,0},{5,7},{6,2},{7,5},{8,12},{9,11},{10,... | collective-permute-start | bytes 1769480 | tf_op jit(solution)/shard_map/ppermute | solution.py:30
  184.3 20.9 %collective-permute-start.35 = (bf16[2,4,48,1920]{3,2,1,0:T(8,128)(2,1)S(1)}, bf16[2,4,48,1920]{3,2,1,0:T(8,128)(2,1)S(1)}, u32[]{:S(2)}, u32[]{:S(2)}) collective-permute-start(bf16[2,4,48,1920]{3,2,1,0:T(8,128)(2,1)S(1)} %bitcast.129), channel_id=1, source_target_pairs={{0,2},{1,5},{2,0},{3,7},{4,6},{5,1},{6,4},{7,3},{8,10},{9,13},{10,... | collective-permute-start | bytes 4423688 | tf_op jit(solution)/shard_map/ppermute | solution.py:30
  188.0 19.0 %collective-permute-start.28 = (bf16[16,48,1280]{2,1,0:T(8,128)(2,1)S(1)}, bf16[16,48,1280]{2,1,0:T(8,128)(2,1)S(1)}, u32[]{:S(2)}, u32[]{:S(2)}) collective-permute-start(bf16[16,48,1280]{2,1,0:T(8,128)(2,1)S(1)} %give_qkv.1), channel_id=1, source_target_pairs={{0,1},{1,0},{2,3},{3,2},{4,5},{5,4},{6,7},{7,6},{8,9},{9,8},{10,11... | collective-permute-start | bytes 5898248 | tf_op jit(solution)/shard_map/ppermute | solution.py:30
  192.3 12.9 %collective-permute-start.38 = (bf16[192,384]{1,0:T(8,128)(2,1)S(1)}, bf16[192,384]{1,0:T(8,128)(2,1)S(1)}, u32[]{:S(2)}, u32[]{:S(2)}) collective-permute-start(bf16[192,384]{1,0:T(8,128)(2,1)S(1)} %get-tuple-element.216), channel_id=1, source_target_pairs={{0,16},{1,17},{2,18},{3,19},{4,20},{5,21},{6,22},{7,23},{8,24},{9,... | collective-permute-start | bytes 442376 | tf_op jit(solution)/shard_map/ppermute | solution.py:30
  192.3 12.9 %collective-permute-start.37 = (bf16[192,384]{1,0:T(8,128)(2,1)S(1)}, bf16[192,384]{1,0:T(8,128)(2,1)S(1)}, u32[]{:S(2)}, u32[]{:S(2)}) collective-permute-start(bf16[192,384]{1,0:T(8,128)(2,1)S(1)} %get-tuple-element.217), channel_id=1, source_target_pairs={{0,8},{1,9},{2,10},{3,11},{4,12},{5,13},{6,14},{7,15},{8,0},{9,1},... | collective-permute-start | bytes 442376 | tf_op jit(solution)/shard_map/ppermute | solution.py:30
  205.6 19.1 %collective-permute-start.36 = (bf16[4,48,1920]{2,1,0:T(8,128)(2,1)S(1)}, bf16[4,48,1920]{2,1,0:T(8,128)(2,1)S(1)}, u32[]{:S(2)}, u32[]{:S(2)}) collective-permute-start(bf16[4,48,1920]{2,1,0:T(8,128)(2,1)S(1)} %get-tuple-element.207), channel_id=1, source_target_pairs={{0,4},{1,3},{2,6},{3,1},{4,0},{5,7},{6,2},{7,5},{8,12},{9,11},{10,... | collective-permute-start | bytes 2211848 | tf_op jit(solution)/shard_map/ppermute | solution.py:30
  207.5 21.8 %collective-permute-start.29 = (bf16[2,4,48,1280]{3,2,1,0:T(8,128)(2,1)S(1)}, bf16[2,4,48,1280]{3,2,1,0:T(8,128)(2,1)S(1)}, u32[]{:S(2)}, u32[]{:S(2)}) collective-permute-start(bf16[2,4,48,1280]{3,2,1,0:T(8,128)(2,1)S(1)} %bitcast.133), channel_id=1, source_target_pairs={{0,2},{1,5},{2,0},{3,7},{4,6},{5,1},{6,4},{7,3},{8,10},{9,13},{10,... | collective-permute-start | bytes 2949128 | tf_op jit(solution)/shard_map/ppermute | solution.py:30
  224.9 13.5 %collective-permute-start.41 = (bf16[48,1920]{1,0:T(8,128)(2,1)S(1)}, bf16[48,1920]{1,0:T(8,128)(2,1)S(1)}, u32[]{:S(2)}, u32[]{:S(2)}) collective-permute-start(bf16[48,1920]{1,0:T(8,128)(2,1)S(1)} %get-tuple-element.128), channel_id=1, source_target_pairs={{0,16},{1,17},{2,18},{3,19},{4,20},{5,21},{6,22},{7,23},{8,24},{9,... | collective-permute-start | bytes 552968 | tf_op jit(solution)/shard_map/ppermute | solution.py:30
  227.2 11.2 %collective-permute-start.42 = (bf16[48,1920]{1,0:T(8,128)(2,1)S(1)}, bf16[48,1920]{1,0:T(8,128)(2,1)S(1)}, u32[]{:S(2)}, u32[]{:S(2)}) collective-permute-start(bf16[48,1920]{1,0:T(8,128)(2,1)S(1)} %get-tuple-element.129), channel_id=1, source_target_pairs={{0,24},{1,25},{2,26},{3,27},{4,28},{5,29},{6,30},{7,31},{8,16},{9,... | collective-permute-start | bytes 552968 | tf_op jit(solution)/shard_map/ppermute | solution.py:30
  243.6 11.5 %collective-permute-start.32 = (bf16[48,1280]{1,0:T(8,128)(2,1)S(1)}, bf16[48,1280]{1,0:T(8,128)(2,1)S(1)}, u32[]{:S(2)}, u32[]{:S(2)}) collective-permute-start(bf16[48,1280]{1,0:T(8,128)(2,1)S(1)} %get-tuple-element.220), channel_id=1, source_target_pairs={{0,16},{1,17},{2,18},{3,19},{4,20},{5,21},{6,22},{7,23},{8,24},{9,... | collective-permute-start | bytes 368648 | tf_op jit(solution)/shard_map/ppermute | solution.py:30
  (19 other events, 140.0 us)

commit v3 on v2

--- a/solution.py
+++ b/solution.py
@@ -149,7 +149,7 @@
 
 
 def end_scatter(core, begun):
-    begun = [begun[0]] + [near_step(begun[n], FAR_WEIGHTS[n]) for n in (1, 2)]
+    begun = [(begun[0][0], after(begun[0][1], begun[1][0]))] + [near_step(begun[n], FAR_WEIGHTS[n]) for n in (1, 2)]
     results, earlier = [], None
     for n in range(len(begun)):
         near, keep = begun[n]
@@ -161,13 +161,16 @@
             total = total + part.astype(F32)
         total = total.reshape(2, total.shape[0] // 2, total.shape[1])
         mine = jnp.where(core == 0, total[0], total[1])
-        other = send(jnp.where(core == 0, total[1], total[0]), TO_MATE)
+        theirs = jnp.where(core == 0, total[1], total[0])
+        if n == 0:
+            theirs = after(theirs, begun[1][0])
+        other = send(theirs, TO_MATE)
         results.append((jnp.where(core == 0, mine, other), jnp.where(core == 0, other, mine)))
     return results
 
 
 MATE_WEIGHTS = (0, 15, 0)
-FAR_WEIGHTS = (0, 0, 0)
+FAR_WEIGHTS = (40, 0, 0)
 SMALL = 256
 
 
@@ -840,8 +843,11 @@
         kept(up_shape, full(1, inner)), [],
         *COST,
     )
-    up_got = mate_step(give_up)
+    begun.append(begin_scatter(mate_step(give_up), give_up, keep_up, MATE_WEIGHTS[1]))
     state = after(state, begun[0][0])
+    near_0 = near_step(begun[0], FAR_WEIGHTS[0])
+    state = after(state, begun[1][0])
+    begun[1] = far_step(begun[1])
     token_grad, d_mixed_0, g_small = call(
         last_kernel, "last",
         [place]
@@ -855,10 +861,6 @@
         ],
         40 * 10**9, 140 * 2**20,
     )
-    begun.append(begin_scatter(after(up_got, g_small), give_up, keep_up, MATE_WEIGHTS[1]))
-    g_small = after(g_small, begun[1][0])
-    begun[1] = far_step(begun[1])
-    near_0 = near_step(begun[0], FAR_WEIGHTS[0])
     last_shape = low(16, width // 16, 3 * width // 2 + SMALL // 2)
     ends = []
     for name, swapped in (("give_qkv", 1), ("keep_qkv", 0)):
@@ -867,8 +869,9 @@
             functools.partial(qkv_kernel, swapped), name,
             [place] + L(x_norm_0, x_norm, d_mixed_0, d_mixed, after(g_small, *earlier)), kept(last_shape), [], TINY, TINY,
         )
-    near_0 = (near_0[0], after(near_0[1], ends[1]))
-    return output, token_grad, (near_0, begun[1], far_step(begin_scatter(mate_step(ends[0]), *ends, MATE_WEIGHTS[2])))
+    give, keep = begin_scatter(mate_step(ends[0]), *ends, MATE_WEIGHTS[2])
+    near_0 = (near_0[0], after(near_0[1], give))
+    return output, token_grad, (near_0, begun[1], far_step((give, keep)))
 
 
 def per_device(

time: 264 us -> 260 us (0.985)
  waiting for transfers between devices: 107 us -> 103 us
    ppermute x45, waiting for transfers between devices: 107 us -> 103 us  [send(): return lax.ppermute(x, AXES, route)]
where the time goes in v3:
time: 260 us; the launch traced here: 256 us
  waiting for transfers between devices  103 us (40%)
  Pallas kernels  88.6 us (34%)
  starting transfers between devices  45.6 us (18%)
  other arithmetic  8.89 us (3%)
  local copies, waits for them, and re-layouts  8.14 us (3%)
    ppermute x45, waiting for transfers between devices, send(): return lax.ppermute(x, AXES, route)  103 us
    pallas_call x10, Pallas kernels, call(): pl.pallas_call(kernel, out_shape=results, in_specs=[pl.BlockSpec(memory_s...  86.5 us
    ppermute x45, starting transfers between devices, send(): return lax.ppermute(x, AXES, route)  45.6 us
  transfers between devices with their start and end apart: 45, of which 21 were waited for; matrix products, arithmetic and copies ran while one was open for 3% of the time, Pallas kernels for 16%

profile of v3, /device:TPU:0, one launch (start us, length us, event | category | flops | bytes accessed | tf_op | source)
XLA Modules:
  0.0 256.1 jit_solution(1879757526516800501)
XLA Ops:
  6.4 5.1 %collective-permute-start.3 = (bf16[48,1280]{1,0:T(8,128)(2,1)S(1)}, bf16[48,1280]{1,0:T(8,128)(2,1)S(1)}, u32[]{:S(2)}, u32[]{:S(2)}) collective-permute-start(bf16[48,1280]{1,0:T(8,128)(2,1)S(1)} %maximum_select_fusion.3), channel_id=1, source_target_pairs={{0,24},{1,25},{2,26},{3,27},{4,28},{5,29},{6,30},{7,31},{8,16},{9,... | collective-permute-start | bytes 368648 | tf_op jit(solution)/shard_map/ppermute | solution.py:30
  12.2 3.6 %collective-permute-done.3 = bf16[48,1280]{1,0:T(8,128)(2,1)S(1)} collective-permute-done((bf16[48,1280]{1,0:T(8,128)(2,1)S(1)}, bf16[48,1280]{1,0:T(8,128)(2,1)S(1)}, u32[]{:S(2)}, u32[]{:S(2)}) %collective-permute-start.3) | collective-permute-done | bytes 122912 | tf_op jit(solution)/shard_map/ppermute | solution.py:30
  15.8 6.3 %collective-permute-done.2 = bf16[48,1280]{1,0:T(8,128)(2,1)S(1)} collective-permute-done((bf16[48,1280]{1,0:T(8,128)(2,1)S(1)}, bf16[48,1280]{1,0:T(8,128)(2,1)S(1)}, u32[]{:S(2)}, u32[]{:S(2)}) %collective-permute-start.2) | collective-permute-done | bytes 122912 | tf_op jit(solution)/shard_map/ppermute | solution.py:30
  23.8 2.5 collective-permute-start.11
  28.3 5.0 %collective-permute-done.11 = bf16[48,1920]{1,0:T(8,128)(2,1)S(1)} collective-permute-done((bf16[48,1920]{1,0:T(8,128)(2,1)S(1)}, bf16[48,1920]{1,0:T(8,128)(2,1)S(1)}, u32[]{:S(2)}, u32[]{:S(2)}) %collective-permute-start.11) | collective-permute-done | bytes 184352 | tf_op jit(solution)/shard_map/ppermute | solution.py:30
  33.3 7.4 %collective-permute-done.10 = bf16[48,1920]{1,0:T(8,128)(2,1)S(1)} collective-permute-done((bf16[48,1920]{1,0:T(8,128)(2,1)S(1)}, bf16[48,1920]{1,0:T(8,128)(2,1)S(1)}, u32[]{:S(2)}, u32[]{:S(2)}) %collective-permute-start.10) | collective-permute-done | bytes 184352 | tf_op jit(solution)/shard_map/ppermute | solution.py:30
  46.8 3.0 %collective-permute-start.17 = (bf16[192,384]{1,0:T(8,128)(2,1)S(1)}, bf16[192,384]{1,0:T(8,128)(2,1)S(1)}, u32[]{:S(2)}, u32[]{:S(2)}) collective-permute-start(bf16[192,384]{1,0:T(8,128)(2,1)S(1)} %maximum_select_fusion.1.refs_0_), channel_id=1, source_target_pairs={{0,8},{1,9},{2,10},{3,11},{4,12},{5,13},{6,14},{7,15},{8,0},{9,1},... | collective-permute-start | bytes 442376 | tf_op jit(solution)/shard_map/ppermute | solution.py:30
  49.8 10.5 %collective-permute-done.12 = bf16[4,48,1920]{2,1,0:T(8,128)(2,1)S(1)} collective-permute-done((bf16[4,48,1920]{2,1,0:T(8,128)(2,1)S(1)}, bf16[4,48,1920]{2,1,0:T(8,128)(2,1)S(1)}, u32[]{:S(2)}, u32[]{:S(2)}) %collective-permute-start.12) | collective-permute-done | bytes 737312 | tf_op jit(solution)/shard_map/ppermute | solution.py:30
  63.8 14.8 %collective-permute-done.20 = bf16[4,192,384]{2,1,0:T(8,128)(2,1)} collective-permute-done((bf16[4,192,384]{2,1,0:T(8,128)(2,1)S(1)}, bf16[4,192,384]{2,1,0:T(8,128)(2,1)}, u32[]{:S(2)}, u32[]{:S(2)}) %collective-permute-start.20) | collective-permute-done | bytes 589856 | tf_op jit(solution)/shard_map/ppermute | solution.py:30
  81.6 4.6 %collective-permute-done.13.p1 = bf16[2,4,48,1920]{3,2,1,0:T(8,128)(2,1)S(1)} collective-permute-done((bf16[2,4,48,1920]{3,2,1,0:T(8,128)(2,1)S(1)}, bf16[2,4,48,1920]{3,2,1,0:T(8,128)(2,1)S(1)}, u32[]{:S(2)}, u32[]{:S(2)}) %collective-permute-start.13) | collective-permute-done | bytes 1474592 | tf_op jit(solution)/shard_map/ppermute | solution.py:30
  86.2 7.8 %start.1 = (bf16[768,2304]{1,0:T(8,128)(2,1)S(1)}, f32[16,768]{1,0:T(8,128)S(1)}, f32[1,3072]{1,0:T(1,128)S(1)}, f32[192,576]{1,0:T(8,128)S(1)}, bf16[192,768]{1...) custom-call(s32[2]{0:T(128)S(1)} %pad_add_fusion.place_ref, ...), custom_call_target="tpu_custom_call" | custom-call | flops 20000000000 | bytes 73400320 | tf_op jit(solution)/shard_map/start/pallas_call | solution.py:752
  94.1 4.8 %collective-permute-done.21.p1 = bf16[2,4,192,384]{3,2,1,0:T(8,128)(2,1)S(1)} collective-permute-done((bf16[2,4,192,384]{3,2,1,0:T(8,128)(2,1)S(1)}, bf16[2,4,192,384]{3,2,1,0:T(8,128)(2,1)S(1)}, u32[]{:S(2)}, u32[]{:S(2)}) %collective-permute-start.21) | collective-permute-done | bytes 1179680 | tf_op jit(solution)/shard_map/ppermute | solution.py:30
  98.9 5.1 %up.1 = (bf16[768,3072]{1,0:T(8,128)(2,1)S(1)}, bf16[768,768]{1,0:T(8,128)(2,1)S(1)}, f32[192,768]{1,0:T(8,128)S(1)}, bf16[192,768]{1,0:T(8,128)(2,1)S(1)}, bf16...) custom-call(s32[2]{0:T(128)S(1)} %pad_add_fusion.place_ref, ...), custom_call_target="tpu_custom_call" | custom-call | flops 12000000000 | bytes 41943040 | tf_op jit(solution)/shard_map/up/pallas_call | solution.py:752
  104.0 44.0 %main.1 = (bf16[192,768]{1,0:T(8,128)(2,1)}, f32[192,768]{1,0:T(8,128)S(1)}, f32[16,768]{1,0:T(8,128)S(1)}, bf16[384,768]{1,0:T(8,128)(2,1)S(1)}, bf16[384,768]{...) custom-call(s32[2]{0:T(128)S(1)} %pad_add_fusion.place_ref, ...), custom_call_target="tpu_custom_call" | custom-call | flops 36238786560 | bytes 62914560 | tf_op jit(solution)/shard_map/main/pallas_call | solution.py:752
  148.0 3.9 %give_down.1 = bf16[16,192,384]{2,1,0:T(8,128)(2,1)S(1)} custom-call(s32[2]{0:T(128)S(1)} %pad_add_fusion.place_ref, bf16[192,3072]{1,0:T(8,128)(2,1)S(1)} %get-tuple-element.88.active_0, bf16[384,3072]{1,0:T(8,128)(2,1)S(1)} %get-tuple-element.100.active, bf16[576,768]{1,0:T(8,128)(2,1)S(1)} %get-tuple-element.102.d_z), custom_call_target="tpu_custom_call" | custom-call | flops 10000000000 | bytes 36700160 | tf_op jit(solution)/shard_map/give_down/pallas_call | solution.py:752
  152.4 3.6 %keep_down.1 = bf16[16,192,384]{2,1,0:T(8,128)(2,1)S(1)} custom-call(s32[2]{0:T(128)S(1)} %pad_add_fusion.place_ref, bf16[192,3072]{1,0:T(8,128)(2,1)S(1)} %get-tuple-element.88.active_0, bf16[384,3072]{1,0:T(8,128)(2,1)S(1)} %get-tuple-element.100.active, bf16[576,768]{1,0:T(8,128)(2,1)S(1)} %get-tuple-element.102.d_z), custom_call_target="tpu_custom_call" | custom-call | flops 10000000000 | bytes 36700160 | tf_op jit(solution)/shard_map/keep_down/pallas_call | solution.py:752
  159.9 6.3 %give_up.1 = (bf16[16,48,1920]{2,1,0:T(8,128)(2,1)S(1)}, f32[192,768]{1,0:T(8,128)S(1)}, f32[16,768]{1,0:T(8,128)S(1)}, bf16[192,768]{1,0:T(8,128)(2,1)S(1)}, bf16[192,768]{1,0:T(8,128)(2,1)S(1)}) custom-call(s32[2]{0:T(128)S(1)} %pad_add_fusion.place_ref, f32[16,768]{1,0:T(8,128)S(1)} %get-tuple-element.76.vec, ...), custom_call_target="tpu_custom_call" | custom-call | flops 10000000000 | bytes 36700160 | tf_op jit(solution)/shard_map/give_up/pallas_call | solution.py:752
  166.9 4.5 %keep_up.1 = (bf16[16,48,1920]{2,1,0:T(8,128)(2,1)S(1)}, f32[1,3072]{1,0:T(1,128)S(1)}) custom-call(s32[2]{0:T(128)S(1)} %pad_add_fusion.place_ref, bf16[192,768]{1,0:T(8,128)(2,1)S(1)} %get-tuple-element.95.x_mlp_0, bf16[384,768]{1,0:T(8,128)(2,1)S(1)} %get-tuple-element.96.x_mlp, bf16[192,3072]{1,0:T(8,128)(2,1)S(1)} %get-tuple-element.97.d_hidden_0, ...), custom_call_target="tpu_custom_call" | custom-call | flops 10000000000 | bytes 36700160 | tf_op jit(solution)/shard_map/keep_up/pallas_call | solution.py:752
  171.4 3.9 %collective-permute-done.25.got = bf16[2,4,192,384]{3,2,1,0:T(8,128)(2,1)S(1)} collective-permute-done((bf16[2,4,192,384]{3,2,1,0:T(8,128)(2,1)S(1)}, bf16[2,4,192,384]{3,2,1,0:T(8,128)(2,1)S(1)}, u32[]{:S(2)}, u32[]{:S(2)}) %collective-permute-start.25) | collective-permute-done | bytes 1179680 | tf_op jit(solution)/shard_map/ppermute | solution.py:30
  179.0 6.4 %last.1 = (bf16[192,768]{1,0:T(8,128)(2,1)}, bf16[192,2304]{1,0:T(8,128)(2,1)S(1)}, bf16[768,256]{1,0:T(8,128)(2,1)S(1)}) custom-call(s32[2]{0:T(128)S(1)} %pad_add_fusion.place_ref, f32[16,768]{1,0:T(8,128)S(1)} %get-tuple-element.76.vec, bf16[768,2304]{1,0:T(8,128)(2,1)S(1)} %copy-done.4, bf16[192,768]{1,0:T(8,128)(2,1)S(1)} %get-tuple-element.93.q, ...), custom_call_target="tpu_custom_call" | custom-call | flops 40000000000 | bytes 146800640 | tf_op jit(solution)/shard_map/last/pallas_call | solution.py:752
  185.4 6.5 %collective-permute-done.27 = bf16[4,192,384]{2,1,0:T(8,128)(2,1)S(1)} collective-permute-done((bf16[4,192,384]{2,1,0:T(8,128)(2,1)S(1)}, bf16[4,192,384]{2,1,0:T(8,128)(2,1)S(1)}, u32[]{:S(2)}, u32[]{:S(2)}) %collective-permute-start.27) | collective-permute-done | bytes 589856 | tf_op jit(solution)/shard_map/ppermute | solution.py:30
  191.8 2.5 give_qkv.1
  194.4 2.5 keep_qkv.1
  196.8 3.0 %collective-permute-done.35 = bf16[2,4,48,1920]{3,2,1,0:T(8,128)(2,1)S(1)} collective-permute-done((bf16[2,4,48,1920]{3,2,1,0:T(8,128)(2,1)S(1)}, bf16[2,4,48,1920]{3,2,1,0:T(8,128)(2,1)S(1)}, u32[]{:S(2)}, u32[]{:S(2)}) %collective-permute-start.35) | collective-permute-done | bytes 1474592 | tf_op jit(solution)/shard_map/ppermute | solution.py:30
  203.1 3.6 %collective-permute-start.37 = (bf16[192,384]{1,0:T(8,128)(2,1)S(1)}, bf16[192,384]{1,0:T(8,128)(2,1)S(1)}, u32[]{:S(2)}, u32[]{:S(2)}) collective-permute-start(bf16[192,384]{1,0:T(8,128)(2,1)S(1)} %get-tuple-element.221), channel_id=1, source_target_pairs={{0,8},{1,9},{2,10},{3,11},{4,12},{5,13},{6,14},{7,15},{8,0},{9,1},... | collective-permute-start | bytes 442376 | tf_op jit(solution)/shard_map/ppermute | solution.py:30
  207.0 3.9 %collective-permute-done.39 = bf16[192,384]{1,0:T(8,128)(2,1)S(1)} collective-permute-done((bf16[192,384]{1,0:T(8,128)(2,1)S(1)}, bf16[192,384]{1,0:T(8,128)(2,1)S(1)}, u32[]{:S(2)}, u32[]{:S(2)}) %collective-permute-start.39) | collective-permute-done | bytes 147488 | tf_op jit(solution)/shard_map/ppermute | solution.py:30
  210.9 5.8 %collective-permute-done.38 = bf16[192,384]{1,0:T(8,128)(2,1)S(1)} collective-permute-done((bf16[192,384]{1,0:T(8,128)(2,1)S(1)}, bf16[192,384]{1,0:T(8,128)(2,1)S(1)}, u32[]{:S(2)}, u32[]{:S(2)}) %collective-permute-start.38) | collective-permute-done | bytes 147488 | tf_op jit(solution)/shard_map/ppermute | solution.py:30
  223.6 3.6 %collective-permute-done.40 = bf16[48,1920]{1,0:T(8,128)(2,1)S(1)} collective-permute-done((bf16[48,1920]{1,0:T(8,128)(2,1)S(1)}, bf16[48,1920]{1,0:T(8,128)(2,1)S(1)}, u32[]{:S(2)}, u32[]{:S(2)}) %collective-permute-start.40) | collective-permute-done | bytes 184352 | tf_op jit(solution)/shard_map/ppermute | solution.py:30
  227.2 6.4 %collective-permute-done.41 = bf16[48,1920]{1,0:T(8,128)(2,1)S(1)} collective-permute-done((bf16[48,1920]{1,0:T(8,128)(2,1)S(1)}, bf16[48,1920]{1,0:T(8,128)(2,1)S(1)}, u32[]{:S(2)}, u32[]{:S(2)}) %collective-permute-start.41) | collective-permute-done | bytes 184352 | tf_op jit(solution)/shard_map/ppermute | solution.py:30
  233.9 4.1 %collective-permute-start.31 = (bf16[48,1280]{1,0:T(8,128)(2,1)S(1)}, bf16[48,1280]{1,0:T(8,128)(2,1)S(1)}, u32[]{:S(2)}, u32[]{:S(2)}) collective-permute-start(bf16[48,1280]{1,0:T(8,128)(2,1)S(1)} %get-tuple-element.222), channel_id=1, source_target_pairs={{0,8},{1,9},{2,10},{3,11},{4,12},{5,13},{6,14},{7,15},{8,0},{9,1},... | collective-permute-start | bytes 368648 | tf_op jit(solution)/shard_map/ppermute | solution.py:30
  242.0 4.6 %collective-permute-done.33 = bf16[48,1280]{1,0:T(8,128)(2,1)S(1)} collective-permute-done((bf16[48,1280]{1,0:T(8,128)(2,1)S(1)}, bf16[48,1280]{1,0:T(8,128)(2,1)S(1)}, u32[]{:S(2)}, u32[]{:S(2)}) %collective-permute-start.33) | collective-permute-done | bytes 122912 | tf_op jit(solution)/shard_map/ppermute | solution.py:30
  246.6 4.6 %collective-permute-done.32 = bf16[48,1280]{1,0:T(8,128)(2,1)S(1)} collective-permute-done((bf16[48,1280]{1,0:T(8,128)(2,1)S(1)}, bf16[48,1280]{1,0:T(8,128)(2,1)S(1)}, u32[]{:S(2)}, u32[]{:S(2)}) %collective-permute-start.32) | collective-permute-done | bytes 122912 | tf_op jit(solution)/shard_map/ppermute | solution.py:30
  (135 shorter events, 50.4 us)
Async XLA Ops:
  6.3 17.5 %collective-permute-start.8 = (bf16[24,1920]{1,0:T(8,128)(2,1)S(1)}, bf16[24,1920]{1,0:T(8,128)(2,1)S(1)}, u32[]{:S(2)}, u32[]{:S(2)}) collective-permute-start(bf16[24,1920]{1,0:T(8,128)(2,1)S(1)} %get-tuple-element.234), channel_id=1, source_target_pairs={{0,1},{1,0},{2,3},{3,2},{4,5},{5,4},{6,7},{7,6},{8,9},{9,8},{10,11... | collective-permute-start | bytes 276488 | tf_op jit(solution)/shard_map/ppermute | solution.py:30
  11.6 10.6 %collective-permute-start.2 = (bf16[48,1280]{1,0:T(8,128)(2,1)S(1)}, bf16[48,1280]{1,0:T(8,128)(2,1)S(1)}, u32[]{:S(2)}, u32[]{:S(2)}) collective-permute-start(bf16[48,1280]{1,0:T(8,128)(2,1)S(1)} %maximum_select_fusion.3), channel_id=1, source_target_pairs={{0,16},{1,17},{2,18},{3,19},{4,20},{5,21},{6,22},{7,23},{8,24},{9,... | collective-permute-start | bytes 368648 | tf_op jit(solution)/shard_map/ppermute | solution.py:30
  11.6 10.6 %collective-permute-start.1 = (bf16[48,1280]{1,0:T(8,128)(2,1)S(1)}, bf16[48,1280]{1,0:T(8,128)(2,1)S(1)}, u32[]{:S(2)}, u32[]{:S(2)}) collective-permute-start(bf16[48,1280]{1,0:T(8,128)(2,1)S(1)} %maximum_select_fusion.3), channel_id=1, source_target_pairs={{0,8},{1,9},{2,10},{3,11},{4,12},{5,13},{6,14},{7,15},{8,0},{9,1},... | collective-permute-start | bytes 368648 | tf_op jit(solution)/shard_map/ppermute | solution.py:30
  22.2 20.1 %collective-permute-start.4 = (bf16[4,48,1280]{2,1,0:T(8,128)(2,1)S(1)}, bf16[4,48,1280]{2,1,0:T(8,128)(2,1)S(1)}, u32[]{:S(2)}, u32[]{:S(2)}) collective-permute-start(bf16[4,48,1280]{2,1,0:T(8,128)(2,1)S(1)} %pad_maximum_fusion.3.refs_0_), channel_id=1, source_target_pairs={{0,4},{1,3},{2,6},{3,1},{4,0},{5,7},{6,2},{7,5},{8,12},{9,11},{10,... | collective-permute-start | bytes 1474568 | tf_op jit(solution)/shard_map/ppermute | solution.py:30
  26.4 14.4 %collective-permute-start.10 = (bf16[48,1920]{1,0:T(8,128)(2,1)S(1)}, bf16[48,1920]{1,0:T(8,128)(2,1)S(1)}, u32[]{:S(2)}, u32[]{:S(2)}) collective-permute-start(bf16[48,1920]{1,0:T(8,128)(2,1)S(1)} %maximum_select_fusion), channel_id=1, source_target_pairs={{0,16},{1,17},{2,18},{3,19},{4,20},{5,21},{6,22},{7,23},{8,24},{9,... | collective-permute-start | bytes 552968 | tf_op jit(solution)/shard_map/ppermute | solution.py:30
  26.4 14.4 %collective-permute-start.9 = (bf16[48,1920]{1,0:T(8,128)(2,1)S(1)}, bf16[48,1920]{1,0:T(8,128)(2,1)S(1)}, u32[]{:S(2)}, u32[]{:S(2)}) collective-permute-start(bf16[48,1920]{1,0:T(8,128)(2,1)S(1)} %maximum_select_fusion), channel_id=1, source_target_pairs={{0,8},{1,9},{2,10},{3,11},{4,12},{5,13},{6,14},{7,15},{8,0},{9,1},... | collective-permute-start | bytes 552968 | tf_op jit(solution)/shard_map/ppermute | solution.py:30
  40.9 19.4 %collective-permute-start.12 = (bf16[4,48,1920]{2,1,0:T(8,128)(2,1)S(1)}, bf16[4,48,1920]{2,1,0:T(8,128)(2,1)S(1)}, u32[]{:S(2)}, u32[]{:S(2)}) collective-permute-start(bf16[4,48,1920]{2,1,0:T(8,128)(2,1)S(1)} %get-tuple-element.226), channel_id=1, source_target_pairs={{0,4},{1,3},{2,6},{3,1},{4,0},{5,7},{6,2},{7,5},{8,12},{9,11},{10,... | collective-permute-start | bytes 2211848 | tf_op jit(solution)/shard_map/ppermute | solution.py:30
  43.4 18.0 %collective-permute-start.5 = (bf16[2,4,48,1280]{3,2,1,0:T(8,128)(2,1)}, bf16[2,4,48,1280]{3,2,1,0:T(8,128)(2,1)}, u32[]{:S(2)}, u32[]{:S(2)}) collective-permute-start(bf16[2,4,48,1280]{3,2,1,0:T(8,128)(2,1)} %stack.111.p0), channel_id=1, source_target_pairs={{0,2},{1,5},{2,0},{3,7},{4,6},{5,1},{6,4},{7,3},{8,10},{9,13},{10,... | collective-permute-start | bytes 2949128 | tf_op jit(solution)/shard_map/ppermute | solution.py:30
  45.4 15.1 %collective-permute-start.19 = (bf16[192,384]{1,0:T(8,128)(2,1)S(1)}, bf16[192,384]{1,0:T(8,128)(2,1)S(1)}, u32[]{:S(2)}, u32[]{:S(2)}) collective-permute-start(bf16[192,384]{1,0:T(8,128)(2,1)S(1)} %maximum_select_fusion.1.refs_0_), channel_id=1, source_target_pairs={{0,24},{1,25},{2,26},{3,27},{4,28},{5,29},{6,30},{7,31},{8,16},{9,... | collective-permute-start | bytes 442376 | tf_op jit(solution)/shard_map/ppermute | solution.py:30
  46.8 15.3 %collective-permute-start.18 = (bf16[192,384]{1,0:T(8,128)(2,1)S(1)}, bf16[192,384]{1,0:T(8,128)(2,1)S(1)}, u32[]{:S(2)}, u32[]{:S(2)}) collective-permute-start(bf16[192,384]{1,0:T(8,128)(2,1)S(1)} %maximum_select_fusion.1.refs_0_), channel_id=1, source_target_pairs={{0,16},{1,17},{2,18},{3,19},{4,20},{5,21},{6,22},{7,23},{8,24},{9,... | collective-permute-start | bytes 442376 | tf_op jit(solution)/shard_map/ppermute | solution.py:30
  46.8 15.3 %collective-permute-start.17 = (bf16[192,384]{1,0:T(8,128)(2,1)S(1)}, bf16[192,384]{1,0:T(8,128)(2,1)S(1)}, u32[]{:S(2)}, u32[]{:S(2)}) collective-permute-start(bf16[192,384]{1,0:T(8,128)(2,1)S(1)} %maximum_select_fusion.1.refs_0_), channel_id=1, source_target_pairs={{0,8},{1,9},{2,10},{3,11},{4,12},{5,13},{6,14},{7,15},{8,0},{9,1},... | collective-permute-start | bytes 442376 | tf_op jit(solution)/shard_map/ppermute | solution.py:30
  60.3 21.1 %collective-permute-start.6 = (bf16[2,4,48,1280]{3,2,1,0:T(8,128)(2,1)}, bf16[2,4,48,1280]{3,2,1,0:T(8,128)(2,1)}, u32[]{:S(2)}, u32[]{:S(2)}) collective-permute-start(bf16[2,4,48,1280]{3,2,1,0:T(8,128)(2,1)} %stack.111.p0), channel_id=1, source_target_pairs={{0,1},{1,0},{2,3},{3,2},{4,5},{5,4},{6,7},{7,6},{8,9},{9,8},{10,11... | collective-permute-start | bytes 2949128 | tf_op jit(solution)/shard_map/ppermute | solution.py:30
  60.5 25.7 %collective-permute-start.13 = (bf16[2,4,48,1920]{3,2,1,0:T(8,128)(2,1)S(1)}, bf16[2,4,48,1920]{3,2,1,0:T(8,128)(2,1)S(1)}, u32[]{:S(2)}, u32[]{:S(2)}) collective-permute-start(bf16[2,4,48,1920]{3,2,1,0:T(8,128)(2,1)S(1)} %pad_maximum_fusion.p0), channel_id=1, source_target_pairs={{0,2},{1,5},{2,0},{3,7},{4,6},{5,1},{6,4},{7,3},{8,10},{9,13},{10,... | collective-permute-start | bytes 4423688 | tf_op jit(solution)/shard_map/ppermute | solution.py:30
  61.3 24.9 %collective-permute-start.7 = (bf16[2,4,48,1280]{3,2,1,0:T(8,128)(2,1)}, bf16[2,4,48,1280]{3,2,1,0:T(8,128)(2,1)}, u32[]{:S(2)}, u32[]{:S(2)}) collective-permute-start(bf16[2,4,48,1280]{3,2,1,0:T(8,128)(2,1)} %collective-permute-done.5.p1), channel_id=1, source_target_pairs={{0,1},{1,0},{2,3},{3,2},{4,5},{5,4},{6,7},{7,6},{8,9},{9,8},{10,11... | collective-permute-start | bytes 2949128 | tf_op jit(solution)/shard_map/ppermute | solution.py:30
  62.2 16.4 %collective-permute-start.20 = (bf16[4,192,384]{2,1,0:T(8,128)(2,1)S(1)}, bf16[4,192,384]{2,1,0:T(8,128)(2,1)}, u32[]{:S(2)}, u32[]{:S(2)}) collective-permute-start(bf16[4,192,384]{2,1,0:T(8,128)(2,1)S(1)} %stack.112), channel_id=1, source_target_pairs={{0,4},{1,3},{2,6},{3,1},{4,0},{5,7},{6,2},{7,5},{8,12},{9,11},{10,... | collective-permute-start | bytes 1769480 | tf_op jit(solution)/shard_map/ppermute | solution.py:30
  79.8 24.2 %collective-permute-start.22 = (bf16[2,4,192,384]{3,2,1,0:T(8,128)(2,1)S(1)}, bf16[2,4,192,384]{3,2,1,0:T(8,128)(2,1)S(1)}, u32[]{:S(2)}, u32[]{:S(2)}) collective-permute-start(bf16[2,4,192,384]{3,2,1,0:T(8,128)(2,1)S(1)} %pad_maximum_fusion.1.p0), channel_id=1, source_target_pairs={{0,1},{1,0},{2,3},{3,2},{4,5},{5,4},{6,7},{7,6},{8,9},{9,8},{10,11... | collective-permute-start | bytes 3538952 | tf_op jit(solution)/shard_map/ppermute | solution.py:30
  79.9 19.0 %collective-permute-start.21 = (bf16[2,4,192,384]{3,2,1,0:T(8,128)(2,1)S(1)}, bf16[2,4,192,384]{3,2,1,0:T(8,128)(2,1)S(1)}, u32[]{:S(2)}, u32[]{:S(2)}) collective-permute-start(bf16[2,4,192,384]{3,2,1,0:T(8,128)(2,1)S(1)} %pad_maximum_fusion.1.p0), channel_id=1, source_target_pairs={{0,2},{1,5},{2,0},{3,7},{4,6},{5,1},{6,4},{7,3},{8,10},{9,13},{10,... | collective-permute-start | bytes 3538952 | tf_op jit(solution)/shard_map/ppermute | solution.py:30
  81.4 17.4 %collective-permute-start.14 = (bf16[2,4,48,1920]{3,2,1,0:T(8,128)(2,1)S(1)}, bf16[2,4,48,1920]{3,2,1,0:T(8,128)(2,1)S(1)}, u32[]{:S(2)}, u32[]{:S(2)}) collective-permute-start(bf16[2,4,48,1920]{3,2,1,0:T(8,128)(2,1)S(1)} %pad_maximum_fusion.p0), channel_id=1, source_target_pairs={{0,1},{1,0},{2,3},{3,2},{4,5},{5,4},{6,7},{7,6},{8,9},{9,8},{10,11... | collective-permute-start | bytes 4423688 | tf_op jit(solution)/shard_map/ppermute | solution.py:30
  86.2 12.6 %collective-permute-start.15 = (bf16[2,4,48,1920]{3,2,1,0:T(8,128)(2,1)S(1)}, bf16[2,4,48,1920]{3,2,1,0:T(8,128)(2,1)S(1)}, u32[]{:S(2)}, u32[]{:S(2)}) collective-permute-start(bf16[2,4,48,1920]{3,2,1,0:T(8,128)(2,1)S(1)} %collective-permute-done.13.p1), channel_id=1, source_target_pairs={{0,1},{1,0},{2,3},{3,2},{4,5},{5,4},{6,7},{7,6},{8,9},{9,8},{10,11... | collective-permute-start | bytes 4423688 | tf_op jit(solution)/shard_map/ppermute | solution.py:30
  159.0 16.3 %collective-permute-start.25 = (bf16[2,4,192,384]{3,2,1,0:T(8,128)(2,1)S(1)}, bf16[2,4,192,384]{3,2,1,0:T(8,128)(2,1)S(1)}, u32[]{:S(2)}, u32[]{:S(2)}) collective-permute-start(bf16[2,4,192,384]{3,2,1,0:T(8,128)(2,1)S(1)} %bitcast.120), channel_id=1, source_target_pairs={{0,2},{1,5},{2,0},{3,7},{4,6},{5,1},{6,4},{7,3},{8,10},{9,13},{10,... | collective-permute-start | bytes 3538952 | tf_op jit(solution)/shard_map/ppermute | solution.py:30
  166.2 10.8 %collective-permute-start.26 = (bf16[16,48,1920]{2,1,0:T(8,128)(2,1)S(1)}, bf16[16,48,1920]{2,1,0:T(8,128)(2,1)S(1)}, u32[]{:S(2)}, u32[]{:S(2)}) collective-permute-start(bf16[16,48,1920]{2,1,0:T(8,128)(2,1)S(1)} %get-tuple-element.114), channel_id=1, source_target_pairs={{0,1},{1,0},{2,3},{3,2},{4,5},{5,4},{6,7},{7,6},{8,9},{9,8},{10,11... | collective-permute-start | bytes 8847368 | tf_op jit(solution)/shard_map/ppermute | solution.py:30
  175.6 16.3 %collective-permute-start.27 = (bf16[4,192,384]{2,1,0:T(8,128)(2,1)S(1)}, bf16[4,192,384]{2,1,0:T(8,128)(2,1)S(1)}, u32[]{:S(2)}, u32[]{:S(2)}) collective-permute-start(bf16[4,192,384]{2,1,0:T(8,128)(2,1)S(1)} %get-tuple-element.125), channel_id=1, source_target_pairs={{0,4},{1,3},{2,6},{3,1},{4,0},{5,7},{6,2},{7,5},{8,12},{9,11},{10,... | collective-permute-start | bytes 1769480 | tf_op jit(solution)/shard_map/ppermute | solution.py:30
  177.6 22.2 %collective-permute-start.35 = (bf16[2,4,48,1920]{3,2,1,0:T(8,128)(2,1)S(1)}, bf16[2,4,48,1920]{3,2,1,0:T(8,128)(2,1)S(1)}, u32[]{:S(2)}, u32[]{:S(2)}) collective-permute-start(bf16[2,4,48,1920]{3,2,1,0:T(8,128)(2,1)S(1)} %bitcast.117), channel_id=1, source_target_pairs={{0,2},{1,5},{2,0},{3,7},{4,6},{5,1},{6,4},{7,3},{8,10},{9,13},{10,... | collective-permute-start | bytes 4423688 | tf_op jit(solution)/shard_map/ppermute | solution.py:30
  200.2 16.6 %collective-permute-start.36 = (bf16[4,48,1920]{2,1,0:T(8,128)(2,1)S(1)}, bf16[4,48,1920]{2,1,0:T(8,128)(2,1)S(1)}, u32[]{:S(2)}, u32[]{:S(2)}) collective-permute-start(bf16[4,48,1920]{2,1,0:T(8,128)(2,1)S(1)} %get-tuple-element.213), channel_id=1, source_target_pairs={{0,4},{1,3},{2,6},{3,1},{4,0},{5,7},{6,2},{7,5},{8,12},{9,11},{10,... | collective-permute-start | bytes 2211848 | tf_op jit(solution)/shard_map/ppermute | solution.py:30
  203.1 13.6 %collective-permute-start.38 = (bf16[192,384]{1,0:T(8,128)(2,1)S(1)}, bf16[192,384]{1,0:T(8,128)(2,1)S(1)}, u32[]{:S(2)}, u32[]{:S(2)}) collective-permute-start(bf16[192,384]{1,0:T(8,128)(2,1)S(1)} %get-tuple-element.220), channel_id=1, source_target_pairs={{0,16},{1,17},{2,18},{3,19},{4,20},{5,21},{6,22},{7,23},{8,24},{9,... | collective-permute-start | bytes 442376 | tf_op jit(solution)/shard_map/ppermute | solution.py:30
  203.1 13.6 %collective-permute-start.37 = (bf16[192,384]{1,0:T(8,128)(2,1)S(1)}, bf16[192,384]{1,0:T(8,128)(2,1)S(1)}, u32[]{:S(2)}, u32[]{:S(2)}) collective-permute-start(bf16[192,384]{1,0:T(8,128)(2,1)S(1)} %get-tuple-element.221), channel_id=1, source_target_pairs={{0,8},{1,9},{2,10},{3,11},{4,12},{5,13},{6,14},{7,15},{8,0},{9,1},... | collective-permute-start | bytes 442376 | tf_op jit(solution)/shard_map/ppermute | solution.py:30
  206.7 15.7 %collective-permute-start.29 = (bf16[2,4,48,1280]{3,2,1,0:T(8,128)(2,1)S(1)}, bf16[2,4,48,1280]{3,2,1,0:T(8,128)(2,1)S(1)}, u32[]{:S(2)}, u32[]{:S(2)}) collective-permute-start(bf16[2,4,48,1280]{3,2,1,0:T(8,128)(2,1)S(1)} %bitcast.121), channel_id=1, source_target_pairs={{0,2},{1,5},{2,0},{3,7},{4,6},{5,1},{6,4},{7,3},{8,10},{9,13},{10,... | collective-permute-start | bytes 2949128 | tf_op jit(solution)/shard_map/ppermute | solution.py:30
  217.1 10.1 %collective-permute-start.40 = (bf16[48,1920]{1,0:T(8,128)(2,1)S(1)}, bf16[48,1920]{1,0:T(8,128)(2,1)S(1)}, u32[]{:S(2)}, u32[]{:S(2)}) collective-permute-start(bf16[48,1920]{1,0:T(8,128)(2,1)S(1)} %get-tuple-element.132), channel_id=1, source_target_pairs={{0,8},{1,9},{2,10},{3,11},{4,12},{5,13},{6,14},{7,15},{8,0},{9,1},... | collective-permute-start | bytes 552968 | tf_op jit(solution)/shard_map/ppermute | solution.py:30
  217.2 16.4 %collective-permute-start.41 = (bf16[48,1920]{1,0:T(8,128)(2,1)S(1)}, bf16[48,1920]{1,0:T(8,128)(2,1)S(1)}, u32[]{:S(2)}, u32[]{:S(2)}) collective-permute-start(bf16[48,1920]{1,0:T(8,128)(2,1)S(1)} %get-tuple-element.133), channel_id=1, source_target_pairs={{0,16},{1,17},{2,18},{3,19},{4,20},{5,21},{6,22},{7,23},{8,24},{9,... | collective-permute-start | bytes 552968 | tf_op jit(solution)/shard_map/ppermute | solution.py:30
  219.5 14.1 %collective-permute-start.42 = (bf16[48,1920]{1,0:T(8,128)(2,1)S(1)}, bf16[48,1920]{1,0:T(8,128)(2,1)S(1)}, u32[]{:S(2)}, u32[]{:S(2)}) collective-permute-start(bf16[48,1920]{1,0:T(8,128)(2,1)S(1)} %get-tuple-element.134), channel_id=1, source_target_pairs={{0,24},{1,25},{2,26},{3,27},{4,28},{5,29},{6,30},{7,31},{8,16},{9,... | collective-permute-start | bytes 552968 | tf_op jit(solution)/shard_map/ppermute | solution.py:30
  222.7 11.1 %collective-permute-start.30 = (bf16[4,48,1280]{2,1,0:T(8,128)(2,1)S(1)}, bf16[4,48,1280]{2,1,0:T(8,128)(2,1)S(1)}, u32[]{:S(2)}, u32[]{:S(2)}) collective-permute-start(bf16[4,48,1280]{2,1,0:T(8,128)(2,1)S(1)} %get-tuple-element.215), channel_id=1, source_target_pairs={{0,4},{1,3},{2,6},{3,1},{4,0},{5,7},{6,2},{7,5},{8,12},{9,11},{10,... | collective-permute-start | bytes 1474568 | tf_op jit(solution)/shard_map/ppermute | solution.py:30
  239.8 11.4 %collective-permute-start.32 = (bf16[48,1280]{1,0:T(8,128)(2,1)S(1)}, bf16[48,1280]{1,0:T(8,128)(2,1)S(1)}, u32[]{:S(2)}, u32[]{:S(2)}) collective-permute-start(bf16[48,1280]{1,0:T(8,128)(2,1)S(1)} %get-tuple-element.224), channel_id=1, source_target_pairs={{0,16},{1,17},{2,18},{3,19},{4,20},{5,21},{6,22},{7,23},{8,24},{9,... | collective-permute-start | bytes 368648 | tf_op jit(solution)/shard_map/ppermute | solution.py:30
  (19 other events, 144.2 us)

commit v4 on v3

--- a/solution.py
+++ b/solution.py
@@ -532,7 +532,7 @@
     def pair(j, _):
         attend(j, q, k, v, probs, scores, mask, context, 0, length)
 
-    lax.fori_loop(0, width // PAIR, pair, None, unroll=2)
+    lax.fori_loop(0, width // PAIR, pair, None, unroll=3)
 
 
 def up_kernel(
@@ -586,7 +586,7 @@
         def pair(j, _):
             attend(j, q, k_all, v_all, probs[r], scores, mask, context, at, seen)
 
-        lax.fori_loop(0, pair_count, pair, None, unroll=2)
+        lax.fori_loop(0, pair_count, pair, None, unroll=3)
         project_out(context, at, length, w_out, vec, entry, middle)
         norm_forward(middle, at, length, vec, GAIN_MLP, SHIFT_MLP, x_mlp, at)
         feed_up(x_mlp, at, length, w_up, bias_up, active, d_hidden, at)
@@ -624,7 +624,7 @@
                 r == PASSES - 1,
             )
 
-        lax.fori_loop(0, pair_count, pair_back, None, unroll=2)
+        lax.fori_loop(0, pair_count, pair_back, None, unroll=3)
         for b in range(0, length, 64):
             part = slice(at + b, at + b + 64)
             made = slice(r * length + b, r * length + b + 64)
@@ -707,7 +707,7 @@
             j, q, k, v, probs, scores, d_scores, d_context, context_0, 0, length, d_mixed_0, k_grad, v_grad, False
         )
 
-    lax.fori_loop(0, width // PAIR, pair_back, None, unroll=2)
+    lax.fori_loop(0, width // PAIR, pair_back, None, unroll=3)
     for b in range(0, length, 64):
         part = slice(b, b + 64)
         d_mixed_0[part, width : 2 * width] = (k_grad[part, :] * SCALE).astype(BF16)

time: 260 us -> 260 us (level)
  transfers between devices with their start and end apart: 45 -> 45, of which waited for: 21 -> 21; matrix products, arithmetic and copies ran while one was open for 3% -> 3% of each run, Pallas kernels for 16% -> 15%
where the time goes in v4:
time: 260 us; the launch traced here: 255 us
  waiting for transfers between devices  105 us (40%)
  Pallas kernels  86.8 us (33%)
  starting transfers between devices  45.5 us (18%)
  other arithmetic  8.89 us (3%)
  local copies, waits for them, and re-layouts  8.12 us (3%)
    ppermute x45, waiting for transfers between devices, send(): return lax.ppermute(x, AXES, route)  105 us
    pallas_call x10, Pallas kernels, call(): pl.pallas_call(kernel, out_shape=results, in_specs=[pl.BlockSpec(memory_s...  84.8 us
    ppermute x45, starting transfers between devices, send(): return lax.ppermute(x, AXES, route)  45.5 us
  transfers between devices with their start and end apart: 45, of which 21 were waited for; matrix products, arithmetic and copies ran while one was open for 3% of the time, Pallas kernels for 15%

profile of v4, /device:TPU:0, one launch (start us, length us, event | category | flops | bytes accessed | tf_op | source)
XLA Modules:
  0.0 255.4 jit_solution(11148212125716064993)
XLA Ops:
  6.4 5.1 %collective-permute-start.3 = (bf16[48,1280]{1,0:T(8,128)(2,1)S(1)}, bf16[48,1280]{1,0:T(8,128)(2,1)S(1)}, u32[]{:S(2)}, u32[]{:S(2)}) collective-permute-start(bf16[48,1280]{1,0:T(8,128)(2,1)S(1)} %maximum_select_fusion.3), channel_id=1, source_target_pairs={{0,24},{1,25},{2,26},{3,27},{4,28},{5,29},{6,30},{7,31},{8,16},{9,... | collective-permute-start | bytes 368648 | tf_op jit(solution)/shard_map/ppermute | solution.py:30
  12.2 3.6 %collective-permute-done.3 = bf16[48,1280]{1,0:T(8,128)(2,1)S(1)} collective-permute-done((bf16[48,1280]{1,0:T(8,128)(2,1)S(1)}, bf16[48,1280]{1,0:T(8,128)(2,1)S(1)}, u32[]{:S(2)}, u32[]{:S(2)}) %collective-permute-start.3) | collective-permute-done | bytes 122912 | tf_op jit(solution)/shard_map/ppermute | solution.py:30
  15.8 6.3 %collective-permute-done.2 = bf16[48,1280]{1,0:T(8,128)(2,1)S(1)} collective-permute-done((bf16[48,1280]{1,0:T(8,128)(2,1)S(1)}, bf16[48,1280]{1,0:T(8,128)(2,1)S(1)}, u32[]{:S(2)}, u32[]{:S(2)}) %collective-permute-start.2) | collective-permute-done | bytes 122912 | tf_op jit(solution)/shard_map/ppermute | solution.py:30
  23.8 2.5 collective-permute-start.11
  28.3 5.0 %collective-permute-done.11 = bf16[48,1920]{1,0:T(8,128)(2,1)S(1)} collective-permute-done((bf16[48,1920]{1,0:T(8,128)(2,1)S(1)}, bf16[48,1920]{1,0:T(8,128)(2,1)S(1)}, u32[]{:S(2)}, u32[]{:S(2)}) %collective-permute-start.11) | collective-permute-done | bytes 184352 | tf_op jit(solution)/shard_map/ppermute | solution.py:30
  33.3 7.4 %collective-permute-done.10 = bf16[48,1920]{1,0:T(8,128)(2,1)S(1)} collective-permute-done((bf16[48,1920]{1,0:T(8,128)(2,1)S(1)}, bf16[48,1920]{1,0:T(8,128)(2,1)S(1)}, u32[]{:S(2)}, u32[]{:S(2)}) %collective-permute-start.10) | collective-permute-done | bytes 184352 | tf_op jit(solution)/shard_map/ppermute | solution.py:30
  46.8 3.0 %collective-permute-start.17 = (bf16[192,384]{1,0:T(8,128)(2,1)S(1)}, bf16[192,384]{1,0:T(8,128)(2,1)S(1)}, u32[]{:S(2)}, u32[]{:S(2)}) collective-permute-start(bf16[192,384]{1,0:T(8,128)(2,1)S(1)} %maximum_select_fusion.1.refs_0_), channel_id=1, source_target_pairs={{0,8},{1,9},{2,10},{3,11},{4,12},{5,13},{6,14},{7,15},{8,0},{9,1},... | collective-permute-start | bytes 442376 | tf_op jit(solution)/shard_map/ppermute | solution.py:30
  49.8 10.5 %collective-permute-done.12 = bf16[4,48,1920]{2,1,0:T(8,128)(2,1)S(1)} collective-permute-done((bf16[4,48,1920]{2,1,0:T(8,128)(2,1)S(1)}, bf16[4,48,1920]{2,1,0:T(8,128)(2,1)S(1)}, u32[]{:S(2)}, u32[]{:S(2)}) %collective-permute-start.12) | collective-permute-done | bytes 737312 | tf_op jit(solution)/shard_map/ppermute | solution.py:30
  63.8 14.8 %collective-permute-done.20 = bf16[4,192,384]{2,1,0:T(8,128)(2,1)} collective-permute-done((bf16[4,192,384]{2,1,0:T(8,128)(2,1)S(1)}, bf16[4,192,384]{2,1,0:T(8,128)(2,1)}, u32[]{:S(2)}, u32[]{:S(2)}) %collective-permute-start.20) | collective-permute-done | bytes 589856 | tf_op jit(solution)/shard_map/ppermute | solution.py:30
  81.6 4.6 %collective-permute-done.13.p1 = bf16[2,4,48,1920]{3,2,1,0:T(8,128)(2,1)S(1)} collective-permute-done((bf16[2,4,48,1920]{3,2,1,0:T(8,128)(2,1)S(1)}, bf16[2,4,48,1920]{3,2,1,0:T(8,128)(2,1)S(1)}, u32[]{:S(2)}, u32[]{:S(2)}) %collective-permute-start.13) | collective-permute-done | bytes 1474592 | tf_op jit(solution)/shard_map/ppermute | solution.py:30
  86.2 6.9 %start.1 = (bf16[768,2304]{1,0:T(8,128)(2,1)S(1)}, f32[16,768]{1,0:T(8,128)S(1)}, f32[1,3072]{1,0:T(1,128)S(1)}, f32[192,576]{1,0:T(8,128)S(1)}, bf16[192,768]{1...) custom-call(s32[2]{0:T(128)S(1)} %pad_add_fusion.place_ref, ...), custom_call_target="tpu_custom_call" | custom-call | flops 20000000000 | bytes 73400320 | tf_op jit(solution)/shard_map/start/pallas_call | solution.py:752
  93.1 5.7 %collective-permute-done.21.p1 = bf16[2,4,192,384]{3,2,1,0:T(8,128)(2,1)S(1)} collective-permute-done((bf16[2,4,192,384]{3,2,1,0:T(8,128)(2,1)S(1)}, bf16[2,4,192,384]{3,2,1,0:T(8,128)(2,1)S(1)}, u32[]{:S(2)}, u32[]{:S(2)}) %collective-permute-start.21) | collective-permute-done | bytes 1179680 | tf_op jit(solution)/shard_map/ppermute | solution.py:30
  98.9 5.1 %up.1 = (bf16[768,3072]{1,0:T(8,128)(2,1)S(1)}, bf16[768,768]{1,0:T(8,128)(2,1)S(1)}, f32[192,768]{1,0:T(8,128)S(1)}, bf16[192,768]{1,0:T(8,128)(2,1)S(1)}, bf16...) custom-call(s32[2]{0:T(128)S(1)} %pad_add_fusion.place_ref, ...), custom_call_target="tpu_custom_call" | custom-call | flops 12000000000 | bytes 41943040 | tf_op jit(solution)/shard_map/up/pallas_call | solution.py:752
  104.0 43.7 %main.1 = (bf16[192,768]{1,0:T(8,128)(2,1)}, f32[192,768]{1,0:T(8,128)S(1)}, f32[16,768]{1,0:T(8,128)S(1)}, bf16[384,768]{1,0:T(8,128)(2,1)S(1)}, bf16[384,768]{...) custom-call(s32[2]{0:T(128)S(1)} %pad_add_fusion.place_ref, ...), custom_call_target="tpu_custom_call" | custom-call | flops 36238786560 | bytes 62914560 | tf_op jit(solution)/shard_map/main/pallas_call | solution.py:752
  147.7 3.7 %give_down.1 = bf16[16,192,384]{2,1,0:T(8,128)(2,1)S(1)} custom-call(s32[2]{0:T(128)S(1)} %pad_add_fusion.place_ref, bf16[192,3072]{1,0:T(8,128)(2,1)S(1)} %get-tuple-element.88.active_0, bf16[384,3072]{1,0:T(8,128)(2,1)S(1)} %get-tuple-element.100.active, bf16[576,768]{1,0:T(8,128)(2,1)S(1)} %get-tuple-element.102.d_z), custom_call_target="tpu_custom_call" | custom-call | flops 10000000000 | bytes 36700160 | tf_op jit(solution)/shard_map/give_down/pallas_call | solution.py:752
  151.9 3.6 %keep_down.1 = bf16[16,192,384]{2,1,0:T(8,128)(2,1)S(1)} custom-call(s32[2]{0:T(128)S(1)} %pad_add_fusion.place_ref, bf16[192,3072]{1,0:T(8,128)(2,1)S(1)} %get-tuple-element.88.active_0, bf16[384,3072]{1,0:T(8,128)(2,1)S(1)} %get-tuple-element.100.active, bf16[576,768]{1,0:T(8,128)(2,1)S(1)} %get-tuple-element.102.d_z), custom_call_target="tpu_custom_call" | custom-call | flops 10000000000 | bytes 36700160 | tf_op jit(solution)/shard_map/keep_down/pallas_call | solution.py:752
  159.4 6.3 %give_up.1 = (bf16[16,48,1920]{2,1,0:T(8,128)(2,1)S(1)}, f32[192,768]{1,0:T(8,128)S(1)}, f32[16,768]{1,0:T(8,128)S(1)}, bf16[192,768]{1,0:T(8,128)(2,1)S(1)}, bf16[192,768]{1,0:T(8,128)(2,1)S(1)}) custom-call(s32[2]{0:T(128)S(1)} %pad_add_fusion.place_ref, f32[16,768]{1,0:T(8,128)S(1)} %get-tuple-element.76.vec, ...), custom_call_target="tpu_custom_call" | custom-call | flops 10000000000 | bytes 36700160 | tf_op jit(solution)/shard_map/give_up/pallas_call | solution.py:752
  166.3 4.5 %keep_up.1 = (bf16[16,48,1920]{2,1,0:T(8,128)(2,1)S(1)}, f32[1,3072]{1,0:T(1,128)S(1)}) custom-call(s32[2]{0:T(128)S(1)} %pad_add_fusion.place_ref, bf16[192,768]{1,0:T(8,128)(2,1)S(1)} %get-tuple-element.95.x_mlp_0, bf16[384,768]{1,0:T(8,128)(2,1)S(1)} %get-tuple-element.96.x_mlp, bf16[192,3072]{1,0:T(8,128)(2,1)S(1)} %get-tuple-element.97.d_hidden_0, ...), custom_call_target="tpu_custom_call" | custom-call | flops 10000000000 | bytes 36700160 | tf_op jit(solution)/shard_map/keep_up/pallas_call | solution.py:752
  170.9 3.9 %collective-permute-done.25.got = bf16[2,4,192,384]{3,2,1,0:T(8,128)(2,1)S(1)} collective-permute-done((bf16[2,4,192,384]{3,2,1,0:T(8,128)(2,1)S(1)}, bf16[2,4,192,384]{3,2,1,0:T(8,128)(2,1)S(1)}, u32[]{:S(2)}, u32[]{:S(2)}) %collective-permute-start.25) | collective-permute-done | bytes 1179680 | tf_op jit(solution)/shard_map/ppermute | solution.py:30
  178.5 6.1 %last.1 = (bf16[192,768]{1,0:T(8,128)(2,1)}, bf16[192,2304]{1,0:T(8,128)(2,1)S(1)}, bf16[768,256]{1,0:T(8,128)(2,1)S(1)}) custom-call(s32[2]{0:T(128)S(1)} %pad_add_fusion.place_ref, f32[16,768]{1,0:T(8,128)S(1)} %get-tuple-element.76.vec, bf16[768,2304]{1,0:T(8,128)(2,1)S(1)} %copy-done.4, bf16[192,768]{1,0:T(8,128)(2,1)S(1)} %get-tuple-element.93.q, ...), custom_call_target="tpu_custom_call" | custom-call | flops 40000000000 | bytes 146800640 | tf_op jit(solution)/shard_map/last/pallas_call | solution.py:752
  184.6 6.7 %collective-permute-done.27 = bf16[4,192,384]{2,1,0:T(8,128)(2,1)S(1)} collective-permute-done((bf16[4,192,384]{2,1,0:T(8,128)(2,1)S(1)}, bf16[4,192,384]{2,1,0:T(8,128)(2,1)S(1)}, u32[]{:S(2)}, u32[]{:S(2)}) %collective-permute-start.27) | collective-permute-done | bytes 589856 | tf_op jit(solution)/shard_map/ppermute | solution.py:30
  191.3 2.5 give_qkv.1
  193.9 2.5 keep_qkv.1
  196.3 3.0 %collective-permute-done.35 = bf16[2,4,48,1920]{3,2,1,0:T(8,128)(2,1)S(1)} collective-permute-done((bf16[2,4,48,1920]{3,2,1,0:T(8,128)(2,1)S(1)}, bf16[2,4,48,1920]{3,2,1,0:T(8,128)(2,1)S(1)}, u32[]{:S(2)}, u32[]{:S(2)}) %collective-permute-start.35) | collective-permute-done | bytes 1474592 | tf_op jit(solution)/shard_map/ppermute | solution.py:30
  202.6 3.6 %collective-permute-start.37 = (bf16[192,384]{1,0:T(8,128)(2,1)S(1)}, bf16[192,384]{1,0:T(8,128)(2,1)S(1)}, u32[]{:S(2)}, u32[]{:S(2)}) collective-permute-start(bf16[192,384]{1,0:T(8,128)(2,1)S(1)} %get-tuple-element.221), channel_id=1, source_target_pairs={{0,8},{1,9},{2,10},{3,11},{4,12},{5,13},{6,14},{7,15},{8,0},{9,1},... | collective-permute-start | bytes 442376 | tf_op jit(solution)/shard_map/ppermute | solution.py:30
  206.5 3.9 %collective-permute-done.39 = bf16[192,384]{1,0:T(8,128)(2,1)S(1)} collective-permute-done((bf16[192,384]{1,0:T(8,128)(2,1)S(1)}, bf16[192,384]{1,0:T(8,128)(2,1)S(1)}, u32[]{:S(2)}, u32[]{:S(2)}) %collective-permute-start.39) | collective-permute-done | bytes 147488 | tf_op jit(solution)/shard_map/ppermute | solution.py:30
  210.4 5.8 %collective-permute-done.38 = bf16[192,384]{1,0:T(8,128)(2,1)S(1)} collective-permute-done((bf16[192,384]{1,0:T(8,128)(2,1)S(1)}, bf16[192,384]{1,0:T(8,128)(2,1)S(1)}, u32[]{:S(2)}, u32[]{:S(2)}) %collective-permute-start.38) | collective-permute-done | bytes 147488 | tf_op jit(solution)/shard_map/ppermute | solution.py:30
  223.1 3.6 %collective-permute-done.40 = bf16[48,1920]{1,0:T(8,128)(2,1)S(1)} collective-permute-done((bf16[48,1920]{1,0:T(8,128)(2,1)S(1)}, bf16[48,1920]{1,0:T(8,128)(2,1)S(1)}, u32[]{:S(2)}, u32[]{:S(2)}) %collective-permute-start.40) | collective-permute-done | bytes 184352 | tf_op jit(solution)/shard_map/ppermute | solution.py:30
  226.7 6.4 %collective-permute-done.41 = bf16[48,1920]{1,0:T(8,128)(2,1)S(1)} collective-permute-done((bf16[48,1920]{1,0:T(8,128)(2,1)S(1)}, bf16[48,1920]{1,0:T(8,128)(2,1)S(1)}, u32[]{:S(2)}, u32[]{:S(2)}) %collective-permute-start.41) | collective-permute-done | bytes 184352 | tf_op jit(solution)/shard_map/ppermute | solution.py:30
  233.4 4.1 %collective-permute-start.31 = (bf16[48,1280]{1,0:T(8,128)(2,1)S(1)}, bf16[48,1280]{1,0:T(8,128)(2,1)S(1)}, u32[]{:S(2)}, u32[]{:S(2)}) collective-permute-start(bf16[48,1280]{1,0:T(8,128)(2,1)S(1)} %get-tuple-element.222), channel_id=1, source_target_pairs={{0,8},{1,9},{2,10},{3,11},{4,12},{5,13},{6,14},{7,15},{8,0},{9,1},... | collective-permute-start | bytes 368648 | tf_op jit(solution)/shard_map/ppermute | solution.py:30
  241.5 4.6 %collective-permute-done.33 = bf16[48,1280]{1,0:T(8,128)(2,1)S(1)} collective-permute-done((bf16[48,1280]{1,0:T(8,128)(2,1)S(1)}, bf16[48,1280]{1,0:T(8,128)(2,1)S(1)}, u32[]{:S(2)}, u32[]{:S(2)}) %collective-permute-start.33) | collective-permute-done | bytes 122912 | tf_op jit(solution)/shard_map/ppermute | solution.py:30
  246.1 4.6 %collective-permute-done.32 = bf16[48,1280]{1,0:T(8,128)(2,1)S(1)} collective-permute-done((bf16[48,1280]{1,0:T(8,128)(2,1)S(1)}, bf16[48,1280]{1,0:T(8,128)(2,1)S(1)}, u32[]{:S(2)}, u32[]{:S(2)}) %collective-permute-start.32) | collective-permute-done | bytes 122912 | tf_op jit(solution)/shard_map/ppermute | solution.py:30
  (135 shorter events, 50.4 us)
Async XLA Ops:
  6.3 17.5 %collective-permute-start.8 = (bf16[24,1920]{1,0:T(8,128)(2,1)S(1)}, bf16[24,1920]{1,0:T(8,128)(2,1)S(1)}, u32[]{:S(2)}, u32[]{:S(2)}) collective-permute-start(bf16[24,1920]{1,0:T(8,128)(2,1)S(1)} %get-tuple-element.234), channel_id=1, source_target_pairs={{0,1},{1,0},{2,3},{3,2},{4,5},{5,4},{6,7},{7,6},{8,9},{9,8},{10,11... | collective-permute-start | bytes 276488 | tf_op jit(solution)/shard_map/ppermute | solution.py:30
  11.6 10.6 %collective-permute-start.2 = (bf16[48,1280]{1,0:T(8,128)(2,1)S(1)}, bf16[48,1280]{1,0:T(8,128)(2,1)S(1)}, u32[]{:S(2)}, u32[]{:S(2)}) collective-permute-start(bf16[48,1280]{1,0:T(8,128)(2,1)S(1)} %maximum_select_fusion.3), channel_id=1, source_target_pairs={{0,16},{1,17},{2,18},{3,19},{4,20},{5,21},{6,22},{7,23},{8,24},{9,... | collective-permute-start | bytes 368648 | tf_op jit(solution)/shard_map/ppermute | solution.py:30
  11.6 10.6 %collective-permute-start.1 = (bf16[48,1280]{1,0:T(8,128)(2,1)S(1)}, bf16[48,1280]{1,0:T(8,128)(2,1)S(1)}, u32[]{:S(2)}, u32[]{:S(2)}) collective-permute-start(bf16[48,1280]{1,0:T(8,128)(2,1)S(1)} %maximum_select_fusion.3), channel_id=1, source_target_pairs={{0,8},{1,9},{2,10},{3,11},{4,12},{5,13},{6,14},{7,15},{8,0},{9,1},... | collective-permute-start | bytes 368648 | tf_op jit(solution)/shard_map/ppermute | solution.py:30
  22.2 20.1 %collective-permute-start.4 = (bf16[4,48,1280]{2,1,0:T(8,128)(2,1)S(1)}, bf16[4,48,1280]{2,1,0:T(8,128)(2,1)S(1)}, u32[]{:S(2)}, u32[]{:S(2)}) collective-permute-start(bf16[4,48,1280]{2,1,0:T(8,128)(2,1)S(1)} %pad_maximum_fusion.3.refs_0_), channel_id=1, source_target_pairs={{0,4},{1,3},{2,6},{3,1},{4,0},{5,7},{6,2},{7,5},{8,12},{9,11},{10,... | collective-permute-start | bytes 1474568 | tf_op jit(solution)/shard_map/ppermute | solution.py:30
  26.4 14.4 %collective-permute-start.10 = (bf16[48,1920]{1,0:T(8,128)(2,1)S(1)}, bf16[48,1920]{1,0:T(8,128)(2,1)S(1)}, u32[]{:S(2)}, u32[]{:S(2)}) collective-permute-start(bf16[48,1920]{1,0:T(8,128)(2,1)S(1)} %maximum_select_fusion), channel_id=1, source_target_pairs={{0,16},{1,17},{2,18},{3,19},{4,20},{5,21},{6,22},{7,23},{8,24},{9,... | collective-permute-start | bytes 552968 | tf_op jit(solution)/shard_map/ppermute | solution.py:30
  26.4 14.4 %collective-permute-start.9 = (bf16[48,1920]{1,0:T(8,128)(2,1)S(1)}, bf16[48,1920]{1,0:T(8,128)(2,1)S(1)}, u32[]{:S(2)}, u32[]{:S(2)}) collective-permute-start(bf16[48,1920]{1,0:T(8,128)(2,1)S(1)} %maximum_select_fusion), channel_id=1, source_target_pairs={{0,8},{1,9},{2,10},{3,11},{4,12},{5,13},{6,14},{7,15},{8,0},{9,1},... | collective-permute-start | bytes 552968 | tf_op jit(solution)/shard_map/ppermute | solution.py:30
  40.9 19.4 %collective-permute-start.12 = (bf16[4,48,1920]{2,1,0:T(8,128)(2,1)S(1)}, bf16[4,48,1920]{2,1,0:T(8,128)(2,1)S(1)}, u32[]{:S(2)}, u32[]{:S(2)}) collective-permute-start(bf16[4,48,1920]{2,1,0:T(8,128)(2,1)S(1)} %get-tuple-element.226), channel_id=1, source_target_pairs={{0,4},{1,3},{2,6},{3,1},{4,0},{5,7},{6,2},{7,5},{8,12},{9,11},{10,... | collective-permute-start | bytes 2211848 | tf_op jit(solution)/shard_map/ppermute | solution.py:30
  43.4 18.0 %collective-permute-start.5 = (bf16[2,4,48,1280]{3,2,1,0:T(8,128)(2,1)}, bf16[2,4,48,1280]{3,2,1,0:T(8,128)(2,1)}, u32[]{:S(2)}, u32[]{:S(2)}) collective-permute-start(bf16[2,4,48,1280]{3,2,1,0:T(8,128)(2,1)} %stack.111.p0), channel_id=1, source_target_pairs={{0,2},{1,5},{2,0},{3,7},{4,6},{5,1},{6,4},{7,3},{8,10},{9,13},{10,... | collective-permute-start | bytes 2949128 | tf_op jit(solution)/shard_map/ppermute | solution.py:30
  45.4 15.1 %collective-permute-start.19 = (bf16[192,384]{1,0:T(8,128)(2,1)S(1)}, bf16[192,384]{1,0:T(8,128)(2,1)S(1)}, u32[]{:S(2)}, u32[]{:S(2)}) collective-permute-start(bf16[192,384]{1,0:T(8,128)(2,1)S(1)} %maximum_select_fusion.1.refs_0_), channel_id=1, source_target_pairs={{0,24},{1,25},{2,26},{3,27},{4,28},{5,29},{6,30},{7,31},{8,16},{9,... | collective-permute-start | bytes 442376 | tf_op jit(solution)/shard_map/ppermute | solution.py:30
  46.8 15.3 %collective-permute-start.18 = (bf16[192,384]{1,0:T(8,128)(2,1)S(1)}, bf16[192,384]{1,0:T(8,128)(2,1)S(1)}, u32[]{:S(2)}, u32[]{:S(2)}) collective-permute-start(bf16[192,384]{1,0:T(8,128)(2,1)S(1)} %maximum_select_fusion.1.refs_0_), channel_id=1, source_target_pairs={{0,16},{1,17},{2,18},{3,19},{4,20},{5,21},{6,22},{7,23},{8,24},{9,... | collective-permute-start | bytes 442376 | tf_op jit(solution)/shard_map/ppermute | solution.py:30
  46.8 15.3 %collective-permute-start.17 = (bf16[192,384]{1,0:T(8,128)(2,1)S(1)}, bf16[192,384]{1,0:T(8,128)(2,1)S(1)}, u32[]{:S(2)}, u32[]{:S(2)}) collective-permute-start(bf16[192,384]{1,0:T(8,128)(2,1)S(1)} %maximum_select_fusion.1.refs_0_), channel_id=1, source_target_pairs={{0,8},{1,9},{2,10},{3,11},{4,12},{5,13},{6,14},{7,15},{8,0},{9,1},... | collective-permute-start | bytes 442376 | tf_op jit(solution)/shard_map/ppermute | solution.py:30
  60.3 21.1 %collective-permute-start.6 = (bf16[2,4,48,1280]{3,2,1,0:T(8,128)(2,1)}, bf16[2,4,48,1280]{3,2,1,0:T(8,128)(2,1)}, u32[]{:S(2)}, u32[]{:S(2)}) collective-permute-start(bf16[2,4,48,1280]{3,2,1,0:T(8,128)(2,1)} %stack.111.p0), channel_id=1, source_target_pairs={{0,1},{1,0},{2,3},{3,2},{4,5},{5,4},{6,7},{7,6},{8,9},{9,8},{10,11... | collective-permute-start | bytes 2949128 | tf_op jit(solution)/shard_map/ppermute | solution.py:30
  60.5 25.7 %collective-permute-start.13 = (bf16[2,4,48,1920]{3,2,1,0:T(8,128)(2,1)S(1)}, bf16[2,4,48,1920]{3,2,1,0:T(8,128)(2,1)S(1)}, u32[]{:S(2)}, u32[]{:S(2)}) collective-permute-start(bf16[2,4,48,1920]{3,2,1,0:T(8,128)(2,1)S(1)} %pad_maximum_fusion.p0), channel_id=1, source_target_pairs={{0,2},{1,5},{2,0},{3,7},{4,6},{5,1},{6,4},{7,3},{8,10},{9,13},{10,... | collective-permute-start | bytes 4423688 | tf_op jit(solution)/shard_map/ppermute | solution.py:30
  61.3 24.9 %collective-permute-start.7 = (bf16[2,4,48,1280]{3,2,1,0:T(8,128)(2,1)}, bf16[2,4,48,1280]{3,2,1,0:T(8,128)(2,1)}, u32[]{:S(2)}, u32[]{:S(2)}) collective-permute-start(bf16[2,4,48,1280]{3,2,1,0:T(8,128)(2,1)} %collective-permute-done.5.p1), channel_id=1, source_target_pairs={{0,1},{1,0},{2,3},{3,2},{4,5},{5,4},{6,7},{7,6},{8,9},{9,8},{10,11... | collective-permute-start | bytes 2949128 | tf_op jit(solution)/shard_map/ppermute | solution.py:30
  62.2 16.4 %collective-permute-start.20 = (bf16[4,192,384]{2,1,0:T(8,128)(2,1)S(1)}, bf16[4,192,384]{2,1,0:T(8,128)(2,1)}, u32[]{:S(2)}, u32[]{:S(2)}) collective-permute-start(bf16[4,192,384]{2,1,0:T(8,128)(2,1)S(1)} %stack.112), channel_id=1, source_target_pairs={{0,4},{1,3},{2,6},{3,1},{4,0},{5,7},{6,2},{7,5},{8,12},{9,11},{10,... | collective-permute-start | bytes 1769480 | tf_op jit(solution)/shard_map/ppermute | solution.py:30
  79.8 24.2 %collective-permute-start.22 = (bf16[2,4,192,384]{3,2,1,0:T(8,128)(2,1)S(1)}, bf16[2,4,192,384]{3,2,1,0:T(8,128)(2,1)S(1)}, u32[]{:S(2)}, u32[]{:S(2)}) collective-permute-start(bf16[2,4,192,384]{3,2,1,0:T(8,128)(2,1)S(1)} %pad_maximum_fusion.1.p0), channel_id=1, source_target_pairs={{0,1},{1,0},{2,3},{3,2},{4,5},{5,4},{6,7},{7,6},{8,9},{9,8},{10,11... | collective-permute-start | bytes 3538952 | tf_op jit(solution)/shard_map/ppermute | solution.py:30
  79.9 19.0 %collective-permute-start.21 = (bf16[2,4,192,384]{3,2,1,0:T(8,128)(2,1)S(1)}, bf16[2,4,192,384]{3,2,1,0:T(8,128)(2,1)S(1)}, u32[]{:S(2)}, u32[]{:S(2)}) collective-permute-start(bf16[2,4,192,384]{3,2,1,0:T(8,128)(2,1)S(1)} %pad_maximum_fusion.1.p0), channel_id=1, source_target_pairs={{0,2},{1,5},{2,0},{3,7},{4,6},{5,1},{6,4},{7,3},{8,10},{9,13},{10,... | collective-permute-start | bytes 3538952 | tf_op jit(solution)/shard_map/ppermute | solution.py:30
  81.4 17.4 %collective-permute-start.14 = (bf16[2,4,48,1920]{3,2,1,0:T(8,128)(2,1)S(1)}, bf16[2,4,48,1920]{3,2,1,0:T(8,128)(2,1)S(1)}, u32[]{:S(2)}, u32[]{:S(2)}) collective-permute-start(bf16[2,4,48,1920]{3,2,1,0:T(8,128)(2,1)S(1)} %pad_maximum_fusion.p0), channel_id=1, source_target_pairs={{0,1},{1,0},{2,3},{3,2},{4,5},{5,4},{6,7},{7,6},{8,9},{9,8},{10,11... | collective-permute-start | bytes 4423688 | tf_op jit(solution)/shard_map/ppermute | solution.py:30
  86.2 12.6 %collective-permute-start.15 = (bf16[2,4,48,1920]{3,2,1,0:T(8,128)(2,1)S(1)}, bf16[2,4,48,1920]{3,2,1,0:T(8,128)(2,1)S(1)}, u32[]{:S(2)}, u32[]{:S(2)}) collective-permute-start(bf16[2,4,48,1920]{3,2,1,0:T(8,128)(2,1)S(1)} %collective-permute-done.13.p1), channel_id=1, source_target_pairs={{0,1},{1,0},{2,3},{3,2},{4,5},{5,4},{6,7},{7,6},{8,9},{9,8},{10,11... | collective-permute-start | bytes 4423688 | tf_op jit(solution)/shard_map/ppermute | solution.py:30
  158.5 16.3 %collective-permute-start.25 = (bf16[2,4,192,384]{3,2,1,0:T(8,128)(2,1)S(1)}, bf16[2,4,192,384]{3,2,1,0:T(8,128)(2,1)S(1)}, u32[]{:S(2)}, u32[]{:S(2)}) collective-permute-start(bf16[2,4,192,384]{3,2,1,0:T(8,128)(2,1)S(1)} %bitcast.120), channel_id=1, source_target_pairs={{0,2},{1,5},{2,0},{3,7},{4,6},{5,1},{6,4},{7,3},{8,10},{9,13},{10,... | collective-permute-start | bytes 3538952 | tf_op jit(solution)/shard_map/ppermute | solution.py:30
  165.7 10.8 %collective-permute-start.26 = (bf16[16,48,1920]{2,1,0:T(8,128)(2,1)S(1)}, bf16[16,48,1920]{2,1,0:T(8,128)(2,1)S(1)}, u32[]{:S(2)}, u32[]{:S(2)}) collective-permute-start(bf16[16,48,1920]{2,1,0:T(8,128)(2,1)S(1)} %get-tuple-element.114), channel_id=1, source_target_pairs={{0,1},{1,0},{2,3},{3,2},{4,5},{5,4},{6,7},{7,6},{8,9},{9,8},{10,11... | collective-permute-start | bytes 8847368 | tf_op jit(solution)/shard_map/ppermute | solution.py:30
  175.0 16.3 %collective-permute-start.27 = (bf16[4,192,384]{2,1,0:T(8,128)(2,1)S(1)}, bf16[4,192,384]{2,1,0:T(8,128)(2,1)S(1)}, u32[]{:S(2)}, u32[]{:S(2)}) collective-permute-start(bf16[4,192,384]{2,1,0:T(8,128)(2,1)S(1)} %get-tuple-element.125), channel_id=1, source_target_pairs={{0,4},{1,3},{2,6},{3,1},{4,0},{5,7},{6,2},{7,5},{8,12},{9,11},{10,... | collective-permute-start | bytes 1769480 | tf_op jit(solution)/shard_map/ppermute | solution.py:30
  177.1 22.2 %collective-permute-start.35 = (bf16[2,4,48,1920]{3,2,1,0:T(8,128)(2,1)S(1)}, bf16[2,4,48,1920]{3,2,1,0:T(8,128)(2,1)S(1)}, u32[]{:S(2)}, u32[]{:S(2)}) collective-permute-start(bf16[2,4,48,1920]{3,2,1,0:T(8,128)(2,1)S(1)} %bitcast.117), channel_id=1, source_target_pairs={{0,2},{1,5},{2,0},{3,7},{4,6},{5,1},{6,4},{7,3},{8,10},{9,13},{10,... | collective-permute-start | bytes 4423688 | tf_op jit(solution)/shard_map/ppermute | solution.py:30
  199.7 16.6 %collective-permute-start.36 = (bf16[4,48,1920]{2,1,0:T(8,128)(2,1)S(1)}, bf16[4,48,1920]{2,1,0:T(8,128)(2,1)S(1)}, u32[]{:S(2)}, u32[]{:S(2)}) collective-permute-start(bf16[4,48,1920]{2,1,0:T(8,128)(2,1)S(1)} %get-tuple-element.213), channel_id=1, source_target_pairs={{0,4},{1,3},{2,6},{3,1},{4,0},{5,7},{6,2},{7,5},{8,12},{9,11},{10,... | collective-permute-start | bytes 2211848 | tf_op jit(solution)/shard_map/ppermute | solution.py:30
  202.6 13.6 %collective-permute-start.38 = (bf16[192,384]{1,0:T(8,128)(2,1)S(1)}, bf16[192,384]{1,0:T(8,128)(2,1)S(1)}, u32[]{:S(2)}, u32[]{:S(2)}) collective-permute-start(bf16[192,384]{1,0:T(8,128)(2,1)S(1)} %get-tuple-element.220), channel_id=1, source_target_pairs={{0,16},{1,17},{2,18},{3,19},{4,20},{5,21},{6,22},{7,23},{8,24},{9,... | collective-permute-start | bytes 442376 | tf_op jit(solution)/shard_map/ppermute | solution.py:30
  202.6 13.6 %collective-permute-start.37 = (bf16[192,384]{1,0:T(8,128)(2,1)S(1)}, bf16[192,384]{1,0:T(8,128)(2,1)S(1)}, u32[]{:S(2)}, u32[]{:S(2)}) collective-permute-start(bf16[192,384]{1,0:T(8,128)(2,1)S(1)} %get-tuple-element.221), channel_id=1, source_target_pairs={{0,8},{1,9},{2,10},{3,11},{4,12},{5,13},{6,14},{7,15},{8,0},{9,1},... | collective-permute-start | bytes 442376 | tf_op jit(solution)/shard_map/ppermute | solution.py:30
  206.2 15.7 %collective-permute-start.29 = (bf16[2,4,48,1280]{3,2,1,0:T(8,128)(2,1)S(1)}, bf16[2,4,48,1280]{3,2,1,0:T(8,128)(2,1)S(1)}, u32[]{:S(2)}, u32[]{:S(2)}) collective-permute-start(bf16[2,4,48,1280]{3,2,1,0:T(8,128)(2,1)S(1)} %bitcast.121), channel_id=1, source_target_pairs={{0,2},{1,5},{2,0},{3,7},{4,6},{5,1},{6,4},{7,3},{8,10},{9,13},{10,... | collective-permute-start | bytes 2949128 | tf_op jit(solution)/shard_map/ppermute | solution.py:30
  216.6 10.1 %collective-permute-start.40 = (bf16[48,1920]{1,0:T(8,128)(2,1)S(1)}, bf16[48,1920]{1,0:T(8,128)(2,1)S(1)}, u32[]{:S(2)}, u32[]{:S(2)}) collective-permute-start(bf16[48,1920]{1,0:T(8,128)(2,1)S(1)} %get-tuple-element.132), channel_id=1, source_target_pairs={{0,8},{1,9},{2,10},{3,11},{4,12},{5,13},{6,14},{7,15},{8,0},{9,1},... | collective-permute-start | bytes 552968 | tf_op jit(solution)/shard_map/ppermute | solution.py:30
  216.7 16.4 %collective-permute-start.41 = (bf16[48,1920]{1,0:T(8,128)(2,1)S(1)}, bf16[48,1920]{1,0:T(8,128)(2,1)S(1)}, u32[]{:S(2)}, u32[]{:S(2)}) collective-permute-start(bf16[48,1920]{1,0:T(8,128)(2,1)S(1)} %get-tuple-element.133), channel_id=1, source_target_pairs={{0,16},{1,17},{2,18},{3,19},{4,20},{5,21},{6,22},{7,23},{8,24},{9,... | collective-permute-start | bytes 552968 | tf_op jit(solution)/shard_map/ppermute | solution.py:30
  219.0 14.1 %collective-permute-start.42 = (bf16[48,1920]{1,0:T(8,128)(2,1)S(1)}, bf16[48,1920]{1,0:T(8,128)(2,1)S(1)}, u32[]{:S(2)}, u32[]{:S(2)}) collective-permute-start(bf16[48,1920]{1,0:T(8,128)(2,1)S(1)} %get-tuple-element.134), channel_id=1, source_target_pairs={{0,24},{1,25},{2,26},{3,27},{4,28},{5,29},{6,30},{7,31},{8,16},{9,... | collective-permute-start | bytes 552968 | tf_op jit(solution)/shard_map/ppermute | solution.py:30
  222.2 11.1 %collective-permute-start.30 = (bf16[4,48,1280]{2,1,0:T(8,128)(2,1)S(1)}, bf16[4,48,1280]{2,1,0:T(8,128)(2,1)S(1)}, u32[]{:S(2)}, u32[]{:S(2)}) collective-permute-start(bf16[4,48,1280]{2,1,0:T(8,128)(2,1)S(1)} %get-tuple-element.215), channel_id=1, source_target_pairs={{0,4},{1,3},{2,6},{3,1},{4,0},{5,7},{6,2},{7,5},{8,12},{9,11},{10,... | collective-permute-start | bytes 1474568 | tf_op jit(solution)/shard_map/ppermute | solution.py:30
  239.3 11.4 %collective-permute-start.32 = (bf16[48,1280]{1,0:T(8,128)(2,1)S(1)}, bf16[48,1280]{1,0:T(8,128)(2,1)S(1)}, u32[]{:S(2)}, u32[]{:S(2)}) collective-permute-start(bf16[48,1280]{1,0:T(8,128)(2,1)S(1)} %get-tuple-element.224), channel_id=1, source_target_pairs={{0,16},{1,17},{2,18},{3,19},{4,20},{5,21},{6,22},{7,23},{8,24},{9,... | collective-permute-start | bytes 368648 | tf_op jit(solution)/shard_map/ppermute | solution.py:30
  (19 other events, 145.1 us)
